TPU v7x, 256 devices: a whole 4x4x8 slice. The times are simulated.
256 devices in a mesh: seq: 64 (over y, z, core), mp: 4 (over x).
Axes of the slice: x: 4, y: 4, z: 8, core: 2. Of those that a mesh axis runs over, the one named last changes fastest.
Arguments:
- tile_batch: bfloat16 [256, 256, 1536], P('seq', None, 'mp'), may hold values from -6 to 6
- positions: int32 [256], P('seq'), may hold values from 0 to 8191, as said below
- counts: int32 [64], P('seq'), may hold values from 1 to 4, as said below
- vit_gain: float32 [1536], replicated, may hold values from 0.25 to 1.75
- vit_qkv: bfloat16 [1536, 3, 1536], P(None, None, 'mp')
- vit_out: bfloat16 [1536, 1536], P('mp'), may hold values from -0.15625 to 0.15625
- tile_proj: bfloat16 [1536, 768], replicated, may hold values from -0.15625 to 0.15625
- seq_cache: bfloat16 [8192, 768], P('seq'), may hold values from -6 to 6
- long_gain: float32 [768], replicated, may hold values from 0.25 to 1.75
- long_qkv: bfloat16 [768, 3, 768], P(None, None, 'mp')
- long_out: bfloat16 [768, 768], P('mp'), may hold values from -0.4375 to 0.4375
Outputs:
- longnet_out: bfloat16 [8192, 768], P('seq', 'mp')
Inputs may be any that keep to these rules, and one draw needn't show every extreme that they name: The valid slots name distinct positions; all 256 slots name distinct positions. `counts`: some device holds exactly 4 tiles in every draw.
All inputs are finite; a program needn't handle non-finite values.
Results may differ from a plain program's by a relative error of at most 0.015.
Values may be sent and summed in bfloat16 or wider, within the bound.
No kernel may reach another device: no remote copies, remote signals or barrier semaphores. Data moves between devices by JAX's collectives and lax.ppermute only.
A program may use at most 128 MiB of HBM per device.

v0:
```python
import jax
import jax.numpy as jnp
from jax import lax
from jax.sharding import PartitionSpec as P

HDT = 64
HDL = 48
BRANCHES = 5


EPSILON = 1e-05
FLOOR_SCORE = -1e30


def layer_norm(values, gain_row):
    widened = values.astype(jnp.float32)
    centre = widened - jnp.mean(widened, axis=-1, keepdims=True)
    spread = jnp.mean(centre * centre, axis=-1, keepdims=True)
    return (centre * lax.rsqrt(spread + EPSILON) * gain_row).astype(jnp.bfloat16)


def pool_tile(tile_rows, vit_gain, vit_qkv, vit_out):
    col_width = vit_qkv.shape[-1]
    head_count = col_width // HDT
    normed = layer_norm(tile_rows, vit_gain)
    projected = jnp.dot(
        normed, vit_qkv.reshape(vit_qkv.shape[0], 3 * col_width), preferred_element_type=jnp.float32
    )
    projected = projected.astype(jnp.bfloat16).reshape(tile_rows.shape[0], 3, head_count, HDT)
    scores = jnp.einsum(
        "qhe,khe->hqk", projected[:, 0], projected[:, 1], preferred_element_type=jnp.float32
    ) * HDT ** (-0.5)
    peak_score = jnp.max(scores, axis=-1, keepdims=True)
    weights = jnp.exp(scores - peak_score)
    normalized = (weights / jnp.sum(weights, axis=-1, keepdims=True)).astype(jnp.bfloat16)
    mixed_rows = jnp.einsum(
        "hqk,khe->qhe", normalized, projected[:, 2], preferred_element_type=jnp.float32
    ).astype(jnp.bfloat16)
    pooled = (
        jnp.mean(mixed_rows.astype(jnp.float32), axis=0).reshape(1, col_width).astype(jnp.bfloat16)
    )
    partial_value = jnp.dot(pooled, vit_out, preferred_element_type=jnp.float32)[0]
    return (partial_value, jnp.mean(tile_rows.astype(jnp.float32), axis=0))


def pick_rows(values, select):
    stride, head_count = select.shape
    shaped = values.reshape((values.shape[0] // stride, stride, head_count) + values.shape[2:])
    chosen = select.reshape((1, stride, head_count) + (1,) * (values.ndim - 2))
    return jnp.sum(jnp.where(chosen, shaped, jnp.zeros((), values.dtype)), axis=1)


def spread_rows(values, select, fill_value):
    moved = jnp.moveaxis(values, 0, 1)
    stride = select.shape[0]
    tail_dims = moved.shape[2:]
    chosen = select.reshape((1,) + select.shape + (1,) * len(tail_dims))
    placed = jnp.where(chosen, moved[:, None], fill_value)
    return placed.reshape((moved.shape[0] * stride,) + moved.shape[1:])


def make_fold(queries, query_seg, stride, span, head_count):

    def fold(state_now, shard_rows, first_row):
        length = shard_rows.shape[0]
        block_len = min(length, 1024)

        def advance(number, inner):
            highest, totals, weighted = inner
            rows_here = lax.dynamic_slice_in_dim(shard_rows, number * block_len, block_len, 0)
            rows_here = rows_here.reshape(block_len, head_count, 2 * HDL)
            key_rows = rows_here[:, :, :HDL]
            value_rows = rows_here[:, :, HDL:]
            key_seg = (number * block_len + jnp.arange(block_len)) * stride // span
            scores = jnp.einsum(
                "qhe,khe->hqk", queries, key_rows, preferred_element_type=jnp.float32
            ) * HDL ** (-0.5)
            key_mask = (query_seg[:, None] == key_seg[None, :])[None]
            new_high = jnp.maximum(
                highest, jnp.max(jnp.where(key_mask, scores, FLOOR_SCORE), axis=-1)
            )
            weights = jnp.where(key_mask, jnp.exp(scores - new_high[..., None]), 0.0)
            rescale = jnp.exp(highest - new_high)
            totals = totals * rescale + jnp.sum(weights, axis=-1)
            weighted = weighted * rescale[..., None] + jnp.einsum(
                "hqk,khe->hqe",
                weights.astype(jnp.bfloat16),
                value_rows,
                preferred_element_type=jnp.float32,
            )
            return (new_high, totals, weighted)

        return lax.fori_loop(0, length // block_len, advance, state_now)

    return fold


def local(
    tile_batch,
    positions,
    counts,
    vit_gain,
    vit_qkv,
    vit_out,
    tile_proj,
    seq_cache,
    long_gain,
    long_qkv,
    long_out,
):
    slot_count = tile_batch.shape[0]
    work_count = counts[0]
    full_tiles = lax.all_gather(tile_batch, "mp", axis=2, tiled=True)
    feature_width = full_tiles.shape[2]

    def encode(number, state_now):
        partials, means = state_now
        tile_rows = lax.dynamic_index_in_dim(full_tiles, number, 0, keepdims=False)
        partial_value, token_mean = pool_tile(tile_rows, vit_gain, vit_qkv, vit_out)
        partials = lax.dynamic_update_index_in_dim(partials, partial_value, number, 0)
        means = lax.dynamic_update_index_in_dim(means, token_mean, number, 0)
        return (partials, means)

    zero_pool = jnp.zeros((slot_count, feature_width), jnp.float32)
    partials, means = lax.fori_loop(0, work_count, encode, (zero_pool, zero_pool))
    summed = lax.psum(partials, "mp")
    embeds = jnp.dot(
        (summed + means).astype(jnp.bfloat16), tile_proj, preferred_element_type=jnp.float32
    ).astype(jnp.bfloat16)
    sent_pos = jnp.where(jnp.arange(slot_count) < work_count, positions, -1)
    all_embeds, all_pos = (
        lax.all_gather(embeds, "seq", axis=0, tiled=True),
        lax.all_gather(sent_pos, "seq", axis=0, tiled=True),
    )
    row_count = seq_cache.shape[0]
    seq_index = lax.axis_index("seq")
    local_pos = seq_index * row_count + jnp.arange(row_count)
    matches = all_pos[None, :] == local_pos[:, None]
    placed = jnp.dot(matches.astype(jnp.bfloat16), all_embeds, preferred_element_type=jnp.float32)
    found = jnp.any(matches, axis=1)
    sequence = jnp.where(found[:, None], placed.astype(jnp.bfloat16), seq_cache)
    seq_norm = layer_norm(sequence, long_gain)
    col_width = long_qkv.shape[-1]
    head_count = col_width // HDL
    projected = jnp.dot(
        seq_norm,
        long_qkv.reshape(long_qkv.shape[0], 3 * col_width),
        preferred_element_type=jnp.float32,
    )
    projected = projected.astype(jnp.bfloat16).reshape(row_count, 3, head_count, HDL)
    queries = projected[:, 0]
    key_value = jnp.concatenate([projected[:, 1], projected[:, 2]], axis=-1)
    head_ids = lax.axis_index("mp") * head_count + jnp.arange(head_count)
    seq_length = row_count * lax.axis_size("seq")
    branch_peaks = []
    branch_totals = []
    branch_outs = []
    for level in range(BRANCHES):
        stride = 2**level
        span = seq_length // 2 ** (BRANCHES - 1 - level)
        picked_len = row_count // stride
        select = jnp.arange(stride)[:, None] == (head_ids % stride)[None, :]
        q_pick = pick_rows(queries, select)
        kv_pick = pick_rows(key_value, select).reshape(picked_len, head_count * 2 * HDL)
        query_seg = (seq_index * row_count + jnp.arange(picked_len) * stride) // span
        fold = make_fold(q_pick, query_seg, stride, span, head_count)
        initial = (
            jnp.full((head_count, picked_len), FLOOR_SCORE, jnp.float32),
            jnp.zeros((head_count, picked_len), jnp.float32),
            jnp.zeros((head_count, picked_len, HDL), jnp.float32),
        )
        highest, totals, weighted = fold(
            initial, lax.all_gather(kv_pick, "seq", axis=0, tiled=True), jnp.int32(0)
        )
        branch_peaks.append(spread_rows(highest, select, FLOOR_SCORE))
        branch_totals.append(spread_rows(totals, select, 0.0))
        branch_outs.append(spread_rows(weighted, select, 0.0))
    overall = branch_peaks[0]
    for level in range(1, BRANCHES):
        overall = jnp.maximum(overall, branch_peaks[level])
    numer = jnp.zeros((row_count, head_count, HDL), jnp.float32)
    denom = jnp.zeros((row_count, head_count), jnp.float32)
    for level in range(BRANCHES):
        factor = jnp.exp(branch_peaks[level] - overall)
        numer = numer + factor[..., None] * branch_outs[level]
        denom = denom + factor * branch_totals[level]
    attended = (numer / denom[..., None]).astype(jnp.bfloat16).reshape(row_count, head_count * HDL)
    head_terms = jnp.dot(attended, long_out, preferred_element_type=jnp.float32)
    return lax.psum_scatter(head_terms.astype(jnp.bfloat16), "mp", scatter_dimension=1, tiled=True)


def solution(mesh):
    placed = (
        P("seq", None, "mp"),
        P("seq"),
        P("seq"),
        P(),
        P(None, None, "mp"),
        P("mp", None),
        P(),
        P("seq", None),
        P(),
        P(None, None, "mp"),
        P("mp", None),
    )
    return jax.shard_map(
        local, mesh=mesh, in_specs=placed, out_specs=P("seq", "mp"), check_vma=False
    )
```

profile of v0, /device:TPU:1, one launch (start us, length us, event | category | flops | bytes accessed | tf_op | source)
XLA Modules:
  0.0 516.0 jit_solution(3560166779550582399)
XLA Ops:
  7.3 6.2 %copy.147 = bf16[1536,3,384]{0,2,1:T(8,128)(2,1)} copy(bf16[1536,3,384]{2,0,1:T(8,128)(2,1)} %param.23) | data formatting | bytes 7077888 | tf_op jit(solution)/shard_map/while | solution.py:125
  15.6 21.1 %all-reduce = s32[256]{0:T(256)S(1)} all-reduce(s32[256]{0:T(256)S(1)} %fusion.127), channel_id=1, replica_groups=mesh['seq'=64,'mp'=4] {'seq'}, use_global_device_ids=true, to_apply=%add | all-reduce | flops 256 | bytes 2048
  38.5 16.6 %all-gather.6.cloned.1.call-done = bf16[4,256,1536]{2,1,0:T(8,128)(2,1)} async-done(((bf16[4,256,384]{2,1,0:T(8,128)(2,1)}), bf16[4,256,1536]{2,1,0:T(8,128)(2,1)}) %all-gather.6.cloned.1.call-update) | async-done | bytes 3145744 | tf_op jit(solution)/shard_map/all_gather | solution.py:113
  56.3 19.5 %while.86 = (s32[]{:T(128)}, f32[4,1536]{1,0:T(4,128)}, f32[4,1536]{1,0:T(4,128)}, s32[]{:T(128)}, bf16[4,256,1536]{2,1,0:T(8,128)(2,1)}, /*index=5*/f32[1536]{0...) while((s32[]{:T(128)}, f32[4,1536]{1,0:T(4,128)}, ...), condition=%wide.region_8.9_spmd, body=%wide.region_1.8_spmd.sunk | while | flops 1066207872 | bytes 9927851 | solution.py:125
  59.9 4.3 convolution_convert_fusion.7
  64.3 2.1 copy.188
  66.4 2.3 fusion.180
  68.7 2.1 fusion.181
  75.9 12.1 %psum.7 = f32[4,1536]{1,0:T(4,128)S(1)} all-reduce(f32[4,1536]{1,0:T(4,128)} %get-tuple-element.634), channel_id=1, replica_groups=mesh['seq'=64,'mp'=4] {'mp'}, use_global_device_ids=true, to_apply=%region_9.10 | all-reduce | flops 6144 | bytes 49152 | tf_op jit(solution)/shard_map/psum | solution.py:126
  89.2 103.5 %all-gather = bf16[64,4,768]{2,1,0:T(4,128)(2,1)S(1)} all-gather(bf16[1,4,768]{2,1,0:T(4,128)(2,1)S(1)} %fusion.79), channel_id=1, replica_groups=mesh['seq'=64,'mp'=4] {'seq'}, dimensions={0}, use_global_device_ids=true | all-gather | bytes 399360 | tf_op jit(solution)/shard_map/all_gather | solution.py:132
  204.0 47.0 %all_gather.31 = bf16[512,384]{1,0:T(8,128)(2,1)S(1)} all-gather(bf16[8,384]{1,0:T(8,128)(2,1)S(1)} %reshape.949), channel_id=1, replica_groups=mesh['seq'=64,'mp'=4] {'seq'}, dimensions={0}, use_global_device_ids=true | all-gather | bytes 399360 | tf_op jit(solution)/shard_map/all_gather | solution.py:173
  258.4 49.1 %all_gather.30 = bf16[1024,384]{1,0:T(8,128)(2,1)S(1)} all-gather(bf16[16,384]{1,0:T(8,128)(2,1)S(1)} %reshape.947), channel_id=1, replica_groups=mesh['seq'=64,'mp'=4] {'seq'}, dimensions={0}, use_global_device_ids=true | all-gather | bytes 798720 | tf_op jit(solution)/shard_map/all_gather | solution.py:173
  332.0 12.4 %while.89 = (s32[]{:T(128)}, f32[4,32]{1,0:T(4,128)S(1)}, f32[4,32]{1,0:T(4,128)}, f32[4,32,48]{2,1,0:T(8,128)}, bf16[2048,384]{1,0:T(8,128)(2,1)}, /*index=5*/b...) while((s32[]{:T(128)}, f32[4,32]{1,0:T(4,128)S(1)}, ...), condition=%wide.region_27.28_spmd.clone, body=%wide.region_24.27_spmd.clone.sunk | while | flops 26415272 | bytes 5915179 | solution.py:93
  348.7 25.8 %while.88 = (s32[]{:T(128)}, f32[4,64]{1,0:T(4,128)S(1)}, f32[4,64]{1,0:T(4,128)S(1)}, f32[4,64,48]{1,2,0:T(8,128)}, bf16[4096,384]{1,0:T(8,128)(2,1)}, /*index=...) while((s32[]{:T(128)}, f32[4,64]{1,0:T(4,128)S(1)}, ...), condition=%wide.region_21.22_spmd.clone, body=%wide.region_18.21_spmd.clone.sunk | while | flops 52813124 | bytes 7561915 | solution.py:93
  353.0 2.0 convolution_add_fusion.7
  359.5 2.1 convolution_add_fusion.7
  365.9 2.1 convolution_add_fusion.7
  372.4 2.1 convolution_add_fusion.7
  377.9 51.2 %all-gather.8.cloned.1.call-done = bf16[8192,384]{0,1:T(8,128)(2,1)} async-done(((bf16[128,384]{0,1:T(8,128)(2,1)}), bf16[8192,384]{0,1:T(8,128)(2,1)}) %all-gather.8.cloned.1.call-update) | async-done | bytes 6291472 | tf_op jit(solution)/shard_map/all_gather | solution.py:173
  429.1 54.9 %while.87 = (s32[]{:T(128)}, f32[4,128]{1,0:T(4,128)S(1)}, f32[4,128]{1,0:T(4,128)S(1)}, f32[4,128,48]{1,2,0:T(8,128)}, bf16[8192,384]{0,1:T(8,128)(2,1)}, /*ind...) while((s32[]{:T(128)}, f32[4,128]{1,0:T(4,128)S(1)}, ...), condition=%wide.region_15.16_spmd.clone, body=%wide.region_12.15_spmd.clone.sunk | while | flops 106656256 | bytes 18638096 | solution.py:93
  430.6 1.9 fusion.186
  432.5 2.2 fusion.187
  437.4 1.9 fusion.186
  439.4 2.2 fusion.187
  446.2 2.2 fusion.187
  453.1 2.2 fusion.187
  460.0 2.2 fusion.187
  466.8 2.2 fusion.187
  473.7 2.2 fusion.187
  480.6 2.2 fusion.187
  486.7 2.0 convolution_convert_fusion.2
  488.7 20.7 %reduce-scatter.2.cloned.1.call-done = bf16[128,192]{0,1:T(8,128)(2,1)} async-done(((bf16[128,768]{0,1:T(8,128)(2,1)}), bf16[128,192]{0,1:T(8,128)(2,1)}) %reduce-scatter.2.cloned.1.call-update) | async-done | bytes 49168 | tf_op jit(solution)/shard_map/reduce_scatter | solution.py:189
  (387 shorter events, 128.6 us)
Async XLA Ops:
  6.5 81.5 %copy-start = (bf16[1536,768]{1,0:T(8,128)(2,1)S(1)}, bf16[1536,768]{1,0:T(8,128)(2,1)}, u32[]{:S(2)}) copy-start(bf16[1536,768]{1,0:T(8,128)(2,1)} %param.25) | copy-start | bytes 7077892
  6.5 48.6 %all-gather.6.cloned.1.call-start = ((), (), s32[]{:S(2)}) async-start(), calls=%async_computation.1 | async-start | bytes 3932160 | tf_op jit(solution)/shard_map/all_gather | solution.py:113
  7.3 324.8 %all-gather.12.cloned.1.call-start = ((), (), s32[]{:S(2)}) async-start(), calls=%async_computation.4 | async-start | bytes 1597440 | tf_op jit(solution)/shard_map/all_gather | solution.py:173
  7.3 6.9 %copy-start.32 = (u32[256]{0:T(256)S(1)}, u32[256]{0:T(256)}, u32[]{:S(2)}) copy-start(u32[256]{0:T(256)} %constant.623) | copy-start | bytes 3076
  7.3 8.1 %copy-start.31 = (s32[4]{0:T(128)S(1)}, s32[4]{0:T(128)}, u32[]{:S(2)}) copy-start(s32[4]{0:T(128)} %param.20) | copy-start | bytes 52
  7.3 49.0 %copy-start.2 = (bf16[384,1536]{1,0:T(8,128)(2,1)S(1)}, bf16[384,1536]{1,0:T(8,128)(2,1)}, u32[]{:S(2)}) copy-start(bf16[384,1536]{1,0:T(8,128)(2,1)} %param.24) | copy-start | bytes 3538948
  36.7 19.7 %copy-start.17 = (s32[256]{0:T(256)}, s32[256]{0:T(256)S(1)}, u32[]{:S(2)}) copy-start(s32[256]{0:T(256)S(1)} %all-reduce) | copy-start | bytes 3076
  75.8 117.0 %copy-start.8 = (bf16[128,768]{1,0:T(8,128)(2,1)S(1)}, bf16[128,768]{1,0:T(8,128)(2,1)}, u32[]{:S(2)}) copy-start(bf16[128,768]{1,0:T(8,128)(2,1)} %param.26) | copy-start | bytes 589828
  75.8 117.0 %copy-start.18 = (s32[256]{0:T(256)S(1)}, s32[256]{0:T(256)}, u32[]{:S(2)}) copy-start(s32[256]{0:T(256)} %copy-done.17) | copy-start | bytes 3076
  75.8 117.0 %copy-start.29 = (s32[128]{0:T(128)S(1)}, s32[128]{0:T(128)}, u32[]{:S(2)}) copy-start(s32[128]{0:T(128)} %copy-done.28) | copy-start | bytes 1540
  75.8 117.0 %copy-start.30 = (pred[128]{0:T(512)(128)(4,1)S(1)}, pred[128]{0:T(512)(128)(4,1)}, u32[]{:S(2)}) copy-start(pred[128]{0:T(512)(128)(4,1)} %compare_reduce_fusion) | copy-start | bytes 388
  88.0 105.4 %copy-start.27 = (f32[768]{0:T(1024)S(1)}, f32[768]{0:T(1024)}, u32[]{:S(2)}) copy-start(f32[768]{0:T(1024)} %param.27) | copy-start | bytes 9220
  192.7 3.3 copy-start.24
  192.8 4.3 copy-start.33
  197.1 151.5 %all-gather.10.cloned.1.call-start = ((), (), s32[]{:S(2)}) async-start(), calls=%async_computation.3 | async-start | bytes 3194880 | tf_op jit(solution)/shard_map/all_gather | solution.py:173
  197.2 6.4 %copy-start.23 = (pred[2,4]{0,1:T(4,128)(4,1)}, pred[2,4]{0,1:T(4,128)(4,1)S(1)}, u32[]{:S(2)}) copy-start(pred[2,4]{0,1:T(4,128)(4,1)S(1)} %iota_compare_fusion.3) | copy-start | bytes 28
  198.7 230.3 %all-gather.8.cloned.1.call-start = ((), (), s32[]{:S(2)}) async-start(), calls=%async_computation.2 | async-start | bytes 6389760 | tf_op jit(solution)/shard_map/all_gather | solution.py:173
  199.0 5.1 copy-start.26
  251.2 7.0 %copy-start.4 = (bf16[512,384]{0,1:T(8,128)(2,1)}, bf16[512,384]{0,1:T(8,128)(2,1)S(1)}, u32[]{:S(2)}) copy-start(bf16[512,384]{0,1:T(8,128)(2,1)S(1)} %copy.170) | copy-start | bytes 1179652
  254.6 3.7 copy-start.7
  255.2 254.3 %reduce-scatter.2.cloned.1.call-start = ((), (), s32[]{:S(2)}) async-start(), calls=%async_computation.5 | async-start | bytes 245760 | tf_op jit(solution)/shard_map/reduce_scatter | solution.py:189
  308.7 20.5 %copy-start.3 = (bf16[1024,384]{0,1:T(8,128)(2,1)S(1)}, bf16[1024,384]{0,1:T(8,128)(2,1)}, u32[]{:S(2)}) copy-start(bf16[1024,384]{0,1:T(8,128)(2,1)} %copy.165) | copy-start | bytes 2359300
  332.0 16.6 %copy-start.11 = (f32[4,64]{1,0:T(4,128)S(1)}, f32[4,64]{1,0:T(4,128)}, u32[]{:S(2)}) copy-start(f32[4,64]{1,0:T(4,128)} %custom-call.4) | copy-start | bytes 3076
  332.2 4.0 copy-start.12
  332.2 4.1 copy-start.14
  338.4 4.0 copy-start.12
  338.4 4.1 copy-start.14
  348.6 80.4 %copy-start.16 = (bf16[128,4,48]{0,2,1:T(8,128)(2,1)S(1)}, bf16[128,4,48]{0,2,1:T(8,128)(2,1)}, u32[]{:S(2)}) copy-start(bf16[128,4,48]{0,2,1:T(8,128)(2,1)} %get-tuple-element.1162) | copy-start | bytes 147460
  429.1 54.9 %copy-start.20 = (f32[128,4]{0,1:T(4,128)S(1)}, f32[128,4]{0,1:T(4,128)}, u32[]{:S(2)}) copy-start(f32[128,4]{0,1:T(4,128)} %broadcast_in_dim.793) | copy-start | bytes 6148
  429.1 54.9 %copy-start.21 = (f32[128,4]{0,1:T(4,128)S(1)}, f32[128,4]{0,1:T(4,128)}, u32[]{:S(2)}) copy-start(f32[128,4]{0,1:T(4,128)} %broadcast_in_dim.791) | copy-start | bytes 6148
  429.1 56.6 %copy-start.5 = (f32[128,192]{0,1:T(8,128)S(1)}, f32[128,192]{0,1:T(8,128)}, u32[]{:S(2)}) copy-start(f32[128,192]{0,1:T(8,128)} %copy.178) | copy-start | bytes 294916
  429.1 56.6 %copy-start.6 = (f32[128,192]{0,1:T(8,128)S(1)}, f32[128,192]{0,1:T(8,128)}, u32[]{:S(2)}) copy-start(f32[128,192]{0,1:T(8,128)} %copy.176) | copy-start | bytes 294916
  (32 other events, 49.1 us)
Sparse Core Ops, SparseCore 0:
  9.2 45.8 all-gather.5
  197.2 72.6 all-gather.11
  272.7 75.8 all-gather.9
  351.1 77.9 all-gather.7
  488.8 20.5 reduce-scatter.1
where the time goes:
time: 521 us; the launch traced here: 516 us
  blocking collectives  233 us (45%)
  waiting for transfers between devices  89.5 us (17%)
  local copies, waits for them, and re-layouts  73.9 us (14%)
  matrix products  58.3 us (11%)
  other arithmetic  43.8 us (8%)
  between operations  15 us (3%)
    all_gather x1, blocking collectives, local(): lax.all_gather(embeds, 'seq', axis=0, tiled=True)  104 us
    all_gather x2, blocking collectives, local(): lax.all_gather(kv_pick, 'seq', axis=0, tiled=True)  96.1 us
    all_gather x3, waiting for transfers between devices, local(): lax.all_gather(kv_pick, 'seq', axis=0, tiled=True)  51.4 us
    dot_general x16, matrix products, advance(): jnp.einsum('qhe,khe->hqk', queries, key_rows, preferred_element_type=jnp....  26 us
    dynamic_slice x20, local copies, waits for them, and re-layouts, advance(): lax.dynamic_slice_in_dim(shard_rows, number * block_len, block_len, 0)  24 us
    broadcast_in_dim x36, local copies, waits for them, and re-layouts, spread_rows(): placed = jnp.where(chosen, moved[:, None], fill_value)  21.4 us
    reduce_sum x16, other arithmetic, advance(): totals = totals * rescale + jnp.sum(weights, axis=-1)  21.3 us
    unnamed x1, blocking collectives  21.1 us
  transfers between devices with their start and end apart: 5, of which 4 were waited for; matrix products, arithmetic and copies ran while one was open for 18% of the time, Pallas kernels for 0%

commit v1 on v0

v1 whole, which is shorter than its diff:
```python
import functools
import math

import jax
import jax.numpy as jnp
from jax import lax
from jax.experimental import pallas as pl
from jax.experimental.pallas import tpu as pltpu
from jax.sharding import PartitionSpec as P

HDT = 64
HDL = 48
BRANCHES = 5
EPSILON = 1e-05
FLOOR_SCORE = -1e30
BF = jnp.bfloat16
F32 = jnp.float32
ROWS = 128
BASES = (0, 256, 512, 768, 1024)


def params(mib=40):
    return pltpu.CompilerParams(vmem_limit_bytes=mib * 2**20)


def whole(kind=pltpu.VMEM):
    return pl.BlockSpec(memory_space=kind)


def dot(a, b):
    return jnp.dot(a, b, preferred_element_type=F32)


def dot_t(a, b):
    return lax.dot_general(a, b, (((1,), (1,)), ((), ())), preferred_element_type=F32)


def iota(shape, dim):
    return lax.broadcasted_iota(jnp.int32, shape, dim)


def encode_kernel(idx, own, left, right, far_a, far_b, gain, weight, out, xn, qk):
    mp = idx[0]
    tokens, width = own.shape[1], own.shape[2]
    features = 4 * width
    blocks = [lax.rem(mp + shift, 4) for shift in (0, 3, 1, 2)]
    starts = [pl.multiple_of(block * width, 128) for block in blocks]
    for t in range(2):
        far = far_a if t == 0 else far_b
        parts = [own[t], left[t], right[t], far[0]]
        wide = [part.astype(F32) for part in parts]
        total = sum(jnp.sum(part, axis=-1, keepdims=True) for part in wide)
        mean = total * (1.0 / features)
        centred = [part - mean for part in wide]
        spread = sum(jnp.sum(part * part, axis=-1, keepdims=True) for part in centred)
        scale = lax.rsqrt(spread * (1.0 / features) + EPSILON)
        for d in range(4):
            xn[d, t * tokens : (t + 1) * tokens, :] = (
                centred[d] * scale * gain[pl.ds(blocks[d], 1), 0, :]
            ).astype(BF)
        out[t : t + 1, width : 2 * width] = jnp.sum(wide[0], axis=0, keepdims=True) * (1.0 / tokens)
    acc = dot(xn[0], weight[pl.ds(starts[0], width), 0 : 2 * width])
    for d in range(1, 4):
        acc = acc + dot(xn[d], weight[pl.ds(starts[d], width), 0 : 2 * width])
    qk[...] = acc.astype(BF)
    lane = iota((tokens, 2 * HDT), 1)
    pooled = [[] for _ in range(4)]
    for t in range(2):
        low, high = t * tokens, (t + 1) * tokens
        rows = []
        for pair in range(width // (2 * HDT)):
            q2 = qk[low:high, pair * 128 : (pair + 1) * 128]
            k2 = qk[low:high, width + pair * 128 : width + (pair + 1) * 128]
            for half in range(2):
                qm = jnp.where((lane >= HDT) == (half == 1), q2, jnp.zeros((), BF))
                s = dot_t(qm, k2) * HDT ** (-0.5)
                e = jnp.exp(s - jnp.max(s, axis=-1, keepdims=True))
                share = 1.0 / (jnp.sum(e, axis=-1, keepdims=True) * tokens)
                rows.append(jnp.sum(e * share, axis=0, keepdims=True))
        rows.append(jnp.zeros((8 - len(rows), tokens), F32))
        mix = jnp.concatenate(rows, axis=0).astype(BF)
        for d in range(4):
            pooled[d].append(dot(mix, xn[d, low:high, :]))
    acc = jnp.zeros((16, width), F32)
    for d in range(4):
        acc = acc + dot(
            jnp.concatenate(pooled[d], axis=0).astype(BF),
            weight[pl.ds(starts[d], width), 2 * width : 3 * width],
        )
    keep = (iota((16, width), 0) & 7) == (iota((16, width), 1) >> 6)
    acc = jnp.where(keep, acc, 0.0)
    for t in range(2):
        out[t : t + 1, 0:width] = jnp.sum(acc[t * 8 : (t + 1) * 8], axis=0, keepdims=True)


def encode(idx, own, left, right, far_a, far_b, gain, weight):
    tokens, width = own.shape[1], own.shape[2]
    return pl.pallas_call(
        encode_kernel,
        out_shape=jax.ShapeDtypeStruct((2, 2 * width), F32),
        in_specs=[whole(pltpu.SMEM)] + [whole()] * 7,
        out_specs=whole(),
        scratch_shapes=[
            pltpu.VMEM((4, 2 * tokens, width), BF),
            pltpu.VMEM((2 * tokens, 2 * width), BF),
        ],
        compiler_params=params(),
        cost_estimate=pl.CostEstimate(
            flops=6 * 10**9, bytes_accessed=8 * 10**6, transcendentals=8 * 10**5
        ),
        name="encode",
    )(idx, own, left, right, far_a, far_b, gain, weight)


def norm_rows(x, gain):
    mean = jnp.mean(x, axis=-1, keepdims=True)
    centre = x - mean
    spread = jnp.mean(centre * centre, axis=-1, keepdims=True)
    return (centre * lax.rsqrt(spread + EPSILON) * gain).astype(BF)


def embed_kernel(a, b, c, d, tail, gain, weight, out):
    width = weight.shape[1]
    total = (a[...] + b[...]) + (c[...] + d[...])
    normed = norm_rows(total.astype(BF).astype(F32), gain[...])
    out[:, 0:width] = dot(normed, weight[...]).astype(BF)
    out[:, width:] = tail[...]


def embed_rows(parts, tail, gain, weight):
    rows, width = parts[0].shape[0], weight.shape[1]
    return pl.pallas_call(
        embed_kernel,
        out_shape=jax.ShapeDtypeStruct((rows, width + tail.shape[1]), BF),
        in_specs=[whole()] * 7,
        out_specs=whole(),
        compiler_params=params(),
        name="embed_rows",
    )(*parts, tail, gain, weight)


def rev4(x):
    return ((x & 1) << 3) | ((x & 2) << 1) | ((x & 4) >> 1) | ((x & 8) >> 3)


def pick_start(head, level):
    return pl.multiple_of((rev4(head & 15) >> (4 - level)) * (ROWS >> level), 8)


def local_row(j, level, head):
    bits = j >> 3
    free = 4 - level
    turned = rev4(bits) >> (4 - free) if free else bits * 0
    return (j & 7) * 16 + (turned << level) + (head & ((1 << level) - 1))


def slide_kernel(idx, cache, gain, weight, tail, q_out, picks, kv):
    heads_width = q_out.shape[1]
    first_head = idx[0] * 4
    row = iota((ROWS, ROWS), 0)
    turn = (local_row(row, 0, 0) == iota((ROWS, ROWS), 1)).astype(BF)
    normed = norm_rows(cache[...].astype(F32), gain[...])
    normed = dot(turn, normed).astype(BF)
    qkv = dot(normed, weight[...]).astype(BF).astype(F32)
    q_out[...] = qkv[:, 2 * heads_width :]
    kv[...] = qkv[:, : 2 * heads_width]
    base = 0
    for level in range(BRANCHES):
        n = ROWS >> level
        column = iota((n, 2 * heads_width), 1)
        column = jnp.where(column >= heads_width, column - heads_width, column)
        got = jnp.zeros((n, 2 * heads_width), F32)
        for h in range(4):
            here = (column >= h * HDL) & (column < (h + 1) * HDL)
            got = jnp.where(here, kv[pl.ds(pick_start(first_head + h, level), n), :], got)
        if level == BRANCHES - 1:
            got = jnp.concatenate([got, tail[...]], axis=0)
        picks[base : base + got.shape[0], :] = got.astype(BF)
        base += n


def slide_project(idx, cache, gain, weight, tail):
    hw = weight.shape[1] // 3
    return pl.pallas_call(
        slide_kernel,
        out_shape=(
            jax.ShapeDtypeStruct((ROWS, hw), F32),
            jax.ShapeDtypeStruct((2 * ROWS, 2 * hw), BF),
        ),
        in_specs=[whole(pltpu.SMEM)] + [whole()] * 4,
        out_specs=(whole(), whole()),
        scratch_shapes=[pltpu.VMEM((ROWS, 2 * hw), F32)],
        compiler_params=params(),
        name="slide_project",
    )(idx, cache, gain, weight, tail)


def key_rows(level):
    return 512 if level == BRANCHES - 1 else 256


def flag_kernel(idx, pos, out):
    first_head, seq = idx[0] * 4, idx[1]
    slots = pos.shape[0]
    for level in range(BRANCHES):
        half = key_rows(level)
        n = 16 if level == BRANCHES - 1 else ROWS >> level
        shift = n.bit_length() - 1
        k = iota((8, 2 * half), 1)
        in_half = k & (half - 1)
        source = seq ^ (2 * (in_half >> shift) + (k >= half).astype(jnp.int32))
        j = in_half & (n - 1)
        dead = (j >= 8) if level == BRANCHES - 1 else (j < 0)
        for h in range(4):
            if level == 0 and h > 0:
                out[h : h + 1, 0 : 2 * half] = out[0:1, 0 : 2 * half]
                continue
            place = source * ROWS + local_row(j & 7 if n == 16 else j, level, first_head + h)
            hit = jnp.max(
                (pos[...] == place[0:1]).astype(jnp.int32), axis=0, keepdims=True
            )
            gone = (hit > 0) | dead[0:1]
            r = level * 8 + h
            out[r : r + 1, 0 : 2 * half] = jnp.where(gone, FLOOR_SCORE, 0.0)


def key_flags(idx, pos):
    return pl.pallas_call(
        flag_kernel,
        out_shape=jax.ShapeDtypeStruct((8 * BRANCHES, 1024), F32),
        in_specs=[whole(pltpu.SMEM), whole()],
        out_specs=whole(),
        compiler_params=params(),
        name="key_flags",
    )(idx, pos)


def depth_of(x):
    return sum(((x & mask) == 0).astype(jnp.int32) for mask in (1, 3, 7, 15))


def attend_kernel(idx, q_cache, mine, theirs, bias, emb, out_w, o0, o1, o2, o3, q, peak, total, acc):
    mp, seq = idx[0], idx[1]
    first_head = mp * 4
    hw = q_cache.shape[1]
    scale = HDL ** (-0.5)
    slots = emb.shape[0]
    tail = emb[:, 3 * hw :]
    col = iota((8, tail.shape[1]), 1)
    digits = jnp.where(col == 0, 64.0, jnp.where(col == 1, 1.0, 0.0)).astype(BF)
    pos = dot_t(digits, tail).astype(jnp.int32)[0:1]
    own = seq * ROWS + local_row(iota((ROWS, 1), 0), 0, 0)
    match = own == pos
    found = jnp.max(match.astype(jnp.int32), axis=1, keepdims=True) > 0
    placed = dot(match.astype(BF), emb[:, 2 * hw : 3 * hw])
    q[...] = jnp.where(found, placed, q_cache[...])

    def head_mask(n, h):
        column = iota((n, hw), 1)
        return (column >= h * HDL) & (column < (h + 1) * HDL)

    def queries(level):
        n = ROWS >> level
        got = []
        for h in range(4):
            rows = q[...] if level == 0 else q[pl.ds(pick_start(first_head + h, level), n), :]
            got.append(jnp.where(head_mask(n, h), rows, 0.0))
        return jnp.concatenate(got, axis=0).astype(BF)

    full_q = queries(0)
    s = dot_t(full_q, emb[:, 0:hw]) * scale
    cross = (pos ^ (seq * ROWS)) >> 9
    first = sum(((cross >> b) != 0).astype(jnp.int32) for b in range(4))
    times = []
    for h in range(4):
        q_depth = depth_of(own ^ (first_head + h))
        k_depth = jnp.where(pos < 0, -1, depth_of(pos ^ (first_head + h)) - first)
        times.append(jnp.maximum(jnp.minimum(k_depth, q_depth - first) + 1, 0))
    times = jnp.concatenate(times, axis=0).astype(F32)
    s = jnp.where(times > 0.0, s, FLOOR_SCORE)
    m = jnp.max(s, axis=-1, keepdims=True)
    e = times * jnp.exp(s - m)
    peak[...] = jnp.broadcast_to(m, peak.shape)
    total[...] = jnp.broadcast_to(jnp.sum(e, axis=-1, keepdims=True), total.shape)
    acc[...] = dot(e.astype(BF), emb[:, hw : 2 * hw])

    for level in range(BRANCHES):
        n = ROWS >> level
        half = key_rows(level)
        low = BASES[level]
        qb = full_q if level == 0 else queries(level)
        sides = []
        for number, side in enumerate((mine, theirs)):
            s = dot_t(qb, side[low : low + half, 0:hw]) * scale
            flags = bias[level * 8 : level * 8 + 4, number * half : (number + 1) * half]
            s = s.reshape(4, n, half) + flags[:, None, :]
            sides.append(s.reshape(4 * n, half))
        m = jnp.maximum(
            jnp.max(sides[0], axis=-1, keepdims=True), jnp.max(sides[1], axis=-1, keepdims=True)
        )
        e0, e1 = jnp.exp(sides[0] - m), jnp.exp(sides[1] - m)
        t = jnp.sum(e0, axis=-1, keepdims=True) + jnp.sum(e1, axis=-1, keepdims=True)
        o = dot(e0.astype(BF), mine[low : low + half, hw : 2 * hw]) + dot(
            e1.astype(BF), theirs[low : low + half, hw : 2 * hw]
        )
        for h in range(4):
            start = h * ROWS + (0 if level == 0 else pick_start(first_head + h, level))
            at = pl.ds(pl.multiple_of(start, 8), n)
            part = slice(h * n, (h + 1) * n)
            before = peak[at, :]
            after = jnp.maximum(before, m[part])
            keep, add = jnp.exp(before - after), jnp.exp(m[part] - after)
            peak[at, :] = after
            total[at, :] = total[at, :] * keep + t[part] * add
            acc[at, :] = acc[at, :] * keep[:, 0:1] + o[part] * add[:, 0:1]

    attended = jnp.zeros((ROWS, hw), F32)
    for h in range(4):
        rows = slice(h * ROWS, (h + 1) * ROWS)
        attended = jnp.where(head_mask(ROWS, h), acc[rows, :] / total[rows, 0:1], attended)
    turn = (local_row(iota((ROWS, ROWS), 1), 0, 0) == iota((ROWS, ROWS), 0)).astype(BF)
    attended = dot(turn, attended.astype(BF)).astype(BF)
    for d, o in enumerate((o0, o1, o2, o3)):
        o[...] = dot(attended, out_w[lax.rem(mp + d, 4)]).astype(BF)


def attend(idx, q_cache, mine, theirs, bias, emb, out_w):
    hw = q_cache.shape[1]
    return pl.pallas_call(
        attend_kernel,
        out_shape=(jax.ShapeDtypeStruct((ROWS, hw), BF),) * 4,
        in_specs=[whole(pltpu.SMEM)] + [whole()] * 6,
        out_specs=(whole(),) * 4,
        scratch_shapes=[
            pltpu.VMEM((ROWS, hw), F32),
            pltpu.VMEM((4 * ROWS, 128), F32),
            pltpu.VMEM((4 * ROWS, 128), F32),
            pltpu.VMEM((4 * ROWS, hw), F32),
        ],
        compiler_params=params(),
        name="attend",
    )(idx, q_cache, mine, theirs, bias, emb, out_w)


def combine_kernel(a, b, c, d, out):
    out[...] = ((a[...].astype(F32) + b[...]) + (c[...].astype(F32) + d[...])).astype(BF)


def shift_mp(x, k):
    return lax.ppermute(x, "mp", [(i, (i + k) % 4) for i in range(4)])


def swap_seq(x, bit):
    return lax.ppermute(x, "seq", [(i, i ^ bit) for i in range(64)])


def local(
    tile_batch,
    positions,
    counts,
    vit_gain,
    vit_qkv,
    vit_out,
    tile_proj,
    seq_cache,
    long_gain,
    long_qkv,
    long_out,
):
    mp, seq = lax.axis_index("mp"), lax.axis_index("seq")
    idx = jnp.stack([mp, seq]).astype(jnp.int32)
    slots, _, width = tile_batch.shape
    model = seq_cache.shape[1]
    hw = long_qkv.shape[-1]

    chunks = [tile_batch[0:2], tile_batch[2:4]]
    near = [(shift_mp(chunk, 1), shift_mp(chunk, 3)) for chunk in chunks]
    far = [(shift_mp(a[0:1], 1), shift_mp(b[1:2], 3)) for a, b in near]

    sent = jnp.where(jnp.arange(slots) < counts[0], positions, -64)
    high, low = (sent >> 6).astype(F32), (sent & 63).astype(F32)

    slide_w = jnp.concatenate([long_qkv[:, 1], long_qkv[:, 2], long_qkv[:, 0]], axis=1)
    tail_row = jnp.zeros((8, 2 * hw), F32).at[0, 0:8].set(jnp.concatenate([high, low]))
    gain_row = long_gain.reshape(1, model)
    q_cache, picks = slide_project(idx, seq_cache, gain_row, slide_w, tail_row)
    have = picks[None]
    kept = []
    for level, bit in enumerate((2, 4, 8, 16, 32)):
        have = jnp.concatenate([have, swap_seq(have, bit)], axis=0)
        n = ROWS >> level
        if level < BRANCHES - 1:
            kept.append(have[:, 0:n].reshape(-1, 2 * hw))
            have = have[:, n:]
        else:
            kept.append(have.reshape(-1, 2 * hw))
    mine = jnp.concatenate(kept, axis=0)
    theirs = swap_seq(mine, 1)
    marks = jnp.concatenate([mine[1024:], theirs[1024:]], axis=0)
    marks = marks.reshape(64, 16, 2 * hw)[:, 8, 0:8].astype(jnp.int32)
    all_pos = (marks[:, 0:4] * 64 + marks[:, 4:8]).reshape(64 * slots, 1)
    bias = key_flags(idx, all_pos)

    tile_w = vit_qkv.reshape(vit_qkv.shape[0], 3 * width)
    gain = vit_gain.reshape(4, 1, width)
    rows = [
        encode(idx, chunk, a, b, c, d, gain, tile_w)
        for chunk, (a, b), (c, d) in zip(chunks, near, far)
    ]
    proj_here = lax.dynamic_slice_in_dim(tile_proj, mp * width, width, 0)
    joined = jnp.concatenate([dot(vit_out, tile_proj).astype(BF), proj_here], axis=0)
    partial = dot(jnp.concatenate(rows, axis=0).astype(BF), joined)
    shares = [partial] + [shift_mp(partial, k) for k in (1, 3, 2)]
    tail = jnp.zeros((slots, 64), F32).at[:, 0].set(high).at[:, 1].set(low).astype(BF)
    emb = embed_rows(shares, tail, gain_row, slide_w)
    emb = lax.all_to_all(jnp.broadcast_to(emb[None], (64,) + emb.shape), "seq", 0, 0)
    emb = emb.reshape(64 * slots, emb.shape[2])

    out_w = long_out.reshape(hw, 4, hw).transpose(1, 0, 2)
    o0, o1, o2, o3 = attend(idx, q_cache, mine, theirs, bias, emb, out_w)
    terms = [o0, shift_mp(o1, 1), shift_mp(o2, 2), shift_mp(o3, 3)]
    return pl.pallas_call(
        combine_kernel,
        out_shape=jax.ShapeDtypeStruct((ROWS, hw), BF),
        in_specs=[whole()] * 4,
        out_specs=whole(),
        name="combine",
    )(*terms)


def solution(mesh):
    placed = (
        P("seq", None, "mp"),
        P("seq"),
        P("seq"),
        P(),
        P(None, None, "mp"),
        P("mp", None),
        P(),
        P("seq", None),
        P(),
        P(None, None, "mp"),
        P("mp", None),
    )
    return jax.shard_map(
        local, mesh=mesh, in_specs=placed, out_specs=P("seq", "mp"), check_vma=False
    )
```

time: 521 us -> 132 us (0.25)
  blocking collectives: 233 us -> 0 us
  waiting for transfers between devices: 89.5 us -> 22 us
  matrix products: 58.3 us -> 2.17 us
  starting transfers between devices: 0.17 us -> 43.7 us
  local copies, waits for them, and re-layouts: 73.9 us -> 31.1 us
  other arithmetic: 43.8 us -> 7.86 us
  Pallas kernels: 0 us -> 23 us
  between operations: 15 us -> 1.08 us
    all_gather x3 -> x0, blocking collectives: 200 us -> none  [the longest x1 104 us: local(): lax.all_gather(embeds, 'seq', axis=0, tiled=True)]
    all_gather x4 -> x0, waiting for transfers between devices: 68 us -> none  [the longest x3 51.4 us: local(): lax.all_gather(kv_pick, 'seq', axis=0, tiled=True)]
    dot_general x39 -> x2, matrix products: 56.1 us -> 2.17 us  [dot(): return jnp.dot(a, b, preferred_element_type=F32)]
    ppermute x0 -> x20, starting transfers between devices: none -> 35.7 us  [the longest x6 19.3 us: swap_seq(): return lax.ppermute(x, 'seq', [(i, i ^ bit) for i in range(64)])]
    reduce_sum x27 -> x0, other arithmetic: 30.8 us -> none  [the longest x16 21.3 us: advance(): totals = totals * rescale + jnp.sum(weights, axis=-1)]
    dynamic_slice x20 -> x1, local copies, waits for them, and re-layouts: 24 us -> 0.05 us  [local(): proj_here = lax.dynamic_slice_in_dim(tile_proj, mp * width, width, 0)]
    pallas_call x0 -> x7, Pallas kernels: none -> 23 us  [the longest x2 12.8 us: encode(): pl.pallas_call(encode_kernel, out_shape=jax.ShapeDtypeStruct((2, 2 * widt...]
    broadcast_in_dim x38 -> x1, local copies, waits for them, and re-layouts: 22.6 us -> 0.83 us  [local(): jnp.broadcast_to(emb[None], (64,) + emb.shape)]
  transfers between devices with their start and end apart: 5 -> 21, of which waited for: 4 -> 5; matrix products, arithmetic and copies ran while one was open for 18% -> 21% of each run, Pallas kernels for 0% -> 10%
where the time goes in v1:
time: 132 us; the launch traced here: 131 us
  starting transfers between devices  43.7 us (33%)
  local copies, waits for them, and re-layouts  31.1 us (24%)
  Pallas kernels  23 us (17%)
  waiting for transfers between devices  22 us (17%)
  other arithmetic  7.86 us (6%)
  matrix products  2.17 us (2%)
    ppermute x6, starting transfers between devices, swap_seq(): return lax.ppermute(x, 'seq', [(i, i ^ bit) for i in range(64)])  19.3 us
    ppermute x14, starting transfers between devices, shift_mp(): return lax.ppermute(x, 'mp', [(i, (i + k) % 4) for i in range(4)])  16.4 us
    unnamed x40, local copies, waits for them, and re-layouts  13 us
    all_to_all x1, waiting for transfers between devices, local(): lax.all_to_all(jnp.broadcast_to(emb[None], (64,) + emb.shape), 'seq', 0, 0)  12.8 us
    pallas_call x2, Pallas kernels, encode(): pl.pallas_call(encode_kernel, out_shape=jax.ShapeDtypeStruct((2, 2 * widt...  12.8 us
    all_to_all x1, starting transfers between devices, local(): lax.all_to_all(jnp.broadcast_to(emb[None], (64,) + emb.shape), 'seq', 0, 0)  8.02 us
    ppermute x14, waiting for transfers between devices, shift_mp(): return lax.ppermute(x, 'mp', [(i, (i + k) % 4) for i in range(4)])  7.23 us
    reshape x1, local copies, waits for them, and re-layouts, local(): tile_w = vit_qkv.reshape(vit_qkv.shape[0], 3 * width)  5.79 us
  transfers between devices with their start and end apart: 21, of which 5 were waited for; matrix products, arithmetic and copies ran while one was open for 21% of the time, Pallas kernels for 10%

profile of v1, /device:TPU:1, one launch (start us, length us, event | category | flops | bytes accessed | tf_op | source)
XLA Modules:
  0.0 131.0 jit_solution(3342966877482186674)
XLA Ops:
  1.4 1.2 fusion.15
  6.2 1.3 %fusion.12 = (bf16[4,1]{0,1:T(2,128)(2,1)S(1)}, f32[4]{0:T(128)S(1)}, bf16[4,1]{0,1:T(2,128)(2,1)S(1)}, f32[4]{0:T(128)S(1)}) fusion(pred[]{:T(512)} %compare_reduce_fusion.1, s32[4]{0:T(128)S(1)} %copy-done.13, s32[]{:T(128)} %bitcast.30, pred[]{:T(512)} %compare_reduce_fusion), kind=kLoop, calls=%fused_computation.42 | loop fusion | flops 32 | bytes 70 | tf_op jit(solution)/shard_map/reshape.85
  7.6 1.6 %pad_maximum_fusion.weight = bf16[768,576]{1,0:T(8,128)(2,1)S(1)} fusion(bf16[768,192]{1,0:T(8,128)(2,1)} %bitcast.39, bf16[768,192]{1,0:T(8,128)(2,1)} %bitcast.38, bf16[768,192]{1,0:T(8,128)(2,1)} %bitcast.37), kind=kLoop, calls=%fused_computation.5 | loop fusion | flops 2654208 | bytes 1769472 | tf_op jit(solution)/shard_map/concatenate | solution.py:383
  9.3 1.2 slide_project.1
  10.5 2.6 %collective-permute-start = (bf16[1,256,384]{2,1,0:T(8,128)(2,1)S(1)}, bf16[1,256,384]{2,1,0:T(8,128)(2,1)S(1)}, u32[]{:S(2)}, u32[]{:S(2)}) collective-permute-start(bf16[1,256,384]{2,1,0:T(8,128)(2,1)S(1)} %bitcast.32), channel_id=1, source_target_pairs={{0,8},{4,12},{8,0},{12,4},{16,24},{20,28},{24,16},{28,20},{32,40},... | collective-permute-start | bytes 589832 | tf_op jit(solution)/shard_map/ppermute | solution.py:354
  14.1 1.2 collective-permute-start.6
  15.3 1.5 %collective-permute-start.7 = (bf16[2,256,384]{2,1,0:T(8,128)(2,1)}, bf16[2,256,384]{2,1,0:T(8,128)(2,1)}, u32[]{:S(2)}, u32[]{:S(2)}) collective-permute-start(bf16[2,256,384]{2,1,0:T(8,128)(2,1)} %get-tuple-element.60.own), channel_id=1, source_target_pairs={{0,3},{1,0},{2,1},{3,2},{4,7},{5,4},{6,5},{7,6},{8,11},{9,8},{10,9... | collective-permute-start | bytes 1179656 | tf_op jit(solution)/shard_map/ppermute | solution.py:350
  16.7 2.7 %collective-permute-start.11 = (bf16[2,256,384]{2,1,0:T(8,128)(2,1)}, bf16[2,256,384]{2,1,0:T(8,128)(2,1)}, u32[]{:S(2)}, u32[]{:S(2)}) collective-permute-start(bf16[2,256,384]{2,1,0:T(8,128)(2,1)} %get-tuple-element.61.own), channel_id=1, source_target_pairs={{0,3},{1,0},{2,1},{3,2},{4,7},{5,4},{6,5},{7,6},{8,11},{9,8},{10,9... | collective-permute-start | bytes 1179656 | tf_op jit(solution)/shard_map/ppermute | solution.py:350
  20.2 3.0 %collective-permute-start.1 = (bf16[2,128,384]{2,1,0:T(8,128)(2,1)}, bf16[2,128,384]{2,1,0:T(8,128)(2,1)}, u32[]{:S(2)}, u32[]{:S(2)}) collective-permute-start(bf16[2,128,384]{2,1,0:T(8,128)(2,1)} %get-tuple-element.68), channel_id=1, source_target_pairs={{0,16},{4,20},{8,24},{12,28},{16,0},{20,4},{24,8},{28,12},{32,48},... | collective-permute-start | bytes 589832 | tf_op jit(solution)/shard_map/ppermute | solution.py:354
  23.2 1.9 %convolution_convert_fusion = bf16[384,768]{1,0:T(8,128)(2,1)} fusion(bf16[384,1536]{1,0:T(8,128)(2,1)S(1)} %copy-done.14, bf16[1536,768]{1,0:T(8,128)(2,1)S(1)} %copy-done), kind=kOutput, calls=%fused_computation | convolution fusion | flops 906264576 | bytes 4128768 | tf_op jit(solution)/shard_map/dot_general | solution.py:31
  25.1 6.1 %copy.24 = bf16[1536,3,384]{0,2,1:T(8,128)(2,1)} copy(bf16[1536,3,384]{2,0,1:T(8,128)(2,1)} %param.21) | data formatting | bytes 7077888 | tf_op args[4]
  31.2 5.8 %copy.25.weight = bf16[1536,1152]{1,0:T(8,128)(2,1)} copy(bf16[1536,1152]{0,1:T(8,128)(2,1)} %bitcast.34) | data formatting | bytes 7077888 | tf_op jit(solution)/shard_map/reshape | solution.py:404
  37.1 1.2 pad_maximum_fusion.5
  38.3 4.3 %collective-permute-start.2 = (bf16[4,64,384]{2,1,0:T(8,128)(2,1)S(1)}, bf16[4,64,384]{2,1,0:T(8,128)(2,1)S(1)}, u32[]{:S(2)}, u32[]{:S(2)}) collective-permute-start(bf16[4,64,384]{2,1,0:T(8,128)(2,1)S(1)} %get-tuple-element.66), channel_id=1, source_target_pairs={{0,32},{4,36},{8,40},{12,44},{16,48},{20,52},{24,56},{28,60},{32,0... | collective-permute-start | bytes 589832 | tf_op jit(solution)/shard_map/ppermute | solution.py:354
  45.3 2.7 %collective-permute-start.9 = (bf16[1,256,384]{2,1,0:T(8,128)(2,1)S(1)}, bf16[1,256,384]{2,1,0:T(8,128)(2,1)S(1)}, u32[]{:S(2)}, u32[]{:S(2)}) collective-permute-start(bf16[1,256,384]{2,1,0:T(8,128)(2,1)S(1)} %slice.142), channel_id=1, source_target_pairs={{0,3},{1,0},{2,1},{3,2},{4,7},{5,4},{6,5},{7,6},{8,11},{9,8},{10,9... | collective-permute-start | bytes 589832 | tf_op jit(solution)/shard_map/ppermute | solution.py:350
  50.1 2.7 %collective-permute-start.13 = (bf16[1,256,384]{2,1,0:T(8,128)(2,1)S(1)}, bf16[1,256,384]{2,1,0:T(8,128)(2,1)S(1)}, u32[]{:S(2)}, u32[]{:S(2)}) collective-permute-start(bf16[1,256,384]{2,1,0:T(8,128)(2,1)S(1)} %slice.144), channel_id=1, source_target_pairs={{0,3},{1,0},{2,1},{3,2},{4,7},{5,4},{6,5},{7,6},{8,11},{9,8},{10,9... | collective-permute-start | bytes 589832 | tf_op jit(solution)/shard_map/ppermute | solution.py:350
  53.5 1.6 %collective-permute-start.3 = (bf16[8,32,384]{2,1,0:T(8,128)(2,1)S(1)}, bf16[8,32,384]{2,1,0:T(8,128)(2,1)S(1)}, u32[]{:S(2)}, u32[]{:S(2)}) collective-permute-start(bf16[8,32,384]{2,1,0:T(8,128)(2,1)S(1)} %get-tuple-element.64), channel_id=1, source_target_pairs={{0,64},{4,68},{8,72},{12,76},{16,80},{20,84},{24,88},{28,92},{32,9... | collective-permute-start | bytes 589832 | tf_op jit(solution)/shard_map/ppermute | solution.py:354
  55.1 6.4 %encode.2 = f32[2,768]{1,0:T(2,128)S(1)} custom-call(s32[2]{0:T(128)S(1)} %pad_add_fusion.idx, bf16[2,256,384]{2,1,0:T(8,128)(2,1)} %get-tuple-element.60.own, bf16[2,256,384]{2,1,0:T(8,128)(2,1)} %collective-permute-done.6.left, bf16[2,256,384]{2,1,0:T(8,128)(2,1)} %collective-permute-done.7.right, bf16[1,256,384]{2,1,0:T(8,128)(2,1)S(1)} %collective-permute-done.8.far_a, ...), custom_call_target="tpu_custom_call" | custom-call | flops 6000000000 | bytes 8000000 | tf_op jit(solution)/shard_map/encode/pallas_call | solution.py:98
  61.6 2.7 %collective-permute-start.4 = (bf16[16,16,384]{2,1,0:T(8,128)(2,1)S(1)}, bf16[16,16,384]{2,1,0:T(8,128)(2,1)S(1)}, u32[]{:S(2)}, u32[]{:S(2)}) collective-permute-start(bf16[16,16,384]{2,1,0:T(8,128)(2,1)S(1)} %get-tuple-element.62), channel_id=1, source_target_pairs={{0,128},{4,132},{8,136},{12,140},{16,144},{20,148},{24,152},{28,15... | collective-permute-start | bytes 589832 | tf_op jit(solution)/shard_map/ppermute | solution.py:354
  65.7 2.0 %collective-permute-done.4 = bf16[16,16,384]{2,1,0:T(8,128)(2,1)S(1)} collective-permute-done((bf16[16,16,384]{2,1,0:T(8,128)(2,1)S(1)}, bf16[16,16,384]{2,1,0:T(8,128)(2,1)S(1)}, u32[]{:S(2)}, u32[]{:S(2)}) %collective-permute-start.4) | collective-permute-done | bytes 196640 | tf_op jit(solution)/shard_map/ppermute | solution.py:354
  68.6 5.2 %collective-permute-start.5 = (bf16[1536,384]{1,0:T(8,128)(2,1)}, bf16[1536,384]{1,0:T(8,128)(2,1)}, u32[]{:S(2)}, u32[]{:S(2)}) collective-permute-start(bf16[1536,384]{1,0:T(8,128)(2,1)} %constant_dynamic-update-slice_fusion.mine), channel_id=1, source_target_pairs={{0,4},{4,0},{8,12},{12,8},{16,20},{20,16},{24,28},{28,24},{32,36},... | collective-permute-start | bytes 3538952 | tf_op jit(solution)/shard_map/ppermute | solution.py:354
  73.8 6.4 %encode.3 = f32[2,768]{1,0:T(2,128)S(1)} custom-call(s32[2]{0:T(128)S(1)} %pad_add_fusion.idx, bf16[2,256,384]{2,1,0:T(8,128)(2,1)} %get-tuple-element.61.own, bf16[2,256,384]{2,1,0:T(8,128)(2,1)} %collective-permute-done.10.left, bf16[2,256,384]{2,1,0:T(8,128)(2,1)} %collective-permute-done.11.right, ...), custom_call_target="tpu_custom_call" | custom-call | flops 6000000000 | bytes 8000000 | tf_op jit(solution)/shard_map/encode/pallas_call | solution.py:98
  80.5 2.7 %collective-permute-start.15 = (f32[4,768]{1,0:T(4,128)S(1)}, f32[4,768]{1,0:T(4,128)S(1)}, u32[]{:S(2)}, u32[]{:S(2)}) collective-permute-start(f32[4,768]{1,0:T(4,128)S(1)} %fusion.a), channel_id=1, source_target_pairs={{0,3},{1,0},{2,1},{3,2},{4,7},{5,4},{6,5},{7,6},{8,11},{9,8},{10,9... | collective-permute-start | bytes 36872 | tf_op jit(solution)/shard_map/ppermute | solution.py:350
  84.3 3.0 %collective-permute-done.16.d = f32[4,768]{1,0:T(4,128)S(1)} collective-permute-done((f32[4,768]{1,0:T(4,128)S(1)}, f32[4,768]{1,0:T(4,128)S(1)}, u32[]{:S(2)}, u32[]{:S(2)}) %collective-permute-start.16) | collective-permute-done | bytes 12320 | tf_op jit(solution)/shard_map/ppermute | solution.py:350
  88.5 8.0 %all-to-all-start = ((bf16[64,4,640]{2,1,0:T(4,128)(2,1)}), bf16[64,4,640]{2,1,0:T(4,128)(2,1)}, u32[]{:S(2)}, u32[]{:S(2)}) async-start(bf16[64,4,640]{2,1,0:T(4,128)(2,1)} %broadcast_in_dim.17), calls=%async_computation | async-start | bytes 655360 | tf_op jit(solution)/shard_map/all_to_all | solution.py:416
  96.9 12.8 %all-to-all-done = bf16[64,4,640]{2,1,0:T(4,128)(2,1)} async-done(((bf16[64,4,640]{2,1,0:T(4,128)(2,1)}), bf16[64,4,640]{2,1,0:T(4,128)(2,1)}, u32[]{:S(2)}, u32[]{:S(2)}) %all-to-all-start) | async-done | bytes 327712 | tf_op jit(solution)/shard_map/all_to_all | solution.py:416
  113.1 2.3 %key_flags.1.bias = f32[40,1024]{1,0:T(8,128)S(1)} custom-call(s32[2]{0:T(128)S(1)} %pad_add_fusion.idx, s32[256,1]{1,0:T(8,128)S(1)} %reshape.136.pos), custom_call_target="tpu_custom_call" | custom-call | tf_op jit(solution)/shard_map/key_flags/pallas_call | solution.py:228
  115.3 4.8 %attend.1 = (bf16[128,192]{1,0:T(8,128)(2,1)S(1)}, bf16[128,192]{1,0:T(8,128)(2,1)S(1)}, bf16[128,192]{1,0:T(8,128)(2,1)S(1)}, bf16[128,192]{1,0:T(8,128)(2,1)S(1)}) custom-call(s32[2]{0:T(128)S(1)} %pad_add_fusion.idx, f32[128,192]{1,0:T(8,128)S(1)} %get-tuple-element.47.q_cache, bf16[1536,384]{1,0:T(8,128)(2,1)} %constant_dynamic-update-slice_fusion.mine, ...), custom_call_target="tpu_custom_call" | custom-call | tf_op jit(solution)/shard_map/attend/pallas_call | solution.py:329
  121.7 1.8 %collective-permute-start.19 = (bf16[128,192]{1,0:T(8,128)(2,1)S(1)}, bf16[128,192]{1,0:T(8,128)(2,1)S(1)}, u32[]{:S(2)}, u32[]{:S(2)}) collective-permute-start(bf16[128,192]{1,0:T(8,128)(2,1)S(1)} %get-tuple-element.52), channel_id=1, source_target_pairs={{0,3},{1,0},{2,1},{3,2},{4,7},{5,4},{6,5},{7,6},{8,11},{9,8},{10,9... | collective-permute-start | bytes 147464 | tf_op jit(solution)/shard_map/ppermute | solution.py:350
  123.5 3.7 %collective-permute-done.17.b = bf16[128,192]{1,0:T(8,128)(2,1)S(1)} collective-permute-done((bf16[128,192]{1,0:T(8,128)(2,1)S(1)}, bf16[128,192]{1,0:T(8,128)(2,1)S(1)}, u32[]{:S(2)}, u32[]{:S(2)}) %collective-permute-start.17) | collective-permute-done | bytes 49184 | tf_op jit(solution)/shard_map/ppermute | solution.py:350
  127.8 1.6 %combine.1 = bf16[128,192]{1,0:T(8,128)(2,1)} custom-call(bf16[128,192]{1,0:T(8,128)(2,1)} %copy-done.3, bf16[128,192]{1,0:T(8,128)(2,1)} %copy-done.8, bf16[128,192]{1,0:T(8,128)(2,1)} %copy-done.9, bf16[128,192]{1,0:T(8,128)(2,1)} %copy-done.10), custom_call_target="tpu_custom_call" | custom-call | tf_op jit(solution)/shard_map/combine/pallas_call | solution.py:422
  129.4 1.6 %copy.30 = bf16[128,192]{0,1:T(8,128)(2,1)} copy(bf16[128,192]{1,0:T(8,128)(2,1)} %combine.1) | data formatting | bytes 98304 | tf_op jit(solution)/shard_map/combine/pallas_call | solution.py:422
  (99 shorter events, 22.5 us)
Async XLA Ops:
  0.0 23.2 %copy-start = (bf16[1536,768]{1,0:T(8,128)(2,1)S(1)}, bf16[1536,768]{1,0:T(8,128)(2,1)}, u32[]{:S(2)}) copy-start(bf16[1536,768]{1,0:T(8,128)(2,1)} %param.23) | copy-start | bytes 7077892
  2.6 3.6 %copy-start.13 = (s32[4]{0:T(128)S(1)}, s32[4]{0:T(128)}, u32[]{:S(2)}) copy-start(s32[4]{0:T(128)} %param.18) | copy-start | bytes 52
  5.4 3.9 %copy-start.2 = (bf16[128,768]{1,0:T(8,128)(2,1)S(1)}, bf16[128,768]{1,0:T(8,128)(2,1)}, u32[]{:S(2)}) copy-start(bf16[128,768]{1,0:T(8,128)(2,1)} %cache.1) | copy-start | bytes 589828
  7.6 5.5 %copy-start.5 = (bf16[4,256,384]{2,1,0:T(8,128)(2,1)S(1)}, bf16[4,256,384]{2,1,0:T(8,128)(2,1)}, u32[]{:S(2)}) copy-start(bf16[4,256,384]{2,1,0:T(8,128)(2,1)} %param.17) | copy-start | bytes 2359300
  10.5 12.7 %copy-start.14 = (bf16[384,1536]{1,0:T(8,128)(2,1)S(1)}, bf16[384,1536]{1,0:T(8,128)(2,1)}, u32[]{:S(2)}) copy-start(bf16[384,1536]{1,0:T(8,128)(2,1)} %param.22) | copy-start | bytes 3538948
  10.5 8.9 %collective-permute-start = (bf16[1,256,384]{2,1,0:T(8,128)(2,1)S(1)}, bf16[1,256,384]{2,1,0:T(8,128)(2,1)S(1)}, u32[]{:S(2)}, u32[]{:S(2)}) collective-permute-start(bf16[1,256,384]{2,1,0:T(8,128)(2,1)S(1)} %bitcast.32), channel_id=1, source_target_pairs={{0,8},{4,12},{8,0},{12,4},{16,24},{20,28},{24,16},{28,20},{32,40},... | collective-permute-start | bytes 589832 | tf_op jit(solution)/shard_map/ppermute | solution.py:354
  14.1 29.2 %collective-permute-start.6 = (bf16[2,256,384]{2,1,0:T(8,128)(2,1)}, bf16[2,256,384]{2,1,0:T(8,128)(2,1)}, u32[]{:S(2)}, u32[]{:S(2)}) collective-permute-start(bf16[2,256,384]{2,1,0:T(8,128)(2,1)} %get-tuple-element.60.own), channel_id=1, source_target_pairs={{0,1},{1,2},{2,3},{3,0},{4,5},{5,6},{6,7},{7,4},{8,9},{9,10},{10,1... | collective-permute-start | bytes 1179656 | tf_op jit(solution)/shard_map/ppermute | solution.py:350
  15.3 29.1 %collective-permute-start.7 = (bf16[2,256,384]{2,1,0:T(8,128)(2,1)}, bf16[2,256,384]{2,1,0:T(8,128)(2,1)}, u32[]{:S(2)}, u32[]{:S(2)}) collective-permute-start(bf16[2,256,384]{2,1,0:T(8,128)(2,1)} %get-tuple-element.60.own), channel_id=1, source_target_pairs={{0,3},{1,0},{2,1},{3,2},{4,7},{5,4},{6,5},{7,6},{8,11},{9,8},{10,9... | collective-permute-start | bytes 1179656 | tf_op jit(solution)/shard_map/ppermute | solution.py:350
  16.7 31.3 %collective-permute-start.10 = (bf16[2,256,384]{2,1,0:T(8,128)(2,1)}, bf16[2,256,384]{2,1,0:T(8,128)(2,1)}, u32[]{:S(2)}, u32[]{:S(2)}) collective-permute-start(bf16[2,256,384]{2,1,0:T(8,128)(2,1)} %get-tuple-element.61.own), channel_id=1, source_target_pairs={{0,1},{1,2},{2,3},{3,0},{4,5},{5,6},{6,7},{7,4},{8,9},{9,10},{10,1... | collective-permute-start | bytes 1179656 | tf_op jit(solution)/shard_map/ppermute | solution.py:350
  16.7 32.4 %collective-permute-start.11 = (bf16[2,256,384]{2,1,0:T(8,128)(2,1)}, bf16[2,256,384]{2,1,0:T(8,128)(2,1)}, u32[]{:S(2)}, u32[]{:S(2)}) collective-permute-start(bf16[2,256,384]{2,1,0:T(8,128)(2,1)} %get-tuple-element.61.own), channel_id=1, source_target_pairs={{0,3},{1,0},{2,1},{3,2},{4,7},{5,4},{6,5},{7,6},{8,11},{9,8},{10,9... | collective-permute-start | bytes 1179656 | tf_op jit(solution)/shard_map/ppermute | solution.py:350
  20.2 16.8 %collective-permute-start.1 = (bf16[2,128,384]{2,1,0:T(8,128)(2,1)}, bf16[2,128,384]{2,1,0:T(8,128)(2,1)}, u32[]{:S(2)}, u32[]{:S(2)}) collective-permute-start(bf16[2,128,384]{2,1,0:T(8,128)(2,1)} %get-tuple-element.68), channel_id=1, source_target_pairs={{0,16},{4,20},{8,24},{12,28},{16,0},{20,4},{24,8},{28,12},{32,48},... | collective-permute-start | bytes 589832 | tf_op jit(solution)/shard_map/ppermute | solution.py:354
  31.2 5.8 %copy-start.11 = (f32[1536]{0:T(1024)S(1)}, f32[1536]{0:T(1024)}, u32[]{:S(2)}) copy-start(f32[1536]{0:T(1024)} %param.20) | copy-start | bytes 18436
  37.0 5.6 %copy-start.6 = (bf16[2,128,384]{2,1,0:T(8,128)(2,1)S(1)}, bf16[2,128,384]{2,1,0:T(8,128)(2,1)}, u32[]{:S(2)}) copy-start(bf16[2,128,384]{2,1,0:T(8,128)(2,1)} %get-tuple-element.69) | copy-start | bytes 589828
  37.1 18.0 %copy-start.1 = (bf16[1536,1152]{1,0:T(8,128)(2,1)S(1)}, bf16[1536,1152]{1,0:T(8,128)(2,1)}, u32[]{:S(2)}) copy-start(bf16[1536,1152]{1,0:T(8,128)(2,1)} %copy.25.weight) | copy-start | bytes 10616836
  38.3 15.2 %collective-permute-start.2 = (bf16[4,64,384]{2,1,0:T(8,128)(2,1)S(1)}, bf16[4,64,384]{2,1,0:T(8,128)(2,1)S(1)}, u32[]{:S(2)}, u32[]{:S(2)}) collective-permute-start(bf16[4,64,384]{2,1,0:T(8,128)(2,1)S(1)} %get-tuple-element.66), channel_id=1, source_target_pairs={{0,32},{4,36},{8,40},{12,44},{16,48},{20,52},{24,56},{28,60},{32,0... | collective-permute-start | bytes 589832 | tf_op jit(solution)/shard_map/ppermute | solution.py:354
  44.3 10.8 %collective-permute-start.8 = (bf16[1,256,384]{2,1,0:T(8,128)(2,1)S(1)}, bf16[1,256,384]{2,1,0:T(8,128)(2,1)S(1)}, u32[]{:S(2)}, u32[]{:S(2)}) collective-permute-start(bf16[1,256,384]{2,1,0:T(8,128)(2,1)S(1)} %slice.141), channel_id=1, source_target_pairs={{0,1},{1,2},{2,3},{3,0},{4,5},{5,6},{6,7},{7,4},{8,9},{9,10},{10,1... | collective-permute-start | bytes 589832 | tf_op jit(solution)/shard_map/ppermute | solution.py:350
  45.3 9.8 %collective-permute-start.9 = (bf16[1,256,384]{2,1,0:T(8,128)(2,1)S(1)}, bf16[1,256,384]{2,1,0:T(8,128)(2,1)S(1)}, u32[]{:S(2)}, u32[]{:S(2)}) collective-permute-start(bf16[1,256,384]{2,1,0:T(8,128)(2,1)S(1)} %slice.142), channel_id=1, source_target_pairs={{0,3},{1,0},{2,1},{3,2},{4,7},{5,4},{6,5},{7,6},{8,11},{9,8},{10,9... | collective-permute-start | bytes 589832 | tf_op jit(solution)/shard_map/ppermute | solution.py:350
  49.0 24.8 %collective-permute-start.12 = (bf16[1,256,384]{2,1,0:T(8,128)(2,1)S(1)}, bf16[1,256,384]{2,1,0:T(8,128)(2,1)S(1)}, u32[]{:S(2)}, u32[]{:S(2)}) collective-permute-start(bf16[1,256,384]{2,1,0:T(8,128)(2,1)S(1)} %slice.143), channel_id=1, source_target_pairs={{0,1},{1,2},{2,3},{3,0},{4,5},{5,6},{6,7},{7,4},{8,9},{9,10},{10,1... | collective-permute-start | bytes 589832 | tf_op jit(solution)/shard_map/ppermute | solution.py:350
  50.1 23.7 %collective-permute-start.13 = (bf16[1,256,384]{2,1,0:T(8,128)(2,1)S(1)}, bf16[1,256,384]{2,1,0:T(8,128)(2,1)S(1)}, u32[]{:S(2)}, u32[]{:S(2)}) collective-permute-start(bf16[1,256,384]{2,1,0:T(8,128)(2,1)S(1)} %slice.144), channel_id=1, source_target_pairs={{0,3},{1,0},{2,1},{3,2},{4,7},{5,4},{6,5},{7,6},{8,11},{9,8},{10,9... | collective-permute-start | bytes 589832 | tf_op jit(solution)/shard_map/ppermute | solution.py:350
  53.5 8.0 %collective-permute-start.3 = (bf16[8,32,384]{2,1,0:T(8,128)(2,1)S(1)}, bf16[8,32,384]{2,1,0:T(8,128)(2,1)S(1)}, u32[]{:S(2)}, u32[]{:S(2)}) collective-permute-start(bf16[8,32,384]{2,1,0:T(8,128)(2,1)S(1)} %get-tuple-element.64), channel_id=1, source_target_pairs={{0,64},{4,68},{8,72},{12,76},{16,80},{20,84},{24,88},{28,92},{32,9... | collective-permute-start | bytes 589832 | tf_op jit(solution)/shard_map/ppermute | solution.py:354
  61.6 6.1 %collective-permute-start.4 = (bf16[16,16,384]{2,1,0:T(8,128)(2,1)S(1)}, bf16[16,16,384]{2,1,0:T(8,128)(2,1)S(1)}, u32[]{:S(2)}, u32[]{:S(2)}) collective-permute-start(bf16[16,16,384]{2,1,0:T(8,128)(2,1)S(1)} %get-tuple-element.62), channel_id=1, source_target_pairs={{0,128},{4,132},{8,136},{12,140},{16,144},{20,148},{24,152},{28,15... | collective-permute-start | bytes 589832 | tf_op jit(solution)/shard_map/ppermute | solution.py:354
  67.7 6.1 %copy-start.4 = (bf16[32,16,384]{2,1,0:T(8,128)(2,1)}, bf16[32,16,384]{2,1,0:T(8,128)(2,1)S(1)}, u32[]{:S(2)}) copy-start(bf16[32,16,384]{2,1,0:T(8,128)(2,1)S(1)} %pad_maximum_fusion.2) | copy-start | bytes 1179652
  68.6 11.6 %copy-start.15 = (bf16[384,768]{1,0:T(8,128)(2,1)S(1)}, bf16[384,768]{1,0:T(8,128)(2,1)}, u32[]{:S(2)}) copy-start(bf16[384,768]{1,0:T(8,128)(2,1)} %convolution_convert_fusion) | copy-start | bytes 1769476
  68.6 42.1 %collective-permute-start.5 = (bf16[1536,384]{1,0:T(8,128)(2,1)}, bf16[1536,384]{1,0:T(8,128)(2,1)}, u32[]{:S(2)}, u32[]{:S(2)}) collective-permute-start(bf16[1536,384]{1,0:T(8,128)(2,1)} %constant_dynamic-update-slice_fusion.mine), channel_id=1, source_target_pairs={{0,4},{4,0},{8,12},{12,8},{16,20},{20,16},{24,28},{28,24},{32,36},... | collective-permute-start | bytes 3538952 | tf_op jit(solution)/shard_map/ppermute | solution.py:354
  80.5 3.8 %collective-permute-start.14 = (f32[4,768]{1,0:T(4,128)S(1)}, f32[4,768]{1,0:T(4,128)S(1)}, u32[]{:S(2)}, u32[]{:S(2)}) collective-permute-start(f32[4,768]{1,0:T(4,128)S(1)} %fusion.a), channel_id=1, source_target_pairs={{0,1},{1,2},{2,3},{3,0},{4,5},{5,6},{6,7},{7,4},{8,9},{9,10},{10,1... | collective-permute-start | bytes 36872 | tf_op jit(solution)/shard_map/ppermute | solution.py:350
  80.5 3.8 %collective-permute-start.15 = (f32[4,768]{1,0:T(4,128)S(1)}, f32[4,768]{1,0:T(4,128)S(1)}, u32[]{:S(2)}, u32[]{:S(2)}) collective-permute-start(f32[4,768]{1,0:T(4,128)S(1)} %fusion.a), channel_id=1, source_target_pairs={{0,3},{1,0},{2,1},{3,2},{4,7},{5,4},{6,5},{7,6},{8,11},{9,8},{10,9... | collective-permute-start | bytes 36872 | tf_op jit(solution)/shard_map/ppermute | solution.py:350
  83.2 4.0 %collective-permute-start.16 = (f32[4,768]{1,0:T(4,128)S(1)}, f32[4,768]{1,0:T(4,128)S(1)}, u32[]{:S(2)}, u32[]{:S(2)}) collective-permute-start(f32[4,768]{1,0:T(4,128)S(1)} %fusion.a), channel_id=1, source_target_pairs={{0,2},{1,3},{2,0},{3,1},{4,6},{5,7},{6,4},{7,5},{8,10},{9,11},{10,... | collective-permute-start | bytes 36872 | tf_op jit(solution)/shard_map/ppermute | solution.py:350
  87.6 8.9 %copy-start.7 = (bf16[192,768]{1,0:T(8,128)(2,1)S(1)}, bf16[192,768]{1,0:T(8,128)(2,1)}, u32[]{:S(2)}) copy-start(bf16[192,768]{1,0:T(8,128)(2,1)} %param.27) | copy-start | bytes 884740
  88.5 21.2 %all-to-all-start = ((bf16[64,4,640]{2,1,0:T(4,128)(2,1)}), bf16[64,4,640]{2,1,0:T(4,128)(2,1)}, u32[]{:S(2)}, u32[]{:S(2)}) async-start(bf16[64,4,640]{2,1,0:T(4,128)(2,1)} %broadcast_in_dim.17), calls=%async_computation | async-start | bytes 655360 | tf_op jit(solution)/shard_map/all_to_all | solution.py:416
  120.8 6.3 %collective-permute-start.17 = (bf16[128,192]{1,0:T(8,128)(2,1)S(1)}, bf16[128,192]{1,0:T(8,128)(2,1)S(1)}, u32[]{:S(2)}, u32[]{:S(2)}) collective-permute-start(bf16[128,192]{1,0:T(8,128)(2,1)S(1)} %get-tuple-element.50), channel_id=1, source_target_pairs={{0,1},{1,2},{2,3},{3,0},{4,5},{5,6},{6,7},{7,4},{8,9},{9,10},{10,1... | collective-permute-start | bytes 147464 | tf_op jit(solution)/shard_map/ppermute | solution.py:350
  120.8 6.4 %collective-permute-start.18 = (bf16[128,192]{1,0:T(8,128)(2,1)S(1)}, bf16[128,192]{1,0:T(8,128)(2,1)S(1)}, u32[]{:S(2)}, u32[]{:S(2)}) collective-permute-start(bf16[128,192]{1,0:T(8,128)(2,1)S(1)} %get-tuple-element.51), channel_id=1, source_target_pairs={{0,2},{1,3},{2,0},{3,1},{4,6},{5,7},{6,4},{7,5},{8,10},{9,11},{10,... | collective-permute-start | bytes 147464 | tf_op jit(solution)/shard_map/ppermute | solution.py:350
  121.7 5.5 %collective-permute-start.19 = (bf16[128,192]{1,0:T(8,128)(2,1)S(1)}, bf16[128,192]{1,0:T(8,128)(2,1)S(1)}, u32[]{:S(2)}, u32[]{:S(2)}) collective-permute-start(bf16[128,192]{1,0:T(8,128)(2,1)S(1)} %get-tuple-element.52), channel_id=1, source_target_pairs={{0,3},{1,0},{2,1},{3,2},{4,7},{5,4},{6,5},{7,6},{8,11},{9,8},{10,9... | collective-permute-start | bytes 147464 | tf_op jit(solution)/shard_map/ppermute | solution.py:350
  (5 other events, 6.0 us)

commit v2 on v1

v2 whole, which is shorter than its diff:
```python
import functools
import math

import jax
import jax.numpy as jnp
from jax import lax
from jax.experimental import pallas as pl
from jax.experimental.pallas import tpu as pltpu
from jax.sharding import PartitionSpec as P

HDT = 64
HDL = 48
BRANCHES = 5
EPSILON = 1e-05
FLOOR_SCORE = -1e30
BF = jnp.bfloat16
F32 = jnp.float32
ROWS = 128
NEAR = 3
NEAR_ROWS = 224


def params(mib=40):
    return pltpu.CompilerParams(vmem_limit_bytes=mib * 2**20)


def whole(kind=pltpu.VMEM):
    return pl.BlockSpec(memory_space=kind)


def dot(a, b):
    return jnp.dot(a, b, preferred_element_type=F32)


def dot_t(a, b):
    return lax.dot_general(a, b, (((1,), (1,)), ((), ())), preferred_element_type=F32)


def iota(shape, dim):
    return lax.broadcasted_iota(jnp.int32, shape, dim)


def encode_kernel(idx, own, left, right, far, gain, weight, out, xn, qk):
    mp = idx[0]
    tokens, width = own.shape[1], own.shape[2]
    unit = HDT ** (-0.5) * math.log2(math.e)
    features = 4 * width
    blocks = [lax.rem(mp + shift, 4) for shift in (0, 3, 1, 2)]
    starts = [pl.multiple_of(block * width, 128) for block in blocks]
    for t in range(2):
        parts = [own[t], left[t], right[t], far[t]]
        wide = [part.astype(F32) for part in parts]
        total = sum(jnp.sum(part, axis=-1, keepdims=True) for part in wide)
        mean = total * (1.0 / features)
        centred = [part - mean for part in wide]
        spread = sum(jnp.sum(part * part, axis=-1, keepdims=True) for part in centred)
        scale = lax.rsqrt(spread * (1.0 / features) + EPSILON)
        for d in range(4):
            xn[d, t * tokens : (t + 1) * tokens, :] = (
                centred[d] * scale * gain[pl.ds(blocks[d], 1), 0, :]
            ).astype(BF)
        out[t : t + 1, width : 2 * width] = jnp.sum(wide[0], axis=0, keepdims=True) * (1.0 / tokens)
    for part in range(2):
        acc = dot(xn[0], weight[part, pl.ds(starts[0], width), :])
        for d in range(1, 4):
            acc = acc + dot(xn[d], weight[part, pl.ds(starts[d], width), :])
        qk[:, part * width : (part + 1) * width] = acc.astype(BF)
    lane = iota((tokens, 2 * HDT), 1)
    pooled = [[] for _ in range(4)]
    for t in range(2):
        low, high = t * tokens, (t + 1) * tokens
        rows = []
        for pair in range(width // (2 * HDT)):
            q2 = qk[low:high, pair * 128 : (pair + 1) * 128]
            k2 = qk[low:high, width + pair * 128 : width + (pair + 1) * 128]
            for half in range(2):
                qm = jnp.where((lane >= HDT) == (half == 1), q2, jnp.zeros((), BF))
                s = dot_t(qm, k2)
                e = jnp.exp2((s - jnp.max(s, axis=-1, keepdims=True)) * unit)
                share = 1.0 / (jnp.sum(e, axis=-1, keepdims=True) * tokens)
                rows.append(jnp.sum(e * share, axis=0, keepdims=True))
        rows.append(jnp.zeros((8 - len(rows), tokens), F32))
        mix = jnp.concatenate(rows, axis=0).astype(BF)
        for d in range(4):
            pooled[d].append(dot(mix, xn[d, low:high, :]))
    acc = jnp.zeros((16, width), F32)
    for d in range(4):
        acc = acc + dot(
            jnp.concatenate(pooled[d], axis=0).astype(BF),
            weight[2, pl.ds(starts[d], width), :],
        )
    keep = (iota((16, width), 0) & 7) == (iota((16, width), 1) >> 6)
    acc = jnp.where(keep, acc, 0.0)
    for t in range(2):
        out[t : t + 1, 0:width] = jnp.sum(acc[t * 8 : (t + 1) * 8], axis=0, keepdims=True)


def encode(idx, chunk, own, left, right, far, gain, weight):
    tokens, width = own.shape[1], own.shape[2]
    block = pl.BlockSpec((2, tokens, width), lambda i: (chunk, 0, 0))
    far_block = pl.BlockSpec((2, tokens, width), lambda i: (0, 0, 0))
    return pl.pallas_call(
        encode_kernel,
        grid=(1,),
        out_shape=jax.ShapeDtypeStruct((2, 2 * width), F32),
        in_specs=[whole(pltpu.SMEM), block, block, block, far_block] + [whole()] * 2,
        out_specs=whole(),
        scratch_shapes=[
            pltpu.VMEM((4, 2 * tokens, width), BF),
            pltpu.VMEM((2 * tokens, 2 * width), BF),
        ],
        compiler_params=params(),
        cost_estimate=pl.CostEstimate(
            flops=6 * 10**9, bytes_accessed=8 * 10**6, transcendentals=8 * 10**5
        ),
        name="encode",
    )(idx, own, left, right, far, gain, weight)


def norm_rows(x, gain):
    mean = jnp.mean(x, axis=-1, keepdims=True)
    centre = x - mean
    spread = jnp.mean(centre * centre, axis=-1, keepdims=True)
    return (centre * lax.rsqrt(spread + EPSILON) * gain).astype(BF)


def slot_digits(idx, slot):
    place = jnp.where(slot < idx[2], idx[3 + slot], -64)
    return (place >> 6).astype(F32), (place & 63).astype(F32)


def embed_kernel(idx, a, b, c, d, gain, weight, out):
    width = weight.shape[0]
    third = width // 3
    total = (a[...] + b[...]) + (c[...] + d[...])
    normed = norm_rows(total.astype(BF).astype(F32), gain[...])
    out[:, 0 : 2 * third] = dot_t(normed, weight[third:, :]).astype(BF)
    out[:, 2 * third : width] = dot_t(normed, weight[0:third, :]).astype(BF)
    shape = (out.shape[0], out.shape[1] - width)
    row, column = iota(shape, 0), iota(shape, 1)
    tail = jnp.zeros(shape, F32)
    for slot in range(shape[0]):
        high, low = slot_digits(idx, slot)
        tail = jnp.where((row == slot) & (column == 0), high, tail)
        tail = jnp.where((row == slot) & (column == 1), low, tail)
    out[:, width:] = tail.astype(BF)


def embed_rows(idx, parts, gain, weight):
    rows, width = parts[0].shape[0], weight.shape[0]
    return pl.pallas_call(
        embed_kernel,
        out_shape=jax.ShapeDtypeStruct((rows, width + 64), BF),
        in_specs=[whole(pltpu.SMEM)] + [whole()] * 6,
        out_specs=whole(),
        compiler_params=params(),
        name="embed_rows",
    )(idx, *parts, gain, weight)


def rev4(x):
    return ((x & 1) << 3) | ((x & 2) << 1) | ((x & 4) >> 1) | ((x & 8) >> 3)


def pick_start(head, level):
    return pl.multiple_of((rev4(head & 15) >> (4 - level)) * (ROWS >> level), 8)


def local_row(j, level, head):
    bits = j >> 3
    free = 4 - level
    turned = rev4(bits) >> (4 - free) if free else bits * 0
    return (j & 7) * 16 + (turned << level) + (head & ((1 << level) - 1))


def slide_kernel(idx, cache, gain, weight, q_out, near, light, kv):
    heads_width = q_out.shape[1]
    first_head = idx[0] * 4
    row = iota((ROWS, ROWS), 0)
    turn = (local_row(row, 0, 0) == iota((ROWS, ROWS), 1)).astype(BF)
    normed = norm_rows(cache[...].astype(F32), gain[...])
    normed = dot(turn, normed).astype(BF)
    q_out[...] = dot_t(normed, weight[0:heads_width, :]).astype(BF).astype(F32)
    kv[...] = dot_t(normed, weight[heads_width:, :]).astype(BF).astype(F32)
    base = 0
    for level in range(BRANCHES):
        n = ROWS >> level
        column = iota((n, 2 * heads_width), 1)
        column = jnp.where(column >= heads_width, column - heads_width, column)
        got = jnp.zeros((n, 2 * heads_width), F32)
        for h in range(4):
            here = (column >= h * HDL) & (column < (h + 1) * HDL)
            got = jnp.where(here, kv[pl.ds(pick_start(first_head + h, level), n), :], got)
        if level == BRANCHES - 1:
            lane = iota((8, 2 * heads_width), 1)
            tail = jnp.zeros((8, 2 * heads_width), F32)
            for slot in range(4):
                high, low = slot_digits(idx, slot)
                tail = jnp.where(lane == slot, high, jnp.where(lane == slot + 4, low, tail))
            got = jnp.concatenate([got, tail], axis=0)
        picks = near if level < NEAR else light
        base = 0 if level == NEAR else base
        picks[base : base + got.shape[0], :] = got.astype(BF)
        base += n


def slide_project(idx, cache, gain, weight):
    hw = weight.shape[0] // 3
    return pl.pallas_call(
        slide_kernel,
        out_shape=(
            jax.ShapeDtypeStruct((ROWS, hw), F32),
            jax.ShapeDtypeStruct((NEAR_ROWS, 2 * hw), BF),
            jax.ShapeDtypeStruct((32, 2 * hw), BF),
        ),
        in_specs=[whole(pltpu.SMEM)] + [whole()] * 3,
        out_specs=(whole(),) * 3,
        scratch_shapes=[pltpu.VMEM((ROWS, 2 * hw), F32)],
        compiler_params=params(),
        name="slide_project",
    )(idx, cache, gain, weight)


def flag_kernel(idx, pos, out):
    first_head, seq = idx[0] * 4, idx[1]
    for level in range(BRANCHES):
        last = level == BRANCHES - 1
        keys = 1024 if last else 512
        n = 16 if last else ROWS >> level
        shift = n.bit_length() - 1
        k = iota((8, keys), 1)
        j = k & (n - 1)
        source = (seq & -(4 << level)) + (k >> shift)
        for h in range(4):
            r = level * 8 + h
            if level == 0 and h > 0:
                out[r : r + 1, 0:keys] = out[0:1, 0:keys]
                continue
            place = source * ROWS + local_row(j & 7 if last else j, level, first_head + h)
            hit = jnp.max(jnp.where(pos[...] == place[0:1], 1.0, 0.0), axis=0, keepdims=True)
            gone = (hit > 0.0) | (j[0:1] >= 8) if last else hit > 0.0
            out[r : r + 1, 0:keys] = jnp.where(gone, FLOOR_SCORE, 0.0)


def key_flags(idx, pos):
    return pl.pallas_call(
        flag_kernel,
        out_shape=jax.ShapeDtypeStruct((8 * BRANCHES, 1024), F32),
        in_specs=[whole(pltpu.SMEM), whole()],
        out_specs=whole(),
        compiler_params=params(),
        name="key_flags",
    )(idx, pos)


def depth_of(x):
    return sum(((x & mask) == 0).astype(jnp.int32) for mask in (1, 3, 7, 15))


def attend_kernel(
    idx, q_cache, group, light, bias, emb, out_w, o0, o1, o2, o3, q, kv, peak, total, acc, sems
):
    mp, seq = idx[0], idx[1]
    first_head = mp * 4
    hw = q_cache.shape[1]
    scale = HDL ** (-0.5)
    slots = emb.shape[0]
    copies = [[] for _ in range(NEAR)]
    sem = 0
    for level in range(NEAR):
        shards, n = 4 << level, ROWS >> level
        begin = (seq & 15) & -shards
        first_row = sum(ROWS >> b for b in range(level))
        for i in range(shards):
            at = pl.multiple_of((begin + i) * NEAR_ROWS + first_row, 16)
            copy = pltpu.make_async_copy(
                group.at[pl.ds(at, n)],
                kv.at[pl.ds(level * 512 + i * n, n)],
                sems.at[sem],
            )
            copy.start()
            copies[level].append(copy)
            sem += 1
    for i in range(32):
        kv[1536 + i * 16 : 1552 + i * 16, :] = light[(seq & 32) + i, 0:16, :]
    for i in range(64):
        kv[2048 + i * 16 : 2064 + i * 16, :] = light[i, 16:32, :]
    tail = emb[:, 3 * hw :]
    col = iota((8, tail.shape[1]), 1)
    digits = jnp.where(col == 0, 64.0, jnp.where(col == 1, 1.0, 0.0)).astype(BF)
    pos = dot_t(digits, tail).astype(jnp.int32)[0:1]
    own = seq * ROWS + local_row(iota((ROWS, 1), 0), 0, 0)
    match = own == pos
    found = jnp.max(match.astype(jnp.int32), axis=1, keepdims=True) > 0
    placed = dot(match.astype(BF), emb[:, 2 * hw : 3 * hw])
    q[...] = jnp.where(found, placed, q_cache[...])

    def head_mask(n, h):
        column = iota((n, hw), 1)
        return (column >= h * HDL) & (column < (h + 1) * HDL)

    def queries(level):
        n = ROWS >> level
        got = []
        for h in range(4):
            rows = q[...] if level == 0 else q[pl.ds(pick_start(first_head + h, level), n), :]
            got.append(jnp.where(head_mask(n, h), rows, 0.0))
        return jnp.concatenate(got, axis=0).astype(BF)

    full_q = queries(0)
    s = dot_t(full_q, emb[:, 0:hw]) * scale
    cross = (pos ^ (seq * ROWS)) >> 9
    first = sum(((cross >> b) != 0).astype(jnp.int32) for b in range(4))
    times = []
    for h in range(4):
        q_depth = depth_of(own ^ (first_head + h))
        k_depth = jnp.where(pos < 0, -1, depth_of(pos ^ (first_head + h)) - first)
        times.append(jnp.maximum(jnp.minimum(k_depth, q_depth - first) + 1, 0))
    times = jnp.concatenate(times, axis=0).astype(F32)
    s = jnp.where(times > 0.0, s, FLOOR_SCORE)
    m = jnp.max(s, axis=-1, keepdims=True)
    e = times * jnp.exp(s - m)
    peak[...] = jnp.broadcast_to(m, peak.shape)
    total[...] = jnp.broadcast_to(jnp.sum(e, axis=-1, keepdims=True), total.shape)
    acc[...] = dot(e.astype(BF), emb[:, hw : 2 * hw])

    for level in range(BRANCHES):
        n = ROWS >> level
        qb = full_q if level == 0 else queries(level)
        for copy in copies[level] if level < NEAR else ():
            copy.wait()
        low, keys = 512 * level, 1024 if level == BRANCHES - 1 else 512
        s = dot_t(qb, kv[low : low + keys, 0:hw]) * scale
        s = s.reshape(4, n, keys) + bias[level * 8 : level * 8 + 4, 0:keys][:, None, :]
        s = s.reshape(4 * n, keys)
        m = jnp.max(s, axis=-1, keepdims=True)
        e = jnp.exp(s - m)
        t = jnp.sum(e, axis=-1, keepdims=True)
        o = dot(e.astype(BF), kv[low : low + keys, hw : 2 * hw])
        for h in range(4):
            start = h * ROWS + (0 if level == 0 else pick_start(first_head + h, level))
            at = pl.ds(pl.multiple_of(start, 8), n)
            part = slice(h * n, (h + 1) * n)
            before = peak[at, :]
            after = jnp.maximum(before, m[part])
            keep, add = jnp.exp(before - after), jnp.exp(m[part] - after)
            peak[at, :] = after
            total[at, :] = total[at, :] * keep + t[part] * add
            acc[at, :] = acc[at, :] * keep[:, 0:1] + o[part] * add[:, 0:1]

    attended = jnp.zeros((ROWS, hw), F32)
    for h in range(4):
        rows = slice(h * ROWS, (h + 1) * ROWS)
        attended = jnp.where(head_mask(ROWS, h), acc[rows, :] / total[rows, 0:1], attended)
    turn = (local_row(iota((ROWS, ROWS), 1), 0, 0) == iota((ROWS, ROWS), 0)).astype(BF)
    attended = dot(turn, attended.astype(BF)).astype(BF)
    for d, o in enumerate((o0, o1, o2, o3)):
        o[...] = dot(attended, out_w[lax.rem(mp + d, 4)]).astype(BF)


def attend(idx, q_cache, group, light, bias, emb, out_w):
    hw = q_cache.shape[1]
    return pl.pallas_call(
        attend_kernel,
        out_shape=(jax.ShapeDtypeStruct((ROWS, hw), BF),) * 4,
        in_specs=[whole(pltpu.SMEM), whole(), whole(pl.ANY)] + [whole()] * 4,
        out_specs=(whole(),) * 4,
        scratch_shapes=[
            pltpu.VMEM((ROWS, hw), F32),
            pltpu.VMEM((3072, 2 * hw), BF),
            pltpu.VMEM((4 * ROWS, 128), F32),
            pltpu.VMEM((4 * ROWS, 128), F32),
            pltpu.VMEM((4 * ROWS, hw), F32),
            pltpu.SemaphoreType.DMA((28,)),
        ],
        compiler_params=params(),
        name="attend",
    )(idx, q_cache, group, light, bias, emb, out_w)


def shift_mp(x, k):
    return lax.ppermute(x, "mp", [(i, (i + k) % 4) for i in range(4)])


def local(
    tile_batch,
    positions,
    counts,
    vit_gain,
    vit_qkv,
    vit_out,
    tile_proj,
    seq_cache,
    long_gain,
    long_qkv,
    long_out,
):
    mp, seq = lax.axis_index("mp"), lax.axis_index("seq")
    idx = jnp.concatenate([jnp.stack([mp, seq]).astype(jnp.int32), counts, positions])
    slots, _, width = tile_batch.shape
    model = seq_cache.shape[1]
    hw = long_qkv.shape[-1]

    left, right = shift_mp(tile_batch, 1), shift_mp(tile_batch, 3)
    far = [shift_mp(left[0:2], 1), shift_mp(right[2:4], 3)]

    slide_w = long_qkv.transpose(1, 2, 0).reshape(3 * hw, model)
    gain_row = long_gain.reshape(1, model)
    q_cache, heavy, light = slide_project(idx, seq_cache, gain_row, slide_w)
    light = lax.all_to_all(jnp.broadcast_to(light[None], (64,) + light.shape), "seq", 0, 0)
    groups = [[16 * g + i for i in range(16)] for g in range(4)]
    group = lax.all_gather(heavy, "seq", axis=0, tiled=True, axis_index_groups=groups)
    marks = light[:, 24, 0:8].astype(jnp.int32)
    all_pos = (marks[:, 0:4] * 64 + marks[:, 4:8]).reshape(64 * slots, 1)
    bias = key_flags(idx, all_pos)

    tile_w = vit_qkv.transpose(1, 0, 2)
    gain = vit_gain.reshape(4, 1, width)
    rows = [encode(idx, i, tile_batch, left, right, far[i], gain, tile_w) for i in range(2)]
    proj_here = lax.dynamic_slice_in_dim(tile_proj, mp * width, width, 0)
    joined = jnp.concatenate([dot(vit_out, tile_proj).astype(BF), proj_here], axis=0)
    partial = dot(jnp.concatenate(rows, axis=0).astype(BF), joined)
    shares = [partial] + [shift_mp(partial, k) for k in (1, 3, 2)]
    emb = embed_rows(idx, shares, gain_row, slide_w)
    emb, bias = lax.optimization_barrier((emb, bias))
    emb = lax.all_to_all(jnp.broadcast_to(emb[None], (64,) + emb.shape), "seq", 0, 0)
    emb = emb.reshape(64 * slots, emb.shape[2])

    out_w = long_out.reshape(hw, 4, hw).transpose(1, 0, 2)
    o0, o1, o2, o3 = attend(idx, q_cache, group, light, bias, emb, out_w)
    terms = [o0, shift_mp(o1, 1), shift_mp(o2, 2), shift_mp(o3, 3)]
    a, b, c, d = [term.astype(F32) for term in terms]
    return ((a + b) + (c + d)).astype(BF)


def solution(mesh):
    placed = (
        P("seq", None, "mp"),
        P("seq"),
        P("seq"),
        P(),
        P(None, None, "mp"),
        P("mp", None),
        P(),
        P("seq", None),
        P(),
        P(None, None, "mp"),
        P("mp", None),
    )
    return jax.shard_map(
        local, mesh=mesh, in_specs=placed, out_specs=P("seq", "mp"), check_vma=False
    )
```

time: 132 us -> 136 us (1.030)
  waiting for transfers between devices: 22 us -> 41.2 us
  local copies, waits for them, and re-layouts: 31.1 us -> 12.6 us
  between operations: 1.08 us -> 14.4 us
  other arithmetic: 7.86 us -> 1.78 us
  starting transfers between devices: 43.7 us -> 37.9 us
  Pallas kernels: 23 us -> 24.7 us
    ppermute x14 -> x10, waiting for transfers between devices: 7.23 us -> 29 us  [shift_mp(): return lax.ppermute(x, 'mp', [(i, (i + k) % 4) for i in range(4)])]
    ppermute x6 -> x0, starting transfers between devices: 19.3 us -> none  [swap_seq(): return lax.ppermute(x, 'seq', [(i, i ^ bit) for i in range(64)])]
    all_to_all x0 -> x1, starting transfers between devices: none -> 13.3 us  [local(): lax.all_to_all(jnp.broadcast_to(light[None], (64,) + light.shape), 'seq',...]
    unnamed x40 -> x18, local copies, waits for them, and re-layouts: 13 us -> 3.9 us
    reshape x1 -> x0, local copies, waits for them, and re-layouts: 5.79 us -> none  [local(): tile_w = vit_qkv.reshape(vit_qkv.shape[0], 3 * width)]
    all_to_all x1, starting transfers between devices: 8.02 us -> 13.4 us  [local(): lax.all_to_all(jnp.broadcast_to(emb[None], (64,) + emb.shape), 'seq', 0, 0)]
    ppermute x14 -> x10, starting transfers between devices: 16.4 us -> 11.1 us  [shift_mp(): return lax.ppermute(x, 'mp', [(i, (i + k) % 4) for i in range(4)])]
    slice x8 -> x2, local copies, waits for them, and re-layouts: 7.04 us -> 1.82 us  [local(): far = [shift_mp(left[0:2], 1), shift_mp(right[2:4], 3)]]
  transfers between devices with their start and end apart: 21 -> 13, of which waited for: 5 -> 7; matrix products, arithmetic and copies ran while one was open for 21% -> 8% of each run, Pallas kernels for 10% -> 11%
where the time goes in v2:
time: 136 us; the launch traced here: 135 us
  waiting for transfers between devices  41.2 us (30%)
  starting transfers between devices  37.9 us (28%)
  Pallas kernels  24.7 us (18%)
  between operations  14.4 us (11%)
  local copies, waits for them, and re-layouts  12.6 us (9%)
  matrix products  2.77 us (2%)
  other arithmetic  1.78 us (1%)
    ppermute x10, waiting for transfers between devices, shift_mp(): return lax.ppermute(x, 'mp', [(i, (i + k) % 4) for i in range(4)])  29 us
    all_to_all x1, starting transfers between devices, local(): lax.all_to_all(jnp.broadcast_to(emb[None], (64,) + emb.shape), 'seq', 0, 0)  13.4 us
    all_to_all x1, starting transfers between devices, local(): lax.all_to_all(jnp.broadcast_to(light[None], (64,) + light.shape), 'seq',...  13.3 us
    pallas_call x2, Pallas kernels, encode(): pl.pallas_call(encode_kernel, grid=(1,), out_shape=jax.ShapeDtypeStruct((...  11.8 us
    all_to_all x1, waiting for transfers between devices, local(): lax.all_to_all(jnp.broadcast_to(emb[None], (64,) + emb.shape), 'seq', 0, 0)  11.8 us
    ppermute x10, starting transfers between devices, shift_mp(): return lax.ppermute(x, 'mp', [(i, (i + k) % 4) for i in range(4)])  11.1 us
    pallas_call x1, Pallas kernels, attend(): pl.pallas_call(attend_kernel, out_shape=(jax.ShapeDtypeStruct((ROWS, hw),...  8 us
    unnamed x18, local copies, waits for them, and re-layouts  3.9 us
  transfers between devices with their start and end apart: 13, of which 7 were waited for; matrix products, arithmetic and copies ran while one was open for 8% of the time, Pallas kernels for 11%

profile of v2, /device:TPU:1, one launch (start us, length us, event | category | flops | bytes accessed | tf_op | source)
XLA Modules:
  0.0 135.3 jit_solution(6624530479522746579)
XLA Ops:
  8.8 1.2 copy-done.1
  9.9 0.9 copy-done.4
  10.9 2.0 %slide_project.1 = (f32[128,192]{1,0:T(8,128)S(1)}, bf16[224,384]{1,0:T(8,128)(2,1)}, bf16[32,384]{1,0:T(8,128)(2,1)S(1)}) custom-call(s32[7]{0:T(128)S(1)} %pad_add_fusion.idx, bf16[128,768]{1,0:T(8,128)(2,1)S(1)} %copy-done.4, f32[1,768]{1,0:T(1,128)S(1)} %reshape.22.gain, bf16[576,768]{1,0:T(8,128)(2,1)S(1)} %bitcast.12), custom_call_target="tpu_custom_call" | custom-call | tf_op jit(solution)/shard_map/slide_project/pallas_call | solution.py:209
  12.9 1.3 broadcast_in_dim.4
  14.2 13.3 %all-to-all-start = ((bf16[64,32,384]{2,1,0:T(8,128)(2,1)}), bf16[64,32,384]{2,1,0:T(8,128)(2,1)}, u32[]{:S(2)}, u32[]{:S(2)}) async-start(bf16[64,32,384]{2,1,0:T(8,128)(2,1)} %broadcast_in_dim.4), calls=%async_computation | async-start | bytes 3145728 | tf_op jit(solution)/shard_map/all_to_all | solution.py:410
  27.5 1.3 collective-permute-start
  28.8 1.5 %collective-permute-start.1 = (bf16[4,256,384]{2,1,0:T(8,128)(2,1)}, bf16[4,256,384]{2,1,0:T(8,128)(2,1)}, u32[]{:S(2)}, u32[]{:S(2)}) collective-permute-start(bf16[4,256,384]{2,1,0:T(8,128)(2,1)} %own.3), channel_id=1, source_target_pairs={{0,3},{1,0},{2,1},{3,2},{4,7},{5,4},{6,5},{7,6},{8,11},{9,8},{10,9... | collective-permute-start | bytes 2359304 | tf_op jit(solution)/shard_map/ppermute | solution.py:382
  30.3 17.4 %collective-permute-done.left = bf16[4,256,384]{2,1,0:T(8,128)(2,1)S(1)} collective-permute-done((bf16[4,256,384]{2,1,0:T(8,128)(2,1)}, bf16[4,256,384]{2,1,0:T(8,128)(2,1)S(1)}, u32[]{:S(2)}, u32[]{:S(2)}) %collective-permute-start) | collective-permute-done | bytes 786464 | tf_op jit(solution)/shard_map/ppermute | solution.py:382
  47.7 0.8 slice.20
  48.5 0.8 constant_dynamic-slice_fusion
  49.4 2.5 %convolution_convert_fusion = bf16[384,768]{1,0:T(8,128)(2,1)S(1)} fusion(bf16[384,1536]{1,0:T(8,128)(2,1)} %param.16, bf16[1536,768]{1,0:T(8,128)(2,1)S(1)} %copy-done), kind=kOutput, calls=%fused_computation | convolution fusion | flops 906264576 | bytes 4128768 | tf_op jit(solution)/shard_map/dot_general | solution.py:32
  51.9 1.0 slice.21
  52.9 2.9 %collective-permute-start.3 = (bf16[2,256,384]{2,1,0:T(8,128)(2,1)S(1)}, bf16[2,256,384]{2,1,0:T(8,128)(2,1)S(1)}, u32[]{:S(2)}, u32[]{:S(2)}) collective-permute-start(bf16[2,256,384]{2,1,0:T(8,128)(2,1)S(1)} %slice.21), channel_id=1, source_target_pairs={{0,3},{1,0},{2,1},{3,2},{4,7},{5,4},{6,5},{7,6},{8,11},{9,8},{10,9... | collective-permute-start | bytes 1179656 | tf_op jit(solution)/shard_map/ppermute | solution.py:382
  55.9 3.5 %collective-permute-done.2.far = bf16[2,256,384]{2,1,0:T(8,128)(2,1)} collective-permute-done((bf16[2,256,384]{2,1,0:T(8,128)(2,1)}, bf16[2,256,384]{2,1,0:T(8,128)(2,1)}, u32[]{:S(2)}, u32[]{:S(2)}) %collective-permute-start.2) | collective-permute-done | bytes 393248 | tf_op jit(solution)/shard_map/ppermute | solution.py:382
  59.4 5.9 %encode.2 = f32[2,768]{1,0:T(2,128)S(1)} custom-call(s32[7]{0:T(128)S(1)} %pad_add_fusion.idx, bf16[4,256,384]{2,1,0:T(8,128)(2,1)S(1)} %copy-done.6, bf16[4,256,384]{2,1,0:T(8,128)(2,1)S(1)} %collective-permute-done.left, bf16[4,256,384]{2,1,0:T(8,128)(2,1)} %collective-permute-done.1.right, bf16[2,256,384]{2,1,0:T(8,128)(2,1)} %collective-permute-done.2.far, ...), custom_call_target="tpu_custom_call" | custom-call | flops 6000000000 | bytes 8000000 | tf_op jit(solution)/shard_map/encode/pallas_call | solution.py:102
  65.3 5.9 %encode.3 = f32[2,768]{1,0:T(2,128)S(1)} custom-call(s32[7]{0:T(128)S(1)} %pad_add_fusion.idx, bf16[4,256,384]{2,1,0:T(8,128)(2,1)S(1)} %copy-done.6, bf16[4,256,384]{2,1,0:T(8,128)(2,1)S(1)} %collective-permute-done.left, bf16[4,256,384]{2,1,0:T(8,128)(2,1)} %collective-permute-done.1.right, bf16[2,256,384]{2,1,0:T(8,128)(2,1)S(1)} %collective-permute-done.3.far, ...), custom_call_target="tpu_custom_call" | custom-call | flops 6000000000 | bytes 8000000 | tf_op jit(solution)/shard_map/encode/pallas_call | solution.py:102
  71.6 2.7 %collective-permute-start.5 = (f32[4,768]{1,0:T(4,128)S(1)}, f32[4,768]{1,0:T(4,128)S(1)}, u32[]{:S(2)}, u32[]{:S(2)}) collective-permute-start(f32[4,768]{1,0:T(4,128)S(1)} %fusion.a), channel_id=1, source_target_pairs={{0,3},{1,0},{2,1},{3,2},{4,7},{5,4},{6,5},{7,6},{8,11},{9,8},{10,9... | collective-permute-start | bytes 36872 | tf_op jit(solution)/shard_map/ppermute | solution.py:382
  74.2 1.5 %collective-permute-done.4.b = f32[4,768]{1,0:T(4,128)S(1)} collective-permute-done((f32[4,768]{1,0:T(4,128)S(1)}, f32[4,768]{1,0:T(4,128)S(1)}, u32[]{:S(2)}, u32[]{:S(2)}) %collective-permute-start.4) | collective-permute-done | bytes 12320 | tf_op jit(solution)/shard_map/ppermute | solution.py:382
  75.7 3.0 %collective-permute-done.6.d = f32[4,768]{1,0:T(4,128)S(1)} collective-permute-done((f32[4,768]{1,0:T(4,128)S(1)}, f32[4,768]{1,0:T(4,128)S(1)}, u32[]{:S(2)}, u32[]{:S(2)}) %collective-permute-start.6) | collective-permute-done | bytes 12320 | tf_op jit(solution)/shard_map/ppermute | solution.py:382
  78.7 1.0 embed_rows.1
  80.1 0.9 slice_convert_fusion
  81.2 1.8 %key_flags.1.bias = f32[40,1024]{1,0:T(8,128)S(1)} custom-call(s32[7]{0:T(128)S(1)} %pad_add_fusion.idx, s32[256,1]{1,0:T(8,128)S(1)} %reshape.29.pos), custom_call_target="tpu_custom_call" | custom-call | tf_op jit(solution)/shard_map/key_flags/pallas_call | solution.py:246
  83.1 0.8 broadcast_in_dim.5
  83.9 13.4 %all-to-all-start.1 = ((bf16[64,4,640]{2,1,0:T(4,128)(2,1)}), bf16[64,4,640]{2,1,0:T(4,128)(2,1)}, u32[]{:S(2)}, u32[]{:S(2)}) async-start(bf16[64,4,640]{2,1,0:T(4,128)(2,1)} %broadcast_in_dim.5), calls=%async_computation.1 | async-start | bytes 655360 | tf_op jit(solution)/shard_map/all_to_all | solution.py:426
  97.3 1.3 reshape.27
  98.7 11.8 %all-to-all-done.1 = bf16[64,4,640]{2,1,0:T(4,128)(2,1)} async-done(((bf16[64,4,640]{2,1,0:T(4,128)(2,1)}), bf16[64,4,640]{2,1,0:T(4,128)(2,1)}, u32[]{:S(2)}, u32[]{:S(2)}) %all-to-all-start.1) | async-done | bytes 327712 | tf_op jit(solution)/shard_map/all_to_all | solution.py:426
  110.5 1.1 reshape.26.emb
  111.6 1.8 %copy-done.3 = bf16[3584,384]{1,0:T(8,128)(2,1)S(1)} copy-done((bf16[3584,384]{1,0:T(8,128)(2,1)S(1)}, bf16[3584,384]{1,0:T(8,128)(2,1)}, u32[]{:S(2)}) %copy-start.3) | copy-done | bytes 2752536
  113.4 8.0 %attend.1 = (bf16[128,192]{1,0:T(8,128)(2,1)S(1)}, bf16[128,192]{1,0:T(8,128)(2,1)S(1)}, bf16[128,192]{1,0:T(8,128)(2,1)S(1)}, bf16[128,192]{1,0:T(8,128)(2,1)S(1)}) custom-call(s32[7]{0:T(128)S(1)} %pad_add_fusion.idx, f32[128,192]{1,0:T(8,128)S(1)} %get-tuple-element.14.q_cache, bf16[3584,384]{1,0:T(8,128)(2,1)S(1)} %copy-done.3, ...), custom_call_target="tpu_custom_call" | custom-call | tf_op jit(solution)/shard_map/attend/pallas_call | solution.py:363
  121.5 0.9 collective-permute-start.8
  122.4 1.7 %collective-permute-start.9 = (bf16[128,192]{1,0:T(8,128)(2,1)S(1)}, bf16[128,192]{1,0:T(8,128)(2,1)S(1)}, u32[]{:S(2)}, u32[]{:S(2)}) collective-permute-start(bf16[128,192]{1,0:T(8,128)(2,1)S(1)} %get-tuple-element.22), channel_id=1, source_target_pairs={{0,3},{1,0},{2,1},{3,2},{4,7},{5,4},{6,5},{7,6},{8,11},{9,8},{10,9... | collective-permute-start | bytes 147464 | tf_op jit(solution)/shard_map/ppermute | solution.py:382
  124.1 3.6 %collective-permute-done.7 = bf16[128,192]{1,0:T(8,128)(2,1)S(1)} collective-permute-done((bf16[128,192]{1,0:T(8,128)(2,1)S(1)}, bf16[128,192]{1,0:T(8,128)(2,1)S(1)}, u32[]{:S(2)}, u32[]{:S(2)}) %collective-permute-start.7) | collective-permute-done | bytes 49184 | tf_op jit(solution)/shard_map/ppermute | solution.py:382
  (39 shorter events, 3.3 us)
Async XLA Ops:
  6.5 42.0 %copy-start = (bf16[1536,768]{1,0:T(8,128)(2,1)S(1)}, bf16[1536,768]{1,0:T(8,128)(2,1)}, u32[]{:S(2)}) copy-start(bf16[1536,768]{1,0:T(8,128)(2,1)} %param.17) | copy-start | bytes 7077892
  6.5 105.0 %all-gather.2.cloned.1.call-start = ((), (), s32[]{:S(2)}) async-start(), calls=%async_computation.2 | async-start | bytes 2924544 | tf_op jit(solution)/shard_map/all_gather | solution.py:412
  8.8 1.2 copy-start.1
  9.9 0.9 copy-start.4
  14.2 66.0 %all-to-all-start = ((bf16[64,32,384]{2,1,0:T(8,128)(2,1)}), bf16[64,32,384]{2,1,0:T(8,128)(2,1)}, u32[]{:S(2)}, u32[]{:S(2)}) async-start(bf16[64,32,384]{2,1,0:T(8,128)(2,1)} %broadcast_in_dim.4), calls=%async_computation | async-start | bytes 3145728 | tf_op jit(solution)/shard_map/all_to_all | solution.py:410
  27.5 21.8 %copy-start.8 = (f32[1536]{0:T(1024)S(1)}, f32[1536]{0:T(1024)}, u32[]{:S(2)}) copy-start(f32[1536]{0:T(1024)} %param.14) | copy-start | bytes 18436
  27.5 20.2 %collective-permute-start = (bf16[4,256,384]{2,1,0:T(8,128)(2,1)}, bf16[4,256,384]{2,1,0:T(8,128)(2,1)S(1)}, u32[]{:S(2)}, u32[]{:S(2)}) collective-permute-start(bf16[4,256,384]{2,1,0:T(8,128)(2,1)} %own.3), channel_id=1, source_target_pairs={{0,1},{1,2},{2,3},{3,0},{4,5},{5,6},{6,7},{7,4},{8,9},{9,10},{10,1... | collective-permute-start | bytes 2359304 | tf_op jit(solution)/shard_map/ppermute | solution.py:382
  28.8 23.1 %collective-permute-start.1 = (bf16[4,256,384]{2,1,0:T(8,128)(2,1)}, bf16[4,256,384]{2,1,0:T(8,128)(2,1)}, u32[]{:S(2)}, u32[]{:S(2)}) collective-permute-start(bf16[4,256,384]{2,1,0:T(8,128)(2,1)} %own.3), channel_id=1, source_target_pairs={{0,3},{1,0},{2,1},{3,2},{4,7},{5,4},{6,5},{7,6},{8,11},{9,8},{10,9... | collective-permute-start | bytes 2359304 | tf_op jit(solution)/shard_map/ppermute | solution.py:382
  48.5 10.9 %collective-permute-start.2 = (bf16[2,256,384]{2,1,0:T(8,128)(2,1)}, bf16[2,256,384]{2,1,0:T(8,128)(2,1)}, u32[]{:S(2)}, u32[]{:S(2)}) collective-permute-start(bf16[2,256,384]{2,1,0:T(8,128)(2,1)} %slice.20), channel_id=1, source_target_pairs={{0,1},{1,2},{2,3},{3,0},{4,5},{5,6},{6,7},{7,4},{8,9},{9,10},{10,1... | collective-permute-start | bytes 1179656 | tf_op jit(solution)/shard_map/ppermute | solution.py:382
  49.4 10.0 %copy-start.5 = (bf16[1536,3,384]{2,0,1:T(8,128)(2,1)S(1)}, bf16[1536,3,384]{2,0,1:T(8,128)(2,1)}, u32[]{:S(2)}) copy-start(bf16[1536,3,384]{2,0,1:T(8,128)(2,1)} %param.15) | copy-start | bytes 10616836
  49.4 10.0 %copy-start.6 = (bf16[4,256,384]{2,1,0:T(8,128)(2,1)S(1)}, bf16[4,256,384]{2,1,0:T(8,128)(2,1)}, u32[]{:S(2)}) copy-start(bf16[4,256,384]{2,1,0:T(8,128)(2,1)} %own.3) | copy-start | bytes 2359300
  52.9 12.4 %collective-permute-start.3 = (bf16[2,256,384]{2,1,0:T(8,128)(2,1)S(1)}, bf16[2,256,384]{2,1,0:T(8,128)(2,1)S(1)}, u32[]{:S(2)}, u32[]{:S(2)}) collective-permute-start(bf16[2,256,384]{2,1,0:T(8,128)(2,1)S(1)} %slice.21), channel_id=1, source_target_pairs={{0,3},{1,0},{2,1},{3,2},{4,7},{5,4},{6,5},{7,6},{8,11},{9,8},{10,9... | collective-permute-start | bytes 1179656 | tf_op jit(solution)/shard_map/ppermute | solution.py:382
  65.3 6.0 %copy-start.7 = (bf16[384,768]{1,0:T(8,128)(2,1)S(1)}, bf16[384,768]{1,0:T(8,128)(2,1)}, u32[]{:S(2)}) copy-start(bf16[384,768]{1,0:T(8,128)(2,1)} %constant_dynamic-slice_fusion) | copy-start | bytes 1769476
  71.3 7.4 %copy-start.2 = (bf16[768,3,192]{0,2,1:T(8,128)(2,1)S(1)}, bf16[768,3,192]{0,2,1:T(8,128)(2,1)}, u32[]{:S(2)}) copy-start(bf16[768,3,192]{0,2,1:T(8,128)(2,1)} %param.20) | copy-start | bytes 2654212
  71.6 4.2 %collective-permute-start.4 = (f32[4,768]{1,0:T(4,128)S(1)}, f32[4,768]{1,0:T(4,128)S(1)}, u32[]{:S(2)}, u32[]{:S(2)}) collective-permute-start(f32[4,768]{1,0:T(4,128)S(1)} %fusion.a), channel_id=1, source_target_pairs={{0,1},{1,2},{2,3},{3,0},{4,5},{5,6},{6,7},{7,4},{8,9},{9,10},{10,1... | collective-permute-start | bytes 36872 | tf_op jit(solution)/shard_map/ppermute | solution.py:382
  71.6 4.2 %collective-permute-start.5 = (f32[4,768]{1,0:T(4,128)S(1)}, f32[4,768]{1,0:T(4,128)S(1)}, u32[]{:S(2)}, u32[]{:S(2)}) collective-permute-start(f32[4,768]{1,0:T(4,128)S(1)} %fusion.a), channel_id=1, source_target_pairs={{0,3},{1,0},{2,1},{3,2},{4,7},{5,4},{6,5},{7,6},{8,11},{9,8},{10,9... | collective-permute-start | bytes 36872 | tf_op jit(solution)/shard_map/ppermute | solution.py:382
  74.2 4.5 %collective-permute-start.6 = (f32[4,768]{1,0:T(4,128)S(1)}, f32[4,768]{1,0:T(4,128)S(1)}, u32[]{:S(2)}, u32[]{:S(2)}) collective-permute-start(f32[4,768]{1,0:T(4,128)S(1)} %fusion.a), channel_id=1, source_target_pairs={{0,2},{1,3},{2,0},{3,1},{4,6},{5,7},{6,4},{7,5},{8,10},{9,11},{10,... | collective-permute-start | bytes 36872 | tf_op jit(solution)/shard_map/ppermute | solution.py:382
  83.9 26.6 %all-to-all-start.1 = ((bf16[64,4,640]{2,1,0:T(4,128)(2,1)}), bf16[64,4,640]{2,1,0:T(4,128)(2,1)}, u32[]{:S(2)}, u32[]{:S(2)}) async-start(bf16[64,4,640]{2,1,0:T(4,128)(2,1)} %broadcast_in_dim.5), calls=%async_computation.1 | async-start | bytes 655360 | tf_op jit(solution)/shard_map/all_to_all | solution.py:426
  111.6 1.8 %copy-start.3 = (bf16[3584,384]{1,0:T(8,128)(2,1)S(1)}, bf16[3584,384]{1,0:T(8,128)(2,1)}, u32[]{:S(2)}) copy-start(bf16[3584,384]{1,0:T(8,128)(2,1)} %all-gather.2.cloned.1.call-done.group) | copy-start | bytes 8257540
  121.4 6.3 %collective-permute-start.7 = (bf16[128,192]{1,0:T(8,128)(2,1)S(1)}, bf16[128,192]{1,0:T(8,128)(2,1)S(1)}, u32[]{:S(2)}, u32[]{:S(2)}) collective-permute-start(bf16[128,192]{1,0:T(8,128)(2,1)S(1)} %get-tuple-element.20), channel_id=1, source_target_pairs={{0,1},{1,2},{2,3},{3,0},{4,5},{5,6},{6,7},{7,4},{8,9},{9,10},{10,1... | collective-permute-start | bytes 147464 | tf_op jit(solution)/shard_map/ppermute | solution.py:382
  121.5 6.2 %collective-permute-start.8 = (bf16[128,192]{1,0:T(8,128)(2,1)S(1)}, bf16[128,192]{1,0:T(8,128)(2,1)S(1)}, u32[]{:S(2)}, u32[]{:S(2)}) collective-permute-start(bf16[128,192]{1,0:T(8,128)(2,1)S(1)} %get-tuple-element.21), channel_id=1, source_target_pairs={{0,2},{1,3},{2,0},{3,1},{4,6},{5,7},{6,4},{7,5},{8,10},{9,11},{10,... | collective-permute-start | bytes 147464 | tf_op jit(solution)/shard_map/ppermute | solution.py:382
  122.4 5.3 %collective-permute-start.9 = (bf16[128,192]{1,0:T(8,128)(2,1)S(1)}, bf16[128,192]{1,0:T(8,128)(2,1)S(1)}, u32[]{:S(2)}, u32[]{:S(2)}) collective-permute-start(bf16[128,192]{1,0:T(8,128)(2,1)S(1)} %get-tuple-element.22), channel_id=1, source_target_pairs={{0,3},{1,0},{2,1},{3,2},{4,7},{5,4},{6,5},{7,6},{8,11},{9,8},{10,9... | collective-permute-start | bytes 147464 | tf_op jit(solution)/shard_map/ppermute | solution.py:382
Sparse Core Ops, SparseCore 0:
  13.0 64.5 all-gather.1

commit v3 on v2

--- a/solution.py
+++ b/solution.py
@@ -16,8 +16,7 @@
 BF = jnp.bfloat16
 F32 = jnp.float32
 ROWS = 128
-NEAR = 3
-NEAR_ROWS = 224
+BASES = (0, 256, 512, 768, 1024)
 
 
 def params(mib=40):
@@ -173,7 +172,7 @@
     return (j & 7) * 16 + (turned << level) + (head & ((1 << level) - 1))
 
 
-def slide_kernel(idx, cache, gain, weight, q_out, near, light, kv):
+def slide_kernel(idx, cache, gain, weight, q_out, picks, kv):
     heads_width = q_out.shape[1]
     first_head = idx[0] * 4
     row = iota((ROWS, ROWS), 0)
@@ -198,8 +197,6 @@
                 high, low = slot_digits(idx, slot)
                 tail = jnp.where(lane == slot, high, jnp.where(lane == slot + 4, low, tail))
             got = jnp.concatenate([got, tail], axis=0)
-        picks = near if level < NEAR else light
-        base = 0 if level == NEAR else base
         picks[base : base + got.shape[0], :] = got.astype(BF)
         base += n
 
@@ -210,11 +207,10 @@
         slide_kernel,
         out_shape=(
             jax.ShapeDtypeStruct((ROWS, hw), F32),
-            jax.ShapeDtypeStruct((NEAR_ROWS, 2 * hw), BF),
-            jax.ShapeDtypeStruct((32, 2 * hw), BF),
+            jax.ShapeDtypeStruct((2 * ROWS, 2 * hw), BF),
         ),
         in_specs=[whole(pltpu.SMEM)] + [whole()] * 3,
-        out_specs=(whole(),) * 3,
+        out_specs=(whole(),) * 2,
         scratch_shapes=[pltpu.VMEM((ROWS, 2 * hw), F32)],
         compiler_params=params(),
         name="slide_project",
@@ -230,7 +226,8 @@
         shift = n.bit_length() - 1
         k = iota((8, keys), 1)
         j = k & (n - 1)
-        source = (seq & -(4 << level)) + (k >> shift)
+        half = keys // 2
+        source = seq ^ (2 * ((k & (half - 1)) >> shift) + (k >= half).astype(jnp.int32))
         for h in range(4):
             r = level * 8 + h
             if level == 0 and h > 0:
@@ -258,33 +255,13 @@
 
 
 def attend_kernel(
-    idx, q_cache, group, light, bias, emb, out_w, o0, o1, o2, o3, q, kv, peak, total, acc, sems
+    idx, q_cache, mine, theirs, bias, emb, out_w, o0, o1, o2, o3, q, peak, total, acc
 ):
     mp, seq = idx[0], idx[1]
     first_head = mp * 4
     hw = q_cache.shape[1]
     scale = HDL ** (-0.5)
     slots = emb.shape[0]
-    copies = [[] for _ in range(NEAR)]
-    sem = 0
-    for level in range(NEAR):
-        shards, n = 4 << level, ROWS >> level
-        begin = (seq & 15) & -shards
-        first_row = sum(ROWS >> b for b in range(level))
-        for i in range(shards):
-            at = pl.multiple_of((begin + i) * NEAR_ROWS + first_row, 16)
-            copy = pltpu.make_async_copy(
-                group.at[pl.ds(at, n)],
-                kv.at[pl.ds(level * 512 + i * n, n)],
-                sems.at[sem],
-            )
-            copy.start()
-            copies[level].append(copy)
-            sem += 1
-    for i in range(32):
-        kv[1536 + i * 16 : 1552 + i * 16, :] = light[(seq & 32) + i, 0:16, :]
-    for i in range(64):
-        kv[2048 + i * 16 : 2064 + i * 16, :] = light[i, 16:32, :]
     tail = emb[:, 3 * hw :]
     col = iota((8, tail.shape[1]), 1)
     digits = jnp.where(col == 0, 64.0, jnp.where(col == 1, 1.0, 0.0)).astype(BF)
@@ -327,16 +304,22 @@
     for level in range(BRANCHES):
         n = ROWS >> level
         qb = full_q if level == 0 else queries(level)
-        for copy in copies[level] if level < NEAR else ():
-            copy.wait()
-        low, keys = 512 * level, 1024 if level == BRANCHES - 1 else 512
-        s = dot_t(qb, kv[low : low + keys, 0:hw]) * scale
-        s = s.reshape(4, n, keys) + bias[level * 8 : level * 8 + 4, 0:keys][:, None, :]
-        s = s.reshape(4 * n, keys)
-        m = jnp.max(s, axis=-1, keepdims=True)
-        e = jnp.exp(s - m)
-        t = jnp.sum(e, axis=-1, keepdims=True)
-        o = dot(e.astype(BF), kv[low : low + keys, hw : 2 * hw])
+        half = 512 if level == BRANCHES - 1 else 256
+        low = BASES[level]
+        sides = []
+        for number, side in enumerate((mine, theirs)):
+            s = dot_t(qb, side[low : low + half, 0:hw]) * scale
+            flags = bias[level * 8 : level * 8 + 4, number * half : (number + 1) * half]
+            s = s.reshape(4, n, half) + flags[:, None, :]
+            sides.append(s.reshape(4 * n, half))
+        m = jnp.maximum(
+            jnp.max(sides[0], axis=-1, keepdims=True), jnp.max(sides[1], axis=-1, keepdims=True)
+        )
+        e0, e1 = jnp.exp(sides[0] - m), jnp.exp(sides[1] - m)
+        t = jnp.sum(e0, axis=-1, keepdims=True) + jnp.sum(e1, axis=-1, keepdims=True)
+        o = dot(e0.astype(BF), mine[low : low + half, hw : 2 * hw]) + dot(
+            e1.astype(BF), theirs[low : low + half, hw : 2 * hw]
+        )
         for h in range(4):
             start = h * ROWS + (0 if level == 0 else pick_start(first_head + h, level))
             at = pl.ds(pl.multiple_of(start, 8), n)
@@ -358,28 +341,30 @@
         o[...] = dot(attended, out_w[lax.rem(mp + d, 4)]).astype(BF)
 
 
-def attend(idx, q_cache, group, light, bias, emb, out_w):
+def attend(idx, q_cache, mine, theirs, bias, emb, out_w):
     hw = q_cache.shape[1]
     return pl.pallas_call(
         attend_kernel,
         out_shape=(jax.ShapeDtypeStruct((ROWS, hw), BF),) * 4,
-        in_specs=[whole(pltpu.SMEM), whole(), whole(pl.ANY)] + [whole()] * 4,
+        in_specs=[whole(pltpu.SMEM)] + [whole()] * 6,
         out_specs=(whole(),) * 4,
         scratch_shapes=[
             pltpu.VMEM((ROWS, hw), F32),
-            pltpu.VMEM((3072, 2 * hw), BF),
             pltpu.VMEM((4 * ROWS, 128), F32),
             pltpu.VMEM((4 * ROWS, 128), F32),
             pltpu.VMEM((4 * ROWS, hw), F32),
-            pltpu.SemaphoreType.DMA((28,)),
         ],
         compiler_params=params(),
         name="attend",
-    )(idx, q_cache, group, light, bias, emb, out_w)
+    )(idx, q_cache, mine, theirs, bias, emb, out_w)
 
 
 def shift_mp(x, k):
     return lax.ppermute(x, "mp", [(i, (i + k) % 4) for i in range(4)])
+
+
+def swap_seq(x, bit):
+    return lax.ppermute(x, "seq", [(i, i ^ bit) for i in range(64)])
 
 
 def local(
@@ -402,21 +387,36 @@
     hw = long_qkv.shape[-1]
 
     left, right = shift_mp(tile_batch, 1), shift_mp(tile_batch, 3)
-    far = [shift_mp(left[0:2], 1), shift_mp(right[2:4], 3)]
+    tile_w = vit_qkv.transpose(1, 0, 2)
+    gain = vit_gain.reshape(4, 1, width)
 
     slide_w = long_qkv.transpose(1, 2, 0).reshape(3 * hw, model)
     gain_row = long_gain.reshape(1, model)
-    q_cache, heavy, light = slide_project(idx, seq_cache, gain_row, slide_w)
-    light = lax.all_to_all(jnp.broadcast_to(light[None], (64,) + light.shape), "seq", 0, 0)
-    groups = [[16 * g + i for i in range(16)] for g in range(4)]
-    group = lax.all_gather(heavy, "seq", axis=0, tiled=True, axis_index_groups=groups)
-    marks = light[:, 24, 0:8].astype(jnp.int32)
+    q_cache, picks = slide_project(idx, seq_cache, gain_row, slide_w)
+    have = picks[None]
+    kept = []
+    for level, bit in enumerate((2, 4, 8, 16, 32)):
+        have = jnp.concatenate([have, swap_seq(have, bit)], axis=0)
+        n = ROWS >> level
+        if level < BRANCHES - 1:
+            kept.append(have[:, 0:n].reshape(-1, 2 * hw))
+            have = have[:, n:]
+        if level == 1:
+            have, left, right = lax.optimization_barrier((have, left, right))
+            far = [shift_mp(left[0:2], 1), shift_mp(right[2:4], 3)]
+        if level == 2:
+            have, *far = lax.optimization_barrier((have, *far))
+        if level == 3:
+            first = encode(idx, 0, tile_batch, left, right, far[0], gain, tile_w)
+            have, first = lax.optimization_barrier((have, first))
+    mine = jnp.concatenate(kept + [have.reshape(-1, 2 * hw)], axis=0)
+    theirs = swap_seq(mine, 1)
+    marks = jnp.concatenate([side[1024:].reshape(32, 16, 2 * hw)[:, 8, 0:8] for side in (mine, theirs)])
+    marks = marks.astype(jnp.int32)
     all_pos = (marks[:, 0:4] * 64 + marks[:, 4:8]).reshape(64 * slots, 1)
     bias = key_flags(idx, all_pos)
 
-    tile_w = vit_qkv.transpose(1, 0, 2)
-    gain = vit_gain.reshape(4, 1, width)
-    rows = [encode(idx, i, tile_batch, left, right, far[i], gain, tile_w) for i in range(2)]
+    rows = [first, encode(idx, 1, tile_batch, left, right, far[1], gain, tile_w)]
     proj_here = lax.dynamic_slice_in_dim(tile_proj, mp * width, width, 0)
     joined = jnp.concatenate([dot(vit_out, tile_proj).astype(BF), proj_here], axis=0)
     partial = dot(jnp.concatenate(rows, axis=0).astype(BF), joined)
@@ -427,7 +427,7 @@
     emb = emb.reshape(64 * slots, emb.shape[2])
 
     out_w = long_out.reshape(hw, 4, hw).transpose(1, 0, 2)
-    o0, o1, o2, o3 = attend(idx, q_cache, group, light, bias, emb, out_w)
+    o0, o1, o2, o3 = attend(idx, q_cache, mine, theirs, bias, emb, out_w)
     terms = [o0, shift_mp(o1, 1), shift_mp(o2, 2), shift_mp(o3, 3)]
     a, b, c, d = [term.astype(F32) for term in terms]
     return ((a + b) + (c + d)).astype(BF)

time: 136 us -> 136 us (level)
  local copies, waits for them, and re-layouts: 12.6 us -> 33.1 us
  between operations: 14.4 us -> 0.94 us
  Pallas kernels: 24.7 us -> 20.2 us
  waiting for transfers between devices: 41.2 us -> 38.1 us
  other arithmetic: 1.78 us -> 3.21 us
  matrix products: 2.77 us -> 1.35 us
    ppermute x0 -> x6, starting transfers between devices: none -> 20.1 us  [swap_seq(): return lax.ppermute(x, 'seq', [(i, i ^ bit) for i in range(64)])]
    ppermute x10, waiting for transfers between devices: 29 us -> 12.6 us  [shift_mp(): return lax.ppermute(x, 'mp', [(i, (i + k) % 4) for i in range(4)])]
    ppermute x0 -> x6, waiting for transfers between devices: none -> 16.2 us  [swap_seq(): return lax.ppermute(x, 'seq', [(i, i ^ bit) for i in range(64)])]
    all_to_all x1 -> x0, starting transfers between devices: 13.3 us -> none  [local(): lax.all_to_all(jnp.broadcast_to(light[None], (64,) + light.shape), 'seq',...]
    unnamed x18 -> x54, local copies, waits for them, and re-layouts: 3.9 us -> 15.9 us
    all_to_all x1, starting transfers between devices: 13.4 us -> 8 us  [local(): lax.all_to_all(jnp.broadcast_to(emb[None], (64,) + emb.shape), 'seq', 0, 0)]
    slice x0 -> x6, local copies, waits for them, and re-layouts: none -> 3.61 us  [the longest x4 3.52 us: local(): side[1024:].reshape(32, 16, 2 * hw)[:, 8, 0:8]]
    pallas_call x1, Pallas kernels: 8 us -> 4.42 us  [attend(): pl.pallas_call(attend_kernel, out_shape=(jax.ShapeDtypeStruct((ROWS, hw),...]
  transfers between devices with their start and end apart: 13 -> 17, of which waited for: 7 -> 12; matrix products, arithmetic and copies ran while one was open for 8% -> 11% of each run, Pallas kernels for 11% -> 10%
where the time goes in v3:
time: 136 us; the launch traced here: 135 us
  starting transfers between devices  38.3 us (28%)
  waiting for transfers between devices  38.1 us (28%)
  local copies, waits for them, and re-layouts  33.1 us (24%)
  Pallas kernels  20.2 us (15%)
  other arithmetic  3.21 us (2%)
    ppermute x6, starting transfers between devices, swap_seq(): return lax.ppermute(x, 'seq', [(i, i ^ bit) for i in range(64)])  20.1 us
    ppermute x6, waiting for transfers between devices, swap_seq(): return lax.ppermute(x, 'seq', [(i, i ^ bit) for i in range(64)])  16.2 us
    unnamed x54, local copies, waits for them, and re-layouts  15.9 us
    ppermute x10, waiting for transfers between devices, shift_mp(): return lax.ppermute(x, 'mp', [(i, (i + k) % 4) for i in range(4)])  12.6 us
    pallas_call x2, Pallas kernels, encode(): pl.pallas_call(encode_kernel, grid=(1,), out_shape=jax.ShapeDtypeStruct((...  11.7 us
    ppermute x10, starting transfers between devices, shift_mp(): return lax.ppermute(x, 'mp', [(i, (i + k) % 4) for i in range(4)])  10.2 us
    all_to_all x1, waiting for transfers between devices, local(): lax.all_to_all(jnp.broadcast_to(emb[None], (64,) + emb.shape), 'seq', 0, 0)  9.29 us
    all_to_all x1, starting transfers between devices, local(): lax.all_to_all(jnp.broadcast_to(emb[None], (64,) + emb.shape), 'seq', 0, 0)  8 us
  transfers between devices with their start and end apart: 17, of which 12 were waited for; matrix products, arithmetic and copies ran while one was open for 11% of the time, Pallas kernels for 10%

profile of v3, /device:TPU:1, one launch (start us, length us, event | category | flops | bytes accessed | tf_op | source)
XLA Modules:
  0.0 135.2 jit_solution(6170591244861688309)
XLA Ops:
  0.0 3.3 %collective-permute-start.3 = (bf16[4,256,384]{2,1,0:T(8,128)(2,1)}, bf16[4,256,384]{2,1,0:T(8,128)(2,1)S(1)}, u32[]{:S(2)}, u32[]{:S(2)}) collective-permute-start(bf16[4,256,384]{2,1,0:T(8,128)(2,1)} %own.3), channel_id=1, source_target_pairs={{0,3},{1,0},{2,1},{3,2},{4,7},{5,4},{6,5},{7,6},{8,11},{9,8},{10,9... | collective-permute-start | bytes 2359304 | tf_op jit(solution)/shard_map/ppermute | solution.py:363
  7.5 1.3 slide_project.1
  8.8 1.7 %collective-permute-start = (bf16[1,256,384]{2,1,0:T(8,128)(2,1)S(1)}, bf16[1,256,384]{2,1,0:T(8,128)(2,1)S(1)}, u32[]{:S(2)}, u32[]{:S(2)}) collective-permute-start(bf16[1,256,384]{2,1,0:T(8,128)(2,1)S(1)} %bitcast.23), channel_id=1, source_target_pairs={{0,8},{4,12},{8,0},{12,4},{16,24},{20,28},{24,16},{28,20},{32,40},... | collective-permute-start | bytes 589832 | tf_op jit(solution)/shard_map/ppermute | solution.py:367
  10.6 3.5 %collective-permute-done = bf16[1,256,384]{2,1,0:T(8,128)(2,1)S(1)} collective-permute-done((bf16[1,256,384]{2,1,0:T(8,128)(2,1)S(1)}, bf16[1,256,384]{2,1,0:T(8,128)(2,1)S(1)}, u32[]{:S(2)}, u32[]{:S(2)}) %collective-permute-start) | collective-permute-done | bytes 196640 | tf_op jit(solution)/shard_map/ppermute | solution.py:367
  14.1 3.9 %collective-permute-start.1 = (bf16[2,128,384]{2,1,0:T(8,128)(2,1)S(1)}, bf16[2,128,384]{2,1,0:T(8,128)(2,1)}, u32[]{:S(2)}, u32[]{:S(2)}) collective-permute-start(bf16[2,128,384]{2,1,0:T(8,128)(2,1)S(1)} %get-tuple-element.43), channel_id=1, source_target_pairs={{0,16},{4,20},{8,24},{12,28},{16,0},{20,4},{24,8},{28,12},{32,48},... | collective-permute-start | bytes 589832 | tf_op jit(solution)/shard_map/ppermute | solution.py:367
  19.4 7.2 %collective-permute-done.1 = bf16[2,128,384]{2,1,0:T(8,128)(2,1)} collective-permute-done((bf16[2,128,384]{2,1,0:T(8,128)(2,1)S(1)}, bf16[2,128,384]{2,1,0:T(8,128)(2,1)}, u32[]{:S(2)}, u32[]{:S(2)}) %collective-permute-start.1) | collective-permute-done | bytes 196640 | tf_op jit(solution)/shard_map/ppermute | solution.py:367
  27.7 6.5 %collective-permute-start.4 = (bf16[4,64,384]{2,1,0:T(8,128)(2,1)S(1)}, bf16[4,64,384]{2,1,0:T(8,128)(2,1)S(1)}, u32[]{:S(2)}, u32[]{:S(2)}) collective-permute-start(bf16[4,64,384]{2,1,0:T(8,128)(2,1)S(1)} %get-tuple-element.23), channel_id=1, source_target_pairs={{0,32},{4,36},{8,40},{12,44},{16,48},{20,52},{24,56},{28,60},{32,0... | collective-permute-start | bytes 589832 | tf_op jit(solution)/shard_map/ppermute | solution.py:367
  36.2 2.5 %collective-permute-start.6 = (bf16[2,256,384]{2,1,0:T(8,128)(2,1)S(1)}, bf16[2,256,384]{2,1,0:T(8,128)(2,1)S(1)}, u32[]{:S(2)}, u32[]{:S(2)}) collective-permute-start(bf16[2,256,384]{2,1,0:T(8,128)(2,1)S(1)} %slice.52), channel_id=1, source_target_pairs={{0,3},{1,0},{2,1},{3,2},{4,7},{5,4},{6,5},{7,6},{8,11},{9,8},{10,9... | collective-permute-start | bytes 1179656 | tf_op jit(solution)/shard_map/ppermute | solution.py:363
  38.6 2.8 %collective-permute-done.4 = bf16[4,64,384]{2,1,0:T(8,128)(2,1)S(1)} collective-permute-done((bf16[4,64,384]{2,1,0:T(8,128)(2,1)S(1)}, bf16[4,64,384]{2,1,0:T(8,128)(2,1)S(1)}, u32[]{:S(2)}, u32[]{:S(2)}) %collective-permute-start.4) | collective-permute-done | bytes 196640 | tf_op jit(solution)/shard_map/ppermute | solution.py:367
  42.3 3.5 %collective-permute-done.6.far = bf16[2,256,384]{2,1,0:T(8,128)(2,1)S(1)} collective-permute-done((bf16[2,256,384]{2,1,0:T(8,128)(2,1)S(1)}, bf16[2,256,384]{2,1,0:T(8,128)(2,1)S(1)}, u32[]{:S(2)}, u32[]{:S(2)}) %collective-permute-start.6) | collective-permute-done | bytes 393248 | tf_op jit(solution)/shard_map/ppermute | solution.py:363
  46.5 2.4 %collective-permute-done.5.far = bf16[2,256,384]{2,1,0:T(8,128)(2,1)S(1)} collective-permute-done((bf16[2,256,384]{2,1,0:T(8,128)(2,1)S(1)}, bf16[2,256,384]{2,1,0:T(8,128)(2,1)S(1)}, u32[]{:S(2)}, u32[]{:S(2)}) %collective-permute-start.5) | collective-permute-done | bytes 393248 | tf_op jit(solution)/shard_map/ppermute | solution.py:363
  48.9 1.3 collective-permute-start.7
  50.1 5.8 %encode.2 = f32[2,768]{1,0:T(2,128)S(1)} custom-call(s32[7]{0:T(128)S(1)} %pad_add_fusion.idx, bf16[4,256,384]{2,1,0:T(8,128)(2,1)S(1)} %copy-done.17, bf16[4,256,384]{2,1,0:T(8,128)(2,1)} %collective-permute-done.2.left, bf16[4,256,384]{2,1,0:T(8,128)(2,1)S(1)} %collective-permute-done.3.right, bf16[2,256,384]{2,1,0:T(8,128)(2,1)S(1)} %collective-permute-done.5.far, ...), custom_call_target="tpu_custom_call" | custom-call | flops 6000000000 | bytes 8000000 | tf_op jit(solution)/shard_map/encode/pallas_call | solution.py:101
  56.1 2.7 %collective-permute-start.8 = (bf16[16,16,384]{2,1,0:T(8,128)(2,1)S(1)}, bf16[16,16,384]{2,1,0:T(8,128)(2,1)S(1)}, u32[]{:S(2)}, u32[]{:S(2)}) collective-permute-start(bf16[16,16,384]{2,1,0:T(8,128)(2,1)S(1)} %get-tuple-element.28), channel_id=1, source_target_pairs={{0,128},{4,132},{8,136},{12,140},{16,144},{20,148},{24,152},{28,15... | collective-permute-start | bytes 589832 | tf_op jit(solution)/shard_map/ppermute | solution.py:367
  59.6 2.7 %collective-permute-done.8 = bf16[16,16,384]{2,1,0:T(8,128)(2,1)S(1)} collective-permute-done((bf16[16,16,384]{2,1,0:T(8,128)(2,1)S(1)}, bf16[16,16,384]{2,1,0:T(8,128)(2,1)S(1)}, u32[]{:S(2)}, u32[]{:S(2)}) %collective-permute-start.8) | collective-permute-done | bytes 196640 | tf_op jit(solution)/shard_map/ppermute | solution.py:367
  63.8 3.9 %collective-permute-start.9 = (bf16[1536,384]{1,0:T(8,128)(2,1)}, bf16[1536,384]{1,0:T(8,128)(2,1)S(1)}, u32[]{:S(2)}, u32[]{:S(2)}) collective-permute-start(bf16[1536,384]{1,0:T(8,128)(2,1)} %constant_dynamic-update-slice_fusion.6.mine), channel_id=1, source_target_pairs={{0,4},{4,0},{8,12},{12,8},{16,20},{20,16},{24,28},{28,24},{32,36},... | collective-permute-start | bytes 3538952 | tf_op jit(solution)/shard_map/ppermute | solution.py:367
  71.5 5.9 %encode.3 = f32[2,768]{1,0:T(2,128)S(1)} custom-call(s32[7]{0:T(128)S(1)} %pad_add_fusion.idx, bf16[4,256,384]{2,1,0:T(8,128)(2,1)S(1)} %copy-done.18, bf16[4,256,384]{2,1,0:T(8,128)(2,1)} %collective-permute-done.2.left, bf16[4,256,384]{2,1,0:T(8,128)(2,1)S(1)} %copy-done.10, bf16[2,256,384]{2,1,0:T(8,128)(2,1)S(1)} %copy-done.20, ...), custom_call_target="tpu_custom_call" | custom-call | flops 6000000000 | bytes 8000000 | tf_op jit(solution)/shard_map/encode/pallas_call | solution.py:101
  79.3 2.5 %collective-permute-done.12.d = f32[4,768]{1,0:T(4,128)S(1)} collective-permute-done((f32[4,768]{1,0:T(4,128)S(1)}, f32[4,768]{1,0:T(4,128)S(1)}, u32[]{:S(2)}, u32[]{:S(2)}) %collective-permute-start.12) | collective-permute-done | bytes 12320 | tf_op jit(solution)/shard_map/ppermute | solution.py:363
  83.7 1.5 %slice.68 = bf16[32,1,8]{2,1,0:T(2,128)(2,1)} slice(bf16[32,16,384]{2,1,0:T(8,128)(2,1)} %copy-done.21), slice={[0:32], [8:9], [0:8]} | slice | bytes 1024 | tf_op jit(solution)/shard_map/slice | solution.py:414
  85.2 1.4 %copy.14 = bf16[32,1,8]{0,2,1:T(8,128)(2,1)} copy(bf16[32,1,8]{2,1,0:T(2,128)(2,1)} %slice.68) | data formatting | bytes 1024 | tf_op jit(solution)/shard_map/slice | solution.py:414
  87.2 1.4 %copy.20 = bf16[32,1,8]{0,2,1:T(8,128)(2,1)} copy(bf16[32,1,8]{2,1,0:T(2,128)(2,1)} %slice.70) | data formatting | bytes 1024
  89.9 1.4 %copy.16 = s32[64,4]{1,0:T(8,128)} copy(s32[64,4]{0,1:T(4,128)} %slice_add_fusion) | data formatting | bytes 2048 | tf_op jit(solution)/shard_map/add | solution.py:416
  91.3 1.5 %reshape.49.pos = s32[256,1]{1,0:T(8,128)} reshape(s32[64,4]{1,0:T(8,128)} %copy.16) | data formatting | bytes 2048 | tf_op jit(solution)/shard_map/reshape | solution.py:416
  93.7 1.8 %key_flags.1.bias = f32[40,1024]{1,0:T(8,128)S(1)} custom-call(s32[7]{0:T(128)S(1)} %pad_add_fusion.idx, s32[256,1]{1,0:T(8,128)S(1)} %copy-done.7), custom_call_target="tpu_custom_call" | custom-call | tf_op jit(solution)/shard_map/key_flags/pallas_call | solution.py:243
  97.1 8.0 %all-to-all-start = ((bf16[64,4,640]{2,1,0:T(4,128)(2,1)}), bf16[64,4,640]{2,1,0:T(4,128)(2,1)}, u32[]{:S(2)}, u32[]{:S(2)}) async-start(bf16[64,4,640]{2,1,0:T(4,128)(2,1)} %broadcast_in_dim.10), calls=%async_computation | async-start | bytes 655360 | tf_op jit(solution)/shard_map/all_to_all | solution.py:426
  105.1 2.1 %reshape.48 = bf16[192,4,192]{2,1,0:T(4,128)(2,1)} reshape(bf16[192,768]{1,0:T(8,128)(2,1)} %param.21) | data formatting | bytes 589824 | tf_op jit(solution)/shard_map/reshape | solution.py:429
  107.2 1.8 %copy.22 = bf16[192,4,192]{2,0,1:T(8,128)(2,1)} copy(bf16[192,4,192]{2,1,0:T(4,128)(2,1)} %reshape.48) | data formatting | bytes 589824 | tf_op jit(solution)/shard_map/reshape | solution.py:429
  109.0 9.3 %all-to-all-done = bf16[64,4,640]{2,1,0:T(4,128)(2,1)} async-done(((bf16[64,4,640]{2,1,0:T(4,128)(2,1)}), bf16[64,4,640]{2,1,0:T(4,128)(2,1)}, u32[]{:S(2)}, u32[]{:S(2)}) %all-to-all-start) | async-done | bytes 327712 | tf_op jit(solution)/shard_map/all_to_all | solution.py:426
  118.3 1.8 %reshape.47.emb = bf16[256,640]{1,0:T(8,128)(2,1)} reshape(bf16[64,4,640]{2,1,0:T(4,128)(2,1)} %all-to-all-done) | data formatting | bytes 655360 | tf_op jit(solution)/shard_map/reshape | solution.py:427
  123.8 4.4 %attend.1 = (bf16[128,192]{1,0:T(8,128)(2,1)S(1)}, bf16[128,192]{1,0:T(8,128)(2,1)S(1)}, bf16[128,192]{1,0:T(8,128)(2,1)S(1)}, bf16[128,192]{1,0:T(8,128)(2,1)S(1)}) custom-call(s32[7]{0:T(128)S(1)} %pad_add_fusion.idx, f32[128,192]{1,0:T(8,128)S(1)} %copy-done.12, bf16[1536,384]{1,0:T(8,128)(2,1)} %constant_dynamic-update-slice_fusion.6.mine, ...), custom_call_target="tpu_custom_call" | custom-call | tf_op jit(solution)/shard_map/attend/pallas_call | solution.py:346
  128.3 2.0 %collective-permute-start.14 = (bf16[128,192]{1,0:T(8,128)(2,1)S(1)}, bf16[128,192]{1,0:T(8,128)(2,1)S(1)}, u32[]{:S(2)}, u32[]{:S(2)}) collective-permute-start(bf16[128,192]{1,0:T(8,128)(2,1)S(1)} %get-tuple-element.35), channel_id=1, source_target_pairs={{0,2},{1,3},{2,0},{3,1},{4,6},{5,7},{6,4},{7,5},{8,10},{9,11},{10,... | collective-permute-start | bytes 147464 | tf_op jit(solution)/shard_map/ppermute | solution.py:363
  131.1 2.3 %collective-permute-done.13 = bf16[128,192]{1,0:T(8,128)(2,1)S(1)} collective-permute-done((bf16[128,192]{1,0:T(8,128)(2,1)S(1)}, bf16[128,192]{1,0:T(8,128)(2,1)S(1)}, u32[]{:S(2)}, u32[]{:S(2)}) %collective-permute-start.13) | collective-permute-done | bytes 49184 | tf_op jit(solution)/shard_map/ppermute | solution.py:363
  (94 shorter events, 30.2 us)
Async XLA Ops:
  0.0 67.7 %copy-start = (bf16[1536,768]{1,0:T(8,128)(2,1)S(1)}, bf16[1536,768]{1,0:T(8,128)(2,1)}, u32[]{:S(2)}) copy-start(bf16[1536,768]{1,0:T(8,128)(2,1)} %param.17) | copy-start | bytes 7077892
  0.0 27.7 %collective-permute-start.3 = (bf16[4,256,384]{2,1,0:T(8,128)(2,1)}, bf16[4,256,384]{2,1,0:T(8,128)(2,1)S(1)}, u32[]{:S(2)}, u32[]{:S(2)}) collective-permute-start(bf16[4,256,384]{2,1,0:T(8,128)(2,1)} %own.3), channel_id=1, source_target_pairs={{0,3},{1,0},{2,1},{3,2},{4,7},{5,4},{6,5},{7,6},{8,11},{9,8},{10,9... | collective-permute-start | bytes 2359304 | tf_op jit(solution)/shard_map/ppermute | solution.py:363
  3.3 24.4 %collective-permute-start.2 = (bf16[4,256,384]{2,1,0:T(8,128)(2,1)}, bf16[4,256,384]{2,1,0:T(8,128)(2,1)}, u32[]{:S(2)}, u32[]{:S(2)}) collective-permute-start(bf16[4,256,384]{2,1,0:T(8,128)(2,1)} %own.3), channel_id=1, source_target_pairs={{0,1},{1,2},{2,3},{3,0},{4,5},{5,6},{6,7},{7,4},{8,9},{9,10},{10,1... | collective-permute-start | bytes 2359304 | tf_op jit(solution)/shard_map/ppermute | solution.py:363
  5.4 1.2 copy-start.1
  8.8 5.2 %copy-start.11 = (f32[128,192]{1,0:T(8,128)}, f32[128,192]{1,0:T(8,128)S(1)}, u32[]{:S(2)}) copy-start(f32[128,192]{1,0:T(8,128)S(1)} %get-tuple-element.21.q_cache) | copy-start | bytes 294916
  8.8 5.2 %collective-permute-start = (bf16[1,256,384]{2,1,0:T(8,128)(2,1)S(1)}, bf16[1,256,384]{2,1,0:T(8,128)(2,1)S(1)}, u32[]{:S(2)}, u32[]{:S(2)}) collective-permute-start(bf16[1,256,384]{2,1,0:T(8,128)(2,1)S(1)} %bitcast.23), channel_id=1, source_target_pairs={{0,8},{4,12},{8,0},{12,4},{16,24},{20,28},{24,16},{28,20},{32,40},... | collective-permute-start | bytes 589832 | tf_op jit(solution)/shard_map/ppermute | solution.py:367
  14.1 12.6 %collective-permute-start.1 = (bf16[2,128,384]{2,1,0:T(8,128)(2,1)S(1)}, bf16[2,128,384]{2,1,0:T(8,128)(2,1)}, u32[]{:S(2)}, u32[]{:S(2)}) collective-permute-start(bf16[2,128,384]{2,1,0:T(8,128)(2,1)S(1)} %get-tuple-element.43), channel_id=1, source_target_pairs={{0,16},{4,20},{8,24},{12,28},{16,0},{20,4},{24,8},{28,12},{32,48},... | collective-permute-start | bytes 589832 | tf_op jit(solution)/shard_map/ppermute | solution.py:367
  26.6 23.5 %copy-start.17 = (bf16[4,256,384]{2,1,0:T(8,128)(2,1)S(1)}, bf16[4,256,384]{2,1,0:T(8,128)(2,1)}, u32[]{:S(2)}) copy-start(bf16[4,256,384]{2,1,0:T(8,128)(2,1)} %own.3) | copy-start | bytes 2359300
  27.7 22.4 %copy-start.9 = (bf16[4,256,384]{2,1,0:T(8,128)(2,1)}, bf16[4,256,384]{2,1,0:T(8,128)(2,1)S(1)}, u32[]{:S(2)}) copy-start(bf16[4,256,384]{2,1,0:T(8,128)(2,1)S(1)} %collective-permute-done.3.right) | copy-start | bytes 2359300
  27.7 13.8 %collective-permute-start.4 = (bf16[4,64,384]{2,1,0:T(8,128)(2,1)S(1)}, bf16[4,64,384]{2,1,0:T(8,128)(2,1)S(1)}, u32[]{:S(2)}, u32[]{:S(2)}) collective-permute-start(bf16[4,64,384]{2,1,0:T(8,128)(2,1)S(1)} %get-tuple-element.23), channel_id=1, source_target_pairs={{0,32},{4,36},{8,40},{12,44},{16,48},{20,52},{24,56},{28,60},{32,0... | collective-permute-start | bytes 589832 | tf_op jit(solution)/shard_map/ppermute | solution.py:367
  34.9 15.2 %copy-start.15 = (bf16[1536,3,384]{2,0,1:T(8,128)(2,1)S(1)}, bf16[1536,3,384]{2,0,1:T(8,128)(2,1)}, u32[]{:S(2)}) copy-start(bf16[1536,3,384]{2,0,1:T(8,128)(2,1)} %param.15) | copy-start | bytes 10616836
  36.2 9.6 %collective-permute-start.6 = (bf16[2,256,384]{2,1,0:T(8,128)(2,1)S(1)}, bf16[2,256,384]{2,1,0:T(8,128)(2,1)S(1)}, u32[]{:S(2)}, u32[]{:S(2)}) collective-permute-start(bf16[2,256,384]{2,1,0:T(8,128)(2,1)S(1)} %slice.52), channel_id=1, source_target_pairs={{0,3},{1,0},{2,1},{3,2},{4,7},{5,4},{6,5},{7,6},{8,11},{9,8},{10,9... | collective-permute-start | bytes 1179656 | tf_op jit(solution)/shard_map/ppermute | solution.py:363
  38.6 10.2 %collective-permute-start.5 = (bf16[2,256,384]{2,1,0:T(8,128)(2,1)S(1)}, bf16[2,256,384]{2,1,0:T(8,128)(2,1)S(1)}, u32[]{:S(2)}, u32[]{:S(2)}) collective-permute-start(bf16[2,256,384]{2,1,0:T(8,128)(2,1)S(1)} %slice.51), channel_id=1, source_target_pairs={{0,1},{1,2},{2,3},{3,0},{4,5},{5,6},{6,7},{7,4},{8,9},{9,10},{10,1... | collective-permute-start | bytes 1179656 | tf_op jit(solution)/shard_map/ppermute | solution.py:363
  48.9 7.2 %collective-permute-start.7 = (bf16[8,32,384]{2,1,0:T(8,128)(2,1)S(1)}, bf16[8,32,384]{2,1,0:T(8,128)(2,1)S(1)}, u32[]{:S(2)}, u32[]{:S(2)}) collective-permute-start(bf16[8,32,384]{2,1,0:T(8,128)(2,1)S(1)} %get-tuple-element.26), channel_id=1, source_target_pairs={{0,64},{4,68},{8,72},{12,76},{16,80},{20,84},{24,88},{28,92},{32,9... | collective-permute-start | bytes 589832 | tf_op jit(solution)/shard_map/ppermute | solution.py:367
  56.0 3.6 %copy-start.13 = (f32[2,768]{1,0:T(2,128)}, f32[2,768]{1,0:T(2,128)S(1)}, u32[]{:S(2)}) copy-start(f32[2,768]{1,0:T(2,128)S(1)} %encode.2) | copy-start | bytes 18436
  56.1 6.1 %collective-permute-start.8 = (bf16[16,16,384]{2,1,0:T(8,128)(2,1)S(1)}, bf16[16,16,384]{2,1,0:T(8,128)(2,1)S(1)}, u32[]{:S(2)}, u32[]{:S(2)}) collective-permute-start(bf16[16,16,384]{2,1,0:T(8,128)(2,1)S(1)} %get-tuple-element.28), channel_id=1, source_target_pairs={{0,128},{4,132},{8,136},{12,140},{16,144},{20,148},{24,152},{28,15... | collective-permute-start | bytes 589832 | tf_op jit(solution)/shard_map/ppermute | solution.py:367
  63.8 22.8 %collective-permute-start.9 = (bf16[1536,384]{1,0:T(8,128)(2,1)}, bf16[1536,384]{1,0:T(8,128)(2,1)S(1)}, u32[]{:S(2)}, u32[]{:S(2)}) collective-permute-start(bf16[1536,384]{1,0:T(8,128)(2,1)} %constant_dynamic-update-slice_fusion.6.mine), channel_id=1, source_target_pairs={{0,4},{4,0},{8,12},{12,8},{16,20},{20,16},{24,28},{28,24},{32,36},... | collective-permute-start | bytes 3538952 | tf_op jit(solution)/shard_map/ppermute | solution.py:367
  67.7 1.3 copy-start.22
  69.0 1.1 copy-start.10
  69.0 2.2 %copy-start.16 = (bf16[1536,3,384]{2,0,1:T(8,128)(2,1)S(1)}, bf16[1536,3,384]{2,0,1:T(8,128)(2,1)}, u32[]{:S(2)}) copy-start(bf16[1536,3,384]{2,0,1:T(8,128)(2,1)} %param.15) | copy-start | bytes 10616836
  69.0 2.4 %copy-start.18 = (bf16[4,256,384]{2,1,0:T(8,128)(2,1)S(1)}, bf16[4,256,384]{2,1,0:T(8,128)(2,1)}, u32[]{:S(2)}) copy-start(bf16[4,256,384]{2,1,0:T(8,128)(2,1)} %own.3) | copy-start | bytes 2359300
  69.0 2.5 %copy-start.20 = (bf16[2,256,384]{2,1,0:T(8,128)(2,1)S(1)}, bf16[2,256,384]{2,1,0:T(8,128)(2,1)}, u32[]{:S(2)}) copy-start(bf16[2,256,384]{2,1,0:T(8,128)(2,1)} %copy-done.19) | copy-start | bytes 1179652
  71.5 5.9 %copy-start.14 = (f32[2,768]{1,0:T(2,128)S(1)}, f32[2,768]{1,0:T(2,128)}, u32[]{:S(2)}) copy-start(f32[2,768]{1,0:T(2,128)} %copy-done.13) | copy-start | bytes 18436
  77.4 5.3 %copy-start.2 = (bf16[768,3,192]{0,2,1:T(8,128)(2,1)S(1)}, bf16[768,3,192]{0,2,1:T(8,128)(2,1)}, u32[]{:S(2)}) copy-start(bf16[768,3,192]{0,2,1:T(8,128)(2,1)} %param.20) | copy-start | bytes 2654212
  77.7 4.1 %collective-permute-start.12 = (f32[4,768]{1,0:T(4,128)S(1)}, f32[4,768]{1,0:T(4,128)S(1)}, u32[]{:S(2)}, u32[]{:S(2)}) collective-permute-start(f32[4,768]{1,0:T(4,128)S(1)} %fusion.a), channel_id=1, source_target_pairs={{0,2},{1,3},{2,0},{3,1},{4,6},{5,7},{6,4},{7,5},{8,10},{9,11},{10,... | collective-permute-start | bytes 36872 | tf_op jit(solution)/shard_map/ppermute | solution.py:363
  77.7 4.1 %collective-permute-start.11 = (f32[4,768]{1,0:T(4,128)S(1)}, f32[4,768]{1,0:T(4,128)S(1)}, u32[]{:S(2)}, u32[]{:S(2)}) collective-permute-start(f32[4,768]{1,0:T(4,128)S(1)} %fusion.a), channel_id=1, source_target_pairs={{0,3},{1,0},{2,1},{3,2},{4,7},{5,4},{6,5},{7,6},{8,11},{9,8},{10,9... | collective-permute-start | bytes 36872 | tf_op jit(solution)/shard_map/ppermute | solution.py:363
  78.9 3.8 %collective-permute-start.10 = (f32[4,768]{1,0:T(4,128)S(1)}, f32[4,768]{1,0:T(4,128)S(1)}, u32[]{:S(2)}, u32[]{:S(2)}) collective-permute-start(f32[4,768]{1,0:T(4,128)S(1)} %fusion.a), channel_id=1, source_target_pairs={{0,1},{1,2},{2,3},{3,0},{4,5},{5,6},{6,7},{7,4},{8,9},{9,10},{10,1... | collective-permute-start | bytes 36872 | tf_op jit(solution)/shard_map/ppermute | solution.py:363
  97.1 21.2 %all-to-all-start = ((bf16[64,4,640]{2,1,0:T(4,128)(2,1)}), bf16[64,4,640]{2,1,0:T(4,128)(2,1)}, u32[]{:S(2)}, u32[]{:S(2)}) async-start(bf16[64,4,640]{2,1,0:T(4,128)(2,1)} %broadcast_in_dim.10), calls=%async_computation | async-start | bytes 655360 | tf_op jit(solution)/shard_map/all_to_all | solution.py:426
  120.0 1.0 copy-start.3
  128.2 5.2 %collective-permute-start.13 = (bf16[128,192]{1,0:T(8,128)(2,1)S(1)}, bf16[128,192]{1,0:T(8,128)(2,1)S(1)}, u32[]{:S(2)}, u32[]{:S(2)}) collective-permute-start(bf16[128,192]{1,0:T(8,128)(2,1)S(1)} %get-tuple-element.34), channel_id=1, source_target_pairs={{0,1},{1,2},{2,3},{3,0},{4,5},{5,6},{6,7},{7,4},{8,9},{9,10},{10,1... | collective-permute-start | bytes 147464 | tf_op jit(solution)/shard_map/ppermute | solution.py:363
  128.3 5.7 %collective-permute-start.14 = (bf16[128,192]{1,0:T(8,128)(2,1)S(1)}, bf16[128,192]{1,0:T(8,128)(2,1)S(1)}, u32[]{:S(2)}, u32[]{:S(2)}) collective-permute-start(bf16[128,192]{1,0:T(8,128)(2,1)S(1)} %get-tuple-element.35), channel_id=1, source_target_pairs={{0,2},{1,3},{2,0},{3,1},{4,6},{5,7},{6,4},{7,5},{8,10},{9,11},{10,... | collective-permute-start | bytes 147464 | tf_op jit(solution)/shard_map/ppermute | solution.py:363
  130.4 4.1 %collective-permute-start.15 = (bf16[128,192]{1,0:T(8,128)(2,1)S(1)}, bf16[128,192]{1,0:T(8,128)(2,1)S(1)}, u32[]{:S(2)}, u32[]{:S(2)}) collective-permute-start(bf16[128,192]{1,0:T(8,128)(2,1)S(1)} %get-tuple-element.36), channel_id=1, source_target_pairs={{0,3},{1,0},{2,1},{3,2},{4,7},{5,4},{6,5},{7,6},{8,11},{9,8},{10,9... | collective-permute-start | bytes 147464 | tf_op jit(solution)/shard_map/ppermute | solution.py:363
  (8 other events, 6.8 us)

commit v4 on v3

--- a/solution.py
+++ b/solution.py
@@ -191,12 +191,7 @@
             here = (column >= h * HDL) & (column < (h + 1) * HDL)
             got = jnp.where(here, kv[pl.ds(pick_start(first_head + h, level), n), :], got)
         if level == BRANCHES - 1:
-            lane = iota((8, 2 * heads_width), 1)
-            tail = jnp.zeros((8, 2 * heads_width), F32)
-            for slot in range(4):
-                high, low = slot_digits(idx, slot)
-                tail = jnp.where(lane == slot, high, jnp.where(lane == slot + 4, low, tail))
-            got = jnp.concatenate([got, tail], axis=0)
+            got = jnp.concatenate([got, jnp.zeros((8, 2 * heads_width), F32)], axis=0)
         picks[base : base + got.shape[0], :] = got.astype(BF)
         base += n
 
@@ -217,55 +212,29 @@
     )(idx, cache, gain, weight)
 
 
-def flag_kernel(idx, pos, out):
-    first_head, seq = idx[0] * 4, idx[1]
-    for level in range(BRANCHES):
-        last = level == BRANCHES - 1
-        keys = 1024 if last else 512
-        n = 16 if last else ROWS >> level
-        shift = n.bit_length() - 1
-        k = iota((8, keys), 1)
-        j = k & (n - 1)
-        half = keys // 2
-        source = seq ^ (2 * ((k & (half - 1)) >> shift) + (k >= half).astype(jnp.int32))
-        for h in range(4):
-            r = level * 8 + h
-            if level == 0 and h > 0:
-                out[r : r + 1, 0:keys] = out[0:1, 0:keys]
-                continue
-            place = source * ROWS + local_row(j & 7 if last else j, level, first_head + h)
-            hit = jnp.max(jnp.where(pos[...] == place[0:1], 1.0, 0.0), axis=0, keepdims=True)
-            gone = (hit > 0.0) | (j[0:1] >= 8) if last else hit > 0.0
-            out[r : r + 1, 0:keys] = jnp.where(gone, FLOOR_SCORE, 0.0)
-
-
-def key_flags(idx, pos):
-    return pl.pallas_call(
-        flag_kernel,
-        out_shape=jax.ShapeDtypeStruct((8 * BRANCHES, 1024), F32),
-        in_specs=[whole(pltpu.SMEM), whole()],
-        out_specs=whole(),
-        compiler_params=params(),
-        name="key_flags",
-    )(idx, pos)
-
-
 def depth_of(x):
     return sum(((x & mask) == 0).astype(jnp.int32) for mask in (1, 3, 7, 15))
 
 
 def attend_kernel(
-    idx, q_cache, mine, theirs, bias, emb, out_w, o0, o1, o2, o3, q, peak, total, acc
+    idx, q_cache, mine_hbm, theirs_hbm, emb, out_w, o0, o1, o2, o3, q, mine, theirs, peak, total, acc, sems
 ):
     mp, seq = idx[0], idx[1]
     first_head = mp * 4
     hw = q_cache.shape[1]
     scale = HDL ** (-0.5)
     slots = emb.shape[0]
+    loads = [
+        pltpu.make_async_copy(mine_hbm, mine, sems.at[0]),
+        pltpu.make_async_copy(theirs_hbm, theirs, sems.at[1]),
+    ]
+    for load in loads:
+        load.start()
     tail = emb[:, 3 * hw :]
     col = iota((8, tail.shape[1]), 1)
     digits = jnp.where(col == 0, 64.0, jnp.where(col == 1, 1.0, 0.0)).astype(BF)
     pos = dot_t(digits, tail).astype(jnp.int32)[0:1]
+    spread = dot_t(tail, digits).astype(jnp.int32)[:, 0:1]
     own = seq * ROWS + local_row(iota((ROWS, 1), 0), 0, 0)
     match = own == pos
     found = jnp.max(match.astype(jnp.int32), axis=1, keepdims=True) > 0
@@ -301,15 +270,31 @@
     total[...] = jnp.broadcast_to(jnp.sum(e, axis=-1, keepdims=True), total.shape)
     acc[...] = dot(e.astype(BF), emb[:, hw : 2 * hw])
 
+    for load in loads:
+        load.wait()
     for level in range(BRANCHES):
         n = ROWS >> level
         qb = full_q if level == 0 else queries(level)
         half = 512 if level == BRANCHES - 1 else 256
         low = BASES[level]
+        last = level == BRANCHES - 1
+        pitch = 16 if last else n
+        turned = (rev4(spread & 15) << 3) + ((spread & 127) >> 4)
+        cross_rows = (spread >> 7) ^ seq
+        key = (cross_rows & 1) * half + (cross_rows >> 1) * pitch + (turned & (n - 1))
+        inside = jnp.where((pos >= 0) & (first <= level), 1, 0)
+        head_row = first_head + iota((8, slots), 0)
+        hits = (((pos ^ head_row) & ((1 << level) - 1)) == 0) & (inside > 0)
+        key_lane = iota((slots, 2 * half), 1)
+        bias = dot(
+            jnp.where(hits, FLOOR_SCORE, 0.0).astype(BF), (key_lane == key).astype(BF)
+        )
+        if last:
+            bias = jnp.where((iota((8, 2 * half), 1) & 15) >= 8, FLOOR_SCORE, bias)
         sides = []
         for number, side in enumerate((mine, theirs)):
             s = dot_t(qb, side[low : low + half, 0:hw]) * scale
-            flags = bias[level * 8 : level * 8 + 4, number * half : (number + 1) * half]
+            flags = bias[0:4, number * half : (number + 1) * half]
             s = s.reshape(4, n, half) + flags[:, None, :]
             sides.append(s.reshape(4 * n, half))
         m = jnp.maximum(
@@ -341,22 +326,25 @@
         o[...] = dot(attended, out_w[lax.rem(mp + d, 4)]).astype(BF)
 
 
-def attend(idx, q_cache, mine, theirs, bias, emb, out_w):
+def attend(idx, q_cache, mine, theirs, emb, out_w):
     hw = q_cache.shape[1]
     return pl.pallas_call(
         attend_kernel,
         out_shape=(jax.ShapeDtypeStruct((ROWS, hw), BF),) * 4,
-        in_specs=[whole(pltpu.SMEM)] + [whole()] * 6,
+        in_specs=[whole(pltpu.SMEM), whole()] + [whole(pl.ANY)] * 2 + [whole()] * 2,
         out_specs=(whole(),) * 4,
         scratch_shapes=[
             pltpu.VMEM((ROWS, hw), F32),
+            pltpu.VMEM(mine.shape, BF),
+            pltpu.VMEM(mine.shape, BF),
             pltpu.VMEM((4 * ROWS, 128), F32),
             pltpu.VMEM((4 * ROWS, 128), F32),
             pltpu.VMEM((4 * ROWS, hw), F32),
+            pltpu.SemaphoreType.DMA((2,)),
         ],
         compiler_params=params(),
         name="attend",
-    )(idx, q_cache, mine, theirs, bias, emb, out_w)
+    )(idx, q_cache, mine, theirs, emb, out_w)
 
 
 def shift_mp(x, k):
@@ -393,41 +381,40 @@
     slide_w = long_qkv.transpose(1, 2, 0).reshape(3 * hw, model)
     gain_row = long_gain.reshape(1, model)
     q_cache, picks = slide_project(idx, seq_cache, gain_row, slide_w)
-    have = picks[None]
-    kept = []
-    for level, bit in enumerate((2, 4, 8, 16, 32)):
-        have = jnp.concatenate([have, swap_seq(have, bit)], axis=0)
-        n = ROWS >> level
-        if level < BRANCHES - 1:
-            kept.append(have[:, 0:n].reshape(-1, 2 * hw))
-            have = have[:, n:]
-        if level == 1:
-            have, left, right = lax.optimization_barrier((have, left, right))
-            far = [shift_mp(left[0:2], 1), shift_mp(right[2:4], 3)]
-        if level == 2:
-            have, *far = lax.optimization_barrier((have, *far))
-        if level == 3:
-            first = encode(idx, 0, tile_batch, left, right, far[0], gain, tile_w)
-            have, first = lax.optimization_barrier((have, first))
-    mine = jnp.concatenate(kept + [have.reshape(-1, 2 * hw)], axis=0)
-    theirs = swap_seq(mine, 1)
-    marks = jnp.concatenate([side[1024:].reshape(32, 16, 2 * hw)[:, 8, 0:8] for side in (mine, theirs)])
-    marks = marks.astype(jnp.int32)
-    all_pos = (marks[:, 0:4] * 64 + marks[:, 4:8]).reshape(64 * slots, 1)
-    bias = key_flags(idx, all_pos)
-
-    rows = [first, encode(idx, 1, tile_batch, left, right, far[1], gain, tile_w)]
     proj_here = lax.dynamic_slice_in_dim(tile_proj, mp * width, width, 0)
     joined = jnp.concatenate([dot(vit_out, tile_proj).astype(BF), proj_here], axis=0)
-    partial = dot(jnp.concatenate(rows, axis=0).astype(BF), joined)
+    far = [shift_mp(left[0:2], 1), shift_mp(right[2:4], 3)]
+
+    kept = []
+
+    def step(have, level):
+        have = jnp.concatenate([have, swap_seq(have, 2 << level)], axis=0)
+        if level == BRANCHES - 1:
+            return have
+        n = ROWS >> level
+        kept.append(have[:, 0:n].reshape(-1, 2 * hw))
+        return have[:, n:]
+
+    have = step(step(picks[None], 0), 1)
+    far[0], have, joined = lax.optimization_barrier((far[0], have, joined))
+    first = encode(idx, 0, tile_batch, left, right, far[0], gain, tile_w)
+    have = step(have, 2)
+    far[1], have, first = lax.optimization_barrier((far[1], have, first))
+    second = encode(idx, 1, tile_batch, left, right, far[1], gain, tile_w)
+    have = step(have, 3)
+    first, second, have = lax.optimization_barrier((first, second, have))
+    partial = dot(jnp.concatenate([first, second], axis=0).astype(BF), joined)
     shares = [partial] + [shift_mp(partial, k) for k in (1, 3, 2)]
+    have = step(have, 4)
+    mine = jnp.concatenate(kept + [have.reshape(-1, 2 * hw)], axis=0)
+    shares, mine = lax.optimization_barrier((shares, mine))
+    theirs = swap_seq(mine, 1)
     emb = embed_rows(idx, shares, gain_row, slide_w)
-    emb, bias = lax.optimization_barrier((emb, bias))
     emb = lax.all_to_all(jnp.broadcast_to(emb[None], (64,) + emb.shape), "seq", 0, 0)
     emb = emb.reshape(64 * slots, emb.shape[2])
 
     out_w = long_out.reshape(hw, 4, hw).transpose(1, 0, 2)
-    o0, o1, o2, o3 = attend(idx, q_cache, mine, theirs, bias, emb, out_w)
+    o0, o1, o2, o3 = attend(idx, q_cache, mine, theirs, emb, out_w)
     terms = [o0, shift_mp(o1, 1), shift_mp(o2, 2), shift_mp(o3, 3)]
     a, b, c, d = [term.astype(F32) for term in terms]
     return ((a + b) + (c + d)).astype(BF)

time: 136 us -> 110 us (0.81)
  waiting for transfers between devices: 38.1 us -> 18.4 us
  local copies, waits for them, and re-layouts: 33.1 us -> 18.9 us
  starting transfers between devices: 38.3 us -> 42.7 us
  matrix products: 1.35 us -> 3.44 us
    ppermute x6, waiting for transfers between devices: 16.2 us -> 4.56 us  [swap_seq(): return lax.ppermute(x, 'seq', [(i, i ^ bit) for i in range(64)])]
    ppermute x10, waiting for transfers between devices: 12.6 us -> 4.54 us  [shift_mp(): return lax.ppermute(x, 'mp', [(i, (i + k) % 4) for i in range(4)])]
    unnamed x54 -> x38, local copies, waits for them, and re-layouts: 15.9 us -> 8.84 us
    slice x6 -> x2, local copies, waits for them, and re-layouts: 3.61 us -> 0.08 us  [step(): kept.append(have[:, 0:n].reshape(-1, 2 * hw))]
    ppermute x10, starting transfers between devices: 10.2 us -> 12.9 us  [shift_mp(): return lax.ppermute(x, 'mp', [(i, (i + k) % 4) for i in range(4)])]
    dot_general x2, matrix products: 1.35 us -> 3.44 us  [dot(): return jnp.dot(a, b, preferred_element_type=F32)]
    pallas_call x1, Pallas kernels: 4.42 us -> 6.46 us  [attend(): pl.pallas_call(attend_kernel, out_shape=(jax.ShapeDtypeStruct((ROWS, hw),...]
    concatenate x2 -> x4, other arithmetic: 1.1 us -> 3.04 us  [the longest x3 1.92 us: step(): have = jnp.concatenate([have, swap_seq(have, 2 << level)], axis=0)]
  transfers between devices with their start and end apart: 17 -> 17, of which waited for: 12 -> 8; matrix products, arithmetic and copies ran while one was open for 11% -> 16% of each run, Pallas kernels for 10% -> 13%
where the time goes in v4:
time: 110 us; the launch traced here: 109 us
  starting transfers between devices  42.7 us (39%)
  Pallas kernels  20.6 us (19%)
  local copies, waits for them, and re-layouts  18.9 us (17%)
  waiting for transfers between devices  18.4 us (17%)
  other arithmetic  3.82 us (3%)
  matrix products  3.44 us (3%)
    ppermute x6, starting transfers between devices, swap_seq(): return lax.ppermute(x, 'seq', [(i, i ^ bit) for i in range(64)])  21.8 us
    ppermute x10, starting transfers between devices, shift_mp(): return lax.ppermute(x, 'mp', [(i, (i + k) % 4) for i in range(4)])  12.9 us
    pallas_call x2, Pallas kernels, encode(): pl.pallas_call(encode_kernel, grid=(1,), out_shape=jax.ShapeDtypeStruct((...  11.8 us
    all_to_all x1, waiting for transfers between devices, local(): lax.all_to_all(jnp.broadcast_to(emb[None], (64,) + emb.shape), 'seq', 0, 0)  9.31 us
    unnamed x38, local copies, waits for them, and re-layouts  8.84 us
    all_to_all x1, starting transfers between devices, local(): lax.all_to_all(jnp.broadcast_to(emb[None], (64,) + emb.shape), 'seq', 0, 0)  8.06 us
    pallas_call x1, Pallas kernels, attend(): pl.pallas_call(attend_kernel, out_shape=(jax.ShapeDtypeStruct((ROWS, hw),...  6.46 us
    ppermute x6, waiting for transfers between devices, swap_seq(): return lax.ppermute(x, 'seq', [(i, i ^ bit) for i in range(64)])  4.56 us
  transfers between devices with their start and end apart: 17, of which 8 were waited for; matrix products, arithmetic and copies ran while one was open for 16% of the time, Pallas kernels for 13%

profile of v4, /device:TPU:1, one launch (start us, length us, event | category | flops | bytes accessed | tf_op | source)
XLA Modules:
  0.0 108.8 jit_solution(15583367870352820029)
XLA Ops:
  0.0 2.0 %collective-permute-start.2 = (bf16[4,256,384]{2,1,0:T(8,128)(2,1)}, bf16[4,256,384]{2,1,0:T(8,128)(2,1)S(1)}, u32[]{:S(2)}, u32[]{:S(2)}) collective-permute-start(bf16[4,256,384]{2,1,0:T(8,128)(2,1)} %own.3), channel_id=1, source_target_pairs={{0,1},{1,2},{2,3},{3,0},{4,5},{5,6},{6,7},{7,4},{8,9},{9,10},{10,1... | collective-permute-start | bytes 2359304 | tf_op jit(solution)/shard_map/ppermute | solution.py:351
  2.0 1.4 %collective-permute-start = (bf16[4,256,384]{2,1,0:T(8,128)(2,1)}, bf16[4,256,384]{2,1,0:T(8,128)(2,1)}, u32[]{:S(2)}, u32[]{:S(2)}) collective-permute-start(bf16[4,256,384]{2,1,0:T(8,128)(2,1)} %own.3), channel_id=1, source_target_pairs={{0,3},{1,0},{2,1},{3,2},{4,7},{5,4},{6,5},{7,6},{8,11},{9,8},{10,9... | collective-permute-start | bytes 2359304 | tf_op jit(solution)/shard_map/ppermute | solution.py:351
  5.5 1.2 %copy-done.1 = bf16[768,3,192]{0,2,1:T(8,128)(2,1)S(1)} copy-done((bf16[768,3,192]{0,2,1:T(8,128)(2,1)S(1)}, bf16[768,3,192]{0,2,1:T(8,128)(2,1)}, u32[]{:S(2)}) %copy-start.1) | copy-done | bytes 884760
  7.6 1.3 %slide_project.1 = (f32[128,192]{1,0:T(8,128)S(1)}, bf16[256,384]{1,0:T(8,128)(2,1)S(1)}) custom-call(s32[7]{0:T(128)S(1)} %pad_add_fusion.idx, bf16[128,768]{1,0:T(8,128)(2,1)S(1)} %copy-done.5, f32[1,768]{1,0:T(1,128)S(1)} %reshape.31.gain, bf16[576,768]{1,0:T(8,128)(2,1)S(1)} %bitcast.18), custom_call_target="tpu_custom_call" | custom-call | tf_op jit(solution)/shard_map/slide_project/pallas_call | solution.py:201
  9.5 1.8 %collective-permute-start.4 = (bf16[1,256,384]{2,1,0:T(8,128)(2,1)S(1)}, bf16[1,256,384]{2,1,0:T(8,128)(2,1)S(1)}, u32[]{:S(2)}, u32[]{:S(2)}) collective-permute-start(bf16[1,256,384]{2,1,0:T(8,128)(2,1)S(1)} %bitcast.21), channel_id=1, source_target_pairs={{0,8},{4,12},{8,0},{12,4},{16,24},{20,28},{24,16},{28,20},{32,40},... | collective-permute-start | bytes 589832 | tf_op jit(solution)/shard_map/ppermute | solution.py:355
  11.3 3.2 %convolution_convert_fusion = bf16[384,768]{1,0:T(8,128)(2,1)} fusion(bf16[384,1536]{1,0:T(8,128)(2,1)} %param.16, bf16[1536,768]{1,0:T(8,128)(2,1)S(1)} %copy-done), kind=kOutput, calls=%fused_computation | convolution fusion | flops 906264576 | bytes 4128768 | tf_op jit(solution)/shard_map/dot_general | solution.py:31
  15.5 3.5 %collective-permute-start.5 = (bf16[2,128,384]{2,1,0:T(8,128)(2,1)}, bf16[2,128,384]{2,1,0:T(8,128)(2,1)}, u32[]{:S(2)}, u32[]{:S(2)}) collective-permute-start(bf16[2,128,384]{2,1,0:T(8,128)(2,1)} %get-tuple-element.52), channel_id=1, source_target_pairs={{0,16},{4,20},{8,24},{12,28},{16,0},{20,4},{24,8},{28,12},{32,48},... | collective-permute-start | bytes 589832 | tf_op jit(solution)/shard_map/ppermute | solution.py:355
  19.9 1.4 %collective-permute-start.3 = (bf16[2,256,384]{2,1,0:T(8,128)(2,1)}, bf16[2,256,384]{2,1,0:T(8,128)(2,1)}, u32[]{:S(2)}, u32[]{:S(2)}) collective-permute-start(bf16[2,256,384]{2,1,0:T(8,128)(2,1)} %slice.41), channel_id=1, source_target_pairs={{0,1},{1,2},{2,3},{3,0},{4,5},{5,6},{6,7},{7,4},{8,9},{9,10},{10,1... | collective-permute-start | bytes 1179656 | tf_op jit(solution)/shard_map/ppermute | solution.py:351
  21.3 1.1 %pad_maximum_fusion = bf16[768,768]{1,0:T(8,128)(2,1)} fusion(bf16[384,768]{1,0:T(8,128)(2,1)S(1)} %constant_dynamic-slice_fusion, bf16[384,768]{1,0:T(8,128)(2,1)S(1)} %copy-done.14), kind=kLoop, calls=%fused_computation.1 | loop fusion | flops 2359296 | bytes 2359296 | tf_op jit(solution)/shard_map/concatenate | solution.py:385
  22.5 1.1 constant_dynamic-update-slice_fusion.8
  23.6 4.3 %collective-permute-done.5 = bf16[2,128,384]{2,1,0:T(8,128)(2,1)} collective-permute-done((bf16[2,128,384]{2,1,0:T(8,128)(2,1)}, bf16[2,128,384]{2,1,0:T(8,128)(2,1)}, u32[]{:S(2)}, u32[]{:S(2)}) %collective-permute-start.5) | collective-permute-done | bytes 196640 | tf_op jit(solution)/shard_map/ppermute | solution.py:355
  27.9 1.1 pad_maximum_fusion.2
  29.0 1.0 slice.40
  30.0 1.3 %collective-permute-start.1 = (bf16[2,256,384]{2,1,0:T(8,128)(2,1)S(1)}, bf16[2,256,384]{2,1,0:T(8,128)(2,1)S(1)}, u32[]{:S(2)}, u32[]{:S(2)}) collective-permute-start(bf16[2,256,384]{2,1,0:T(8,128)(2,1)S(1)} %slice.40), channel_id=1, source_target_pairs={{0,3},{1,0},{2,1},{3,2},{4,7},{5,4},{6,5},{7,6},{8,11},{9,8},{10,9... | collective-permute-start | bytes 1179656 | tf_op jit(solution)/shard_map/ppermute | solution.py:351
  31.4 7.6 %collective-permute-start.6 = (bf16[4,64,384]{2,1,0:T(8,128)(2,1)S(1)}, bf16[4,64,384]{2,1,0:T(8,128)(2,1)S(1)}, u32[]{:S(2)}, u32[]{:S(2)}) collective-permute-start(bf16[4,64,384]{2,1,0:T(8,128)(2,1)S(1)} %get-tuple-element.27), channel_id=1, source_target_pairs={{0,32},{4,36},{8,40},{12,44},{16,48},{20,52},{24,56},{28,60},{32,0... | collective-permute-start | bytes 589832 | tf_op jit(solution)/shard_map/ppermute | solution.py:355
  39.0 2.0 %copy-done.10 = bf16[1536,3,384]{2,0,1:T(8,128)(2,1)S(1)} copy-done((bf16[1536,3,384]{2,0,1:T(8,128)(2,1)S(1)}, bf16[1536,3,384]{2,0,1:T(8,128)(2,1)}, u32[]{:S(2)}) %copy-start.10) | copy-done | bytes 3538968
  41.0 6.0 %encode.2 = f32[2,768]{1,0:T(2,128)S(1)} custom-call(s32[7]{0:T(128)S(1)} %pad_add_fusion.idx, bf16[4,256,384]{2,1,0:T(8,128)(2,1)S(1)} %copy-done.12, bf16[4,256,384]{2,1,0:T(8,128)(2,1)S(1)} %copy-done.7, bf16[4,256,384]{2,1,0:T(8,128)(2,1)} %collective-permute-done.right, bf16[2,256,384]{2,1,0:T(8,128)(2,1)} %collective-permute-done.3.far, ...), custom_call_target="tpu_custom_call" | custom-call | flops 6000000000 | bytes 8000000 | tf_op jit(solution)/shard_map/encode/pallas_call | solution.py:101
  47.2 1.6 %collective-permute-start.7 = (bf16[8,32,384]{2,1,0:T(8,128)(2,1)S(1)}, bf16[8,32,384]{2,1,0:T(8,128)(2,1)S(1)}, u32[]{:S(2)}, u32[]{:S(2)}) collective-permute-start(bf16[8,32,384]{2,1,0:T(8,128)(2,1)S(1)} %get-tuple-element.31), channel_id=1, source_target_pairs={{0,64},{4,68},{8,72},{12,76},{16,80},{20,84},{24,88},{28,92},{32,9... | collective-permute-start | bytes 589832 | tf_op jit(solution)/shard_map/ppermute | solution.py:355
  48.8 5.8 %encode.3 = f32[2,768]{1,0:T(2,128)S(1)} custom-call(s32[7]{0:T(128)S(1)} %pad_add_fusion.idx, bf16[4,256,384]{2,1,0:T(8,128)(2,1)S(1)} %copy-done.12, bf16[4,256,384]{2,1,0:T(8,128)(2,1)S(1)} %copy-done.7, bf16[4,256,384]{2,1,0:T(8,128)(2,1)} %collective-permute-done.right, bf16[2,256,384]{2,1,0:T(8,128)(2,1)S(1)} %collective-permute-done.1.far, ...), custom_call_target="tpu_custom_call" | custom-call | flops 6000000000 | bytes 8000000 | tf_op jit(solution)/shard_map/encode/pallas_call | solution.py:101
  54.8 2.7 %collective-permute-start.11 = (bf16[16,16,384]{2,1,0:T(8,128)(2,1)S(1)}, bf16[16,16,384]{2,1,0:T(8,128)(2,1)S(1)}, u32[]{:S(2)}, u32[]{:S(2)}) collective-permute-start(bf16[16,16,384]{2,1,0:T(8,128)(2,1)S(1)} %get-tuple-element.35), channel_id=1, source_target_pairs={{0,128},{4,132},{8,136},{12,140},{16,144},{20,148},{24,152},{28,15... | collective-permute-start | bytes 589832 | tf_op jit(solution)/shard_map/ppermute | solution.py:355
  58.6 2.4 %collective-permute-start.9 = (f32[4,768]{1,0:T(4,128)S(1)}, f32[4,768]{1,0:T(4,128)S(1)}, u32[]{:S(2)}, u32[]{:S(2)}) collective-permute-start(f32[4,768]{1,0:T(4,128)S(1)} %fusion.2.a), channel_id=1, source_target_pairs={{0,3},{1,0},{2,1},{3,2},{4,7},{5,4},{6,5},{7,6},{8,11},{9,8},{10,9... | collective-permute-start | bytes 36872 | tf_op jit(solution)/shard_map/ppermute | solution.py:351
  62.1 4.6 %collective-permute-start.12 = (bf16[1536,384]{1,0:T(8,128)(2,1)S(1)}, bf16[1536,384]{1,0:T(8,128)(2,1)}, u32[]{:S(2)}, u32[]{:S(2)}) collective-permute-start(bf16[1536,384]{1,0:T(8,128)(2,1)S(1)} %constant_dynamic-update-slice_fusion.4.mine_hbm), channel_id=1, source_target_pairs={{0,4},{4,0},{8,12},{12,8},{16,20},{20,16},{24,28},{28,24},{32,36},... | collective-permute-start | bytes 3538952 | tf_op jit(solution)/shard_map/ppermute | solution.py:355
  66.7 1.0 embed_rows.1
  68.6 8.1 %all-to-all-start = ((bf16[64,4,640]{2,1,0:T(4,128)(2,1)}), bf16[64,4,640]{2,1,0:T(4,128)(2,1)}, u32[]{:S(2)}, u32[]{:S(2)}) async-start(bf16[64,4,640]{2,1,0:T(4,128)(2,1)} %broadcast_in_dim.10), calls=%async_computation | async-start | bytes 655360 | tf_op jit(solution)/shard_map/all_to_all | solution.py:413
  76.6 2.1 %reshape.40 = bf16[192,4,192]{2,1,0:T(4,128)(2,1)} reshape(bf16[192,768]{1,0:T(8,128)(2,1)} %param.21) | data formatting | bytes 589824 | tf_op jit(solution)/shard_map/reshape | solution.py:416
  78.7 1.8 %copy.16 = bf16[192,4,192]{2,0,1:T(8,128)(2,1)} copy(bf16[192,4,192]{2,1,0:T(4,128)(2,1)} %reshape.40) | data formatting | bytes 589824 | tf_op jit(solution)/shard_map/reshape | solution.py:416
  80.5 9.3 %all-to-all-done = bf16[64,4,640]{2,1,0:T(4,128)(2,1)} async-done(((bf16[64,4,640]{2,1,0:T(4,128)(2,1)}), bf16[64,4,640]{2,1,0:T(4,128)(2,1)}, u32[]{:S(2)}, u32[]{:S(2)}) %all-to-all-start) | async-done | bytes 327712 | tf_op jit(solution)/shard_map/all_to_all | solution.py:413
  89.8 1.8 %reshape.39.emb = bf16[256,640]{1,0:T(8,128)(2,1)} reshape(bf16[64,4,640]{2,1,0:T(4,128)(2,1)} %all-to-all-done) | data formatting | bytes 655360 | tf_op jit(solution)/shard_map/reshape | solution.py:414
  91.6 1.0 copy-done.3
  94.4 6.5 %attend.1 = (bf16[128,192]{1,0:T(8,128)(2,1)S(1)}, bf16[128,192]{1,0:T(8,128)(2,1)S(1)}, bf16[128,192]{1,0:T(8,128)(2,1)S(1)}, bf16[128,192]{1,0:T(8,128)(2,1)S(1)}) custom-call(s32[7]{0:T(128)S(1)} %pad_add_fusion.idx, f32[128,192]{1,0:T(8,128)S(1)} %copy-done.9, bf16[1536,384]{1,0:T(8,128)(2,1)S(1)} %constant_dynamic-update-slice_fusion.4.mine_hbm, ...), custom_call_target="tpu_custom_call" | custom-call | tf_op jit(solution)/shard_map/attend/pallas_call | solution.py:331
  101.4 3.0 %collective-permute-start.14 = (bf16[128,192]{1,0:T(8,128)(2,1)S(1)}, bf16[128,192]{1,0:T(8,128)(2,1)S(1)}, u32[]{:S(2)}, u32[]{:S(2)}) collective-permute-start(bf16[128,192]{1,0:T(8,128)(2,1)S(1)} %get-tuple-element.43), channel_id=1, source_target_pairs={{0,2},{1,3},{2,0},{3,1},{4,6},{5,7},{6,4},{7,5},{8,10},{9,11},{10,... | collective-permute-start | bytes 147464 | tf_op jit(solution)/shard_map/ppermute | solution.py:351
  105.3 2.0 %collective-permute-done.14 = bf16[128,192]{1,0:T(8,128)(2,1)S(1)} collective-permute-done((bf16[128,192]{1,0:T(8,128)(2,1)S(1)}, bf16[128,192]{1,0:T(8,128)(2,1)S(1)}, u32[]{:S(2)}, u32[]{:S(2)}) %collective-permute-start.14) | collective-permute-done | bytes 49184 | tf_op jit(solution)/shard_map/ppermute | solution.py:351
  (70 shorter events, 13.0 us)
Async XLA Ops:
  0.0 11.3 %copy-start = (bf16[1536,768]{1,0:T(8,128)(2,1)S(1)}, bf16[1536,768]{1,0:T(8,128)(2,1)}, u32[]{:S(2)}) copy-start(bf16[1536,768]{1,0:T(8,128)(2,1)} %param.17) | copy-start | bytes 7077892
  0.0 19.1 %collective-permute-start.2 = (bf16[4,256,384]{2,1,0:T(8,128)(2,1)}, bf16[4,256,384]{2,1,0:T(8,128)(2,1)S(1)}, u32[]{:S(2)}, u32[]{:S(2)}) collective-permute-start(bf16[4,256,384]{2,1,0:T(8,128)(2,1)} %own.3), channel_id=1, source_target_pairs={{0,1},{1,2},{2,3},{3,0},{4,5},{5,6},{6,7},{7,4},{8,9},{9,10},{10,1... | collective-permute-start | bytes 2359304 | tf_op jit(solution)/shard_map/ppermute | solution.py:351
  2.0 27.0 %collective-permute-start = (bf16[4,256,384]{2,1,0:T(8,128)(2,1)}, bf16[4,256,384]{2,1,0:T(8,128)(2,1)}, u32[]{:S(2)}, u32[]{:S(2)}) collective-permute-start(bf16[4,256,384]{2,1,0:T(8,128)(2,1)} %own.3), channel_id=1, source_target_pairs={{0,3},{1,0},{2,1},{3,2},{4,7},{5,4},{6,5},{7,6},{8,11},{9,8},{10,9... | collective-permute-start | bytes 2359304 | tf_op jit(solution)/shard_map/ppermute | solution.py:351
  5.5 1.2 %copy-start.1 = (bf16[768,3,192]{0,2,1:T(8,128)(2,1)S(1)}, bf16[768,3,192]{0,2,1:T(8,128)(2,1)}, u32[]{:S(2)}) copy-start(bf16[768,3,192]{0,2,1:T(8,128)(2,1)} %param.20) | copy-start | bytes 2654212
  6.6 0.9 copy-start.5
  9.5 5.2 %collective-permute-start.4 = (bf16[1,256,384]{2,1,0:T(8,128)(2,1)S(1)}, bf16[1,256,384]{2,1,0:T(8,128)(2,1)S(1)}, u32[]{:S(2)}, u32[]{:S(2)}) collective-permute-start(bf16[1,256,384]{2,1,0:T(8,128)(2,1)S(1)} %bitcast.21), channel_id=1, source_target_pairs={{0,8},{4,12},{8,0},{12,4},{16,24},{20,28},{24,16},{28,20},{32,40},... | collective-permute-start | bytes 589832 | tf_op jit(solution)/shard_map/ppermute | solution.py:355
  14.5 6.9 %copy-start.14 = (bf16[384,768]{1,0:T(8,128)(2,1)S(1)}, bf16[384,768]{1,0:T(8,128)(2,1)}, u32[]{:S(2)}) copy-start(bf16[384,768]{1,0:T(8,128)(2,1)} %convolution_convert_fusion) | copy-start | bytes 1769476
  15.5 12.3 %collective-permute-start.5 = (bf16[2,128,384]{2,1,0:T(8,128)(2,1)}, bf16[2,128,384]{2,1,0:T(8,128)(2,1)}, u32[]{:S(2)}, u32[]{:S(2)}) collective-permute-start(bf16[2,128,384]{2,1,0:T(8,128)(2,1)} %get-tuple-element.52), channel_id=1, source_target_pairs={{0,16},{4,20},{8,24},{12,28},{16,0},{20,4},{24,8},{28,12},{32,48},... | collective-permute-start | bytes 589832 | tf_op jit(solution)/shard_map/ppermute | solution.py:355
  19.1 3.4 %copy-start.6 = (bf16[4,256,384]{2,1,0:T(8,128)(2,1)}, bf16[4,256,384]{2,1,0:T(8,128)(2,1)S(1)}, u32[]{:S(2)}) copy-start(bf16[4,256,384]{2,1,0:T(8,128)(2,1)S(1)} %collective-permute-done.2.left) | copy-start | bytes 2359300
  19.9 2.6 %copy-start.15 = (f32[1536]{0:T(1024)S(1)}, f32[1536]{0:T(1024)}, u32[]{:S(2)}) copy-start(f32[1536]{0:T(1024)} %param.14) | copy-start | bytes 18436
  19.9 11.5 %collective-permute-start.3 = (bf16[2,256,384]{2,1,0:T(8,128)(2,1)}, bf16[2,256,384]{2,1,0:T(8,128)(2,1)}, u32[]{:S(2)}, u32[]{:S(2)}) collective-permute-start(bf16[2,256,384]{2,1,0:T(8,128)(2,1)} %slice.41), channel_id=1, source_target_pairs={{0,1},{1,2},{2,3},{3,0},{4,5},{5,6},{6,7},{7,4},{8,9},{9,10},{10,1... | collective-permute-start | bytes 1179656 | tf_op jit(solution)/shard_map/ppermute | solution.py:351
  22.5 16.5 %copy-start.7 = (bf16[4,256,384]{2,1,0:T(8,128)(2,1)S(1)}, bf16[4,256,384]{2,1,0:T(8,128)(2,1)}, u32[]{:S(2)}) copy-start(bf16[4,256,384]{2,1,0:T(8,128)(2,1)} %copy-done.6) | copy-start | bytes 2359300
  22.5 16.5 %copy-start.12 = (bf16[4,256,384]{2,1,0:T(8,128)(2,1)S(1)}, bf16[4,256,384]{2,1,0:T(8,128)(2,1)}, u32[]{:S(2)}) copy-start(bf16[4,256,384]{2,1,0:T(8,128)(2,1)} %own.3) | copy-start | bytes 2359300
  30.0 17.2 %collective-permute-start.1 = (bf16[2,256,384]{2,1,0:T(8,128)(2,1)S(1)}, bf16[2,256,384]{2,1,0:T(8,128)(2,1)S(1)}, u32[]{:S(2)}, u32[]{:S(2)}) collective-permute-start(bf16[2,256,384]{2,1,0:T(8,128)(2,1)S(1)} %slice.40), channel_id=1, source_target_pairs={{0,3},{1,0},{2,1},{3,2},{4,7},{5,4},{6,5},{7,6},{8,11},{9,8},{10,9... | collective-permute-start | bytes 1179656 | tf_op jit(solution)/shard_map/ppermute | solution.py:351
  31.4 15.7 %collective-permute-start.6 = (bf16[4,64,384]{2,1,0:T(8,128)(2,1)S(1)}, bf16[4,64,384]{2,1,0:T(8,128)(2,1)S(1)}, u32[]{:S(2)}, u32[]{:S(2)}) collective-permute-start(bf16[4,64,384]{2,1,0:T(8,128)(2,1)S(1)} %get-tuple-element.27), channel_id=1, source_target_pairs={{0,32},{4,36},{8,40},{12,44},{16,48},{20,52},{24,56},{28,60},{32,0... | collective-permute-start | bytes 589832 | tf_op jit(solution)/shard_map/ppermute | solution.py:355
  39.0 2.0 %copy-start.10 = (bf16[1536,3,384]{2,0,1:T(8,128)(2,1)S(1)}, bf16[1536,3,384]{2,0,1:T(8,128)(2,1)}, u32[]{:S(2)}) copy-start(bf16[1536,3,384]{2,0,1:T(8,128)(2,1)} %param.15) | copy-start | bytes 10616836
  41.0 7.8 %copy-start.11 = (bf16[1536,3,384]{2,0,1:T(8,128)(2,1)S(1)}, bf16[1536,3,384]{2,0,1:T(8,128)(2,1)}, u32[]{:S(2)}) copy-start(bf16[1536,3,384]{2,0,1:T(8,128)(2,1)} %param.15) | copy-start | bytes 10616836
  47.2 7.4 %collective-permute-start.7 = (bf16[8,32,384]{2,1,0:T(8,128)(2,1)S(1)}, bf16[8,32,384]{2,1,0:T(8,128)(2,1)S(1)}, u32[]{:S(2)}, u32[]{:S(2)}) collective-permute-start(bf16[8,32,384]{2,1,0:T(8,128)(2,1)S(1)} %get-tuple-element.31), channel_id=1, source_target_pairs={{0,64},{4,68},{8,72},{12,76},{16,80},{20,84},{24,88},{28,92},{32,9... | collective-permute-start | bytes 589832 | tf_op jit(solution)/shard_map/ppermute | solution.py:355
  54.6 2.9 %copy-start.13 = (bf16[768,768]{1,0:T(8,128)(2,1)S(1)}, bf16[768,768]{1,0:T(8,128)(2,1)}, u32[]{:S(2)}) copy-start(bf16[768,768]{1,0:T(8,128)(2,1)} %pad_maximum_fusion) | copy-start | bytes 3538948
  54.8 6.3 %collective-permute-start.11 = (bf16[16,16,384]{2,1,0:T(8,128)(2,1)S(1)}, bf16[16,16,384]{2,1,0:T(8,128)(2,1)S(1)}, u32[]{:S(2)}, u32[]{:S(2)}) collective-permute-start(bf16[16,16,384]{2,1,0:T(8,128)(2,1)S(1)} %get-tuple-element.35), channel_id=1, source_target_pairs={{0,128},{4,132},{8,136},{12,140},{16,144},{20,148},{24,152},{28,15... | collective-permute-start | bytes 589832 | tf_op jit(solution)/shard_map/ppermute | solution.py:355
  57.8 8.9 %copy-start.2 = (bf16[768,3,192]{0,2,1:T(8,128)(2,1)S(1)}, bf16[768,3,192]{0,2,1:T(8,128)(2,1)}, u32[]{:S(2)}) copy-start(bf16[768,3,192]{0,2,1:T(8,128)(2,1)} %param.20) | copy-start | bytes 2654212
  57.8 4.1 %collective-permute-start.10 = (f32[4,768]{1,0:T(4,128)S(1)}, f32[4,768]{1,0:T(4,128)S(1)}, u32[]{:S(2)}, u32[]{:S(2)}) collective-permute-start(f32[4,768]{1,0:T(4,128)S(1)} %fusion.2.a), channel_id=1, source_target_pairs={{0,2},{1,3},{2,0},{3,1},{4,6},{5,7},{6,4},{7,5},{8,10},{9,11},{10,... | collective-permute-start | bytes 36872 | tf_op jit(solution)/shard_map/ppermute | solution.py:351
  58.3 3.8 %collective-permute-start.8 = (f32[4,768]{1,0:T(4,128)S(1)}, f32[4,768]{1,0:T(4,128)S(1)}, u32[]{:S(2)}, u32[]{:S(2)}) collective-permute-start(f32[4,768]{1,0:T(4,128)S(1)} %fusion.2.a), channel_id=1, source_target_pairs={{0,1},{1,2},{2,3},{3,0},{4,5},{5,6},{6,7},{7,4},{8,9},{9,10},{10,1... | collective-permute-start | bytes 36872 | tf_op jit(solution)/shard_map/ppermute | solution.py:351
  58.6 3.4 %collective-permute-start.9 = (f32[4,768]{1,0:T(4,128)S(1)}, f32[4,768]{1,0:T(4,128)S(1)}, u32[]{:S(2)}, u32[]{:S(2)}) collective-permute-start(f32[4,768]{1,0:T(4,128)S(1)} %fusion.2.a), channel_id=1, source_target_pairs={{0,3},{1,0},{2,1},{3,2},{4,7},{5,4},{6,5},{7,6},{8,11},{9,8},{10,9... | collective-permute-start | bytes 36872 | tf_op jit(solution)/shard_map/ppermute | solution.py:351
  62.1 29.5 %collective-permute-start.12 = (bf16[1536,384]{1,0:T(8,128)(2,1)S(1)}, bf16[1536,384]{1,0:T(8,128)(2,1)}, u32[]{:S(2)}, u32[]{:S(2)}) collective-permute-start(bf16[1536,384]{1,0:T(8,128)(2,1)S(1)} %constant_dynamic-update-slice_fusion.4.mine_hbm), channel_id=1, source_target_pairs={{0,4},{4,0},{8,12},{12,8},{16,20},{20,16},{24,28},{28,24},{32,36},... | collective-permute-start | bytes 3538952 | tf_op jit(solution)/shard_map/ppermute | solution.py:355
  68.6 21.2 %all-to-all-start = ((bf16[64,4,640]{2,1,0:T(4,128)(2,1)}), bf16[64,4,640]{2,1,0:T(4,128)(2,1)}, u32[]{:S(2)}, u32[]{:S(2)}) async-start(bf16[64,4,640]{2,1,0:T(4,128)(2,1)} %broadcast_in_dim.10), calls=%async_computation | async-start | bytes 655360 | tf_op jit(solution)/shard_map/all_to_all | solution.py:413
  91.6 1.0 copy-start.3
  92.6 1.0 copy-start.4
  93.5 0.9 copy-start.9
  100.9 4.4 %collective-permute-start.13 = (bf16[128,192]{1,0:T(8,128)(2,1)S(1)}, bf16[128,192]{1,0:T(8,128)(2,1)S(1)}, u32[]{:S(2)}, u32[]{:S(2)}) collective-permute-start(bf16[128,192]{1,0:T(8,128)(2,1)S(1)} %get-tuple-element.42), channel_id=1, source_target_pairs={{0,1},{1,2},{2,3},{3,0},{4,5},{5,6},{6,7},{7,4},{8,9},{9,10},{10,1... | collective-permute-start | bytes 147464 | tf_op jit(solution)/shard_map/ppermute | solution.py:351
  101.4 6.0 %collective-permute-start.14 = (bf16[128,192]{1,0:T(8,128)(2,1)S(1)}, bf16[128,192]{1,0:T(8,128)(2,1)S(1)}, u32[]{:S(2)}, u32[]{:S(2)}) collective-permute-start(bf16[128,192]{1,0:T(8,128)(2,1)S(1)} %get-tuple-element.43), channel_id=1, source_target_pairs={{0,2},{1,3},{2,0},{3,1},{4,6},{5,7},{6,4},{7,5},{8,10},{9,11},{10,... | collective-permute-start | bytes 147464 | tf_op jit(solution)/shard_map/ppermute | solution.py:351
  104.4 3.6 %collective-permute-start.15 = (bf16[128,192]{1,0:T(8,128)(2,1)S(1)}, bf16[128,192]{1,0:T(8,128)(2,1)S(1)}, u32[]{:S(2)}, u32[]{:S(2)}) collective-permute-start(bf16[128,192]{1,0:T(8,128)(2,1)S(1)} %get-tuple-element.44), channel_id=1, source_target_pairs={{0,3},{1,0},{2,1},{3,2},{4,7},{5,4},{6,5},{7,6},{8,11},{9,8},{10,9... | collective-permute-start | bytes 147464 | tf_op jit(solution)/shard_map/ppermute | solution.py:351
  (1 other events, 0.6 us)

commit v5 on v4

--- a/solution.py
+++ b/solution.py
@@ -39,13 +39,18 @@
     return lax.broadcasted_iota(jnp.int32, shape, dim)
 
 
-def encode_kernel(idx, own, left, right, far, gain, weight, out, xn, qk):
+def encode_kernel(idx, own, left, right, far, gain, weight_hbm, out, weight, xn, qk, sems):
     mp = idx[0]
     tokens, width = own.shape[1], own.shape[2]
     unit = HDT ** (-0.5) * math.log2(math.e)
     features = 4 * width
-    blocks = [lax.rem(mp + shift, 4) for shift in (0, 3, 1, 2)]
-    starts = [pl.multiple_of(block * width, 128) for block in blocks]
+    starts = [pl.multiple_of(lax.rem(mp + shift, 4) * width, 128) for shift in (0, 3, 1, 2)]
+    loads = [
+        pltpu.make_async_copy(weight_hbm.at[part], weight.at[part], sems.at[part])
+        for part in range(3)
+    ]
+    for load in loads:
+        load.start()
     for t in range(2):
         parts = [own[t], left[t], right[t], far[t]]
         wide = [part.astype(F32) for part in parts]
@@ -55,17 +60,16 @@
         spread = sum(jnp.sum(part * part, axis=-1, keepdims=True) for part in centred)
         scale = lax.rsqrt(spread * (1.0 / features) + EPSILON)
         for d in range(4):
-            xn[d, t * tokens : (t + 1) * tokens, :] = (
-                centred[d] * scale * gain[pl.ds(blocks[d], 1), 0, :]
+            columns = pl.ds(starts[d], width)
+            xn[t * tokens : (t + 1) * tokens, columns] = (
+                centred[d] * scale * gain[:, columns]
             ).astype(BF)
         out[t : t + 1, width : 2 * width] = jnp.sum(wide[0], axis=0, keepdims=True) * (1.0 / tokens)
     for part in range(2):
-        acc = dot(xn[0], weight[part, pl.ds(starts[0], width), :])
-        for d in range(1, 4):
-            acc = acc + dot(xn[d], weight[part, pl.ds(starts[d], width), :])
-        qk[:, part * width : (part + 1) * width] = acc.astype(BF)
+        loads[part].wait()
+        qk[:, part * width : (part + 1) * width] = dot(xn[...], weight[part]).astype(BF)
     lane = iota((tokens, 2 * HDT), 1)
-    pooled = [[] for _ in range(4)]
+    pooled = []
     for t in range(2):
         low, high = t * tokens, (t + 1) * tokens
         rows = []
@@ -80,14 +84,9 @@
                 rows.append(jnp.sum(e * share, axis=0, keepdims=True))
         rows.append(jnp.zeros((8 - len(rows), tokens), F32))
         mix = jnp.concatenate(rows, axis=0).astype(BF)
-        for d in range(4):
-            pooled[d].append(dot(mix, xn[d, low:high, :]))
-    acc = jnp.zeros((16, width), F32)
-    for d in range(4):
-        acc = acc + dot(
-            jnp.concatenate(pooled[d], axis=0).astype(BF),
-            weight[2, pl.ds(starts[d], width), :],
-        )
+        pooled.append(dot(mix, xn[low:high, :]))
+    loads[2].wait()
+    acc = dot(jnp.concatenate(pooled, axis=0).astype(BF), weight[2])
     keep = (iota((16, width), 0) & 7) == (iota((16, width), 1) >> 6)
     acc = jnp.where(keep, acc, 0.0)
     for t in range(2):
@@ -102,11 +101,13 @@
         encode_kernel,
         grid=(1,),
         out_shape=jax.ShapeDtypeStruct((2, 2 * width), F32),
-        in_specs=[whole(pltpu.SMEM), block, block, block, far_block] + [whole()] * 2,
+        in_specs=[whole(pltpu.SMEM), block, block, block, far_block, whole(), whole(pl.ANY)],
         out_specs=whole(),
         scratch_shapes=[
-            pltpu.VMEM((4, 2 * tokens, width), BF),
+            pltpu.VMEM(weight.shape, BF),
+            pltpu.VMEM((2 * tokens, 4 * width), BF),
             pltpu.VMEM((2 * tokens, 2 * width), BF),
+            pltpu.SemaphoreType.DMA((3,)),
         ],
         compiler_params=params(),
         cost_estimate=pl.CostEstimate(
@@ -217,19 +218,24 @@
 
 
 def attend_kernel(
-    idx, q_cache, mine_hbm, theirs_hbm, emb, out_w, o0, o1, o2, o3, q, mine, theirs, peak, total, acc, sems
+    idx, *refs
 ):
+    sources, (o0, o1, o2, o3), targets = refs[:5], refs[5:9], refs[9:14]
+    q, peak, total, acc, sems = refs[14:]
+    emb, q_cache, mine, theirs, out_w = targets
+    loads = [
+        pltpu.make_async_copy(source, target, sems.at[i])
+        for i, (source, target) in enumerate(zip(sources, targets))
+    ]
+    for load in loads:
+        load.start()
     mp, seq = idx[0], idx[1]
     first_head = mp * 4
     hw = q_cache.shape[1]
     scale = HDL ** (-0.5)
     slots = emb.shape[0]
-    loads = [
-        pltpu.make_async_copy(mine_hbm, mine, sems.at[0]),
-        pltpu.make_async_copy(theirs_hbm, theirs, sems.at[1]),
-    ]
-    for load in loads:
-        load.start()
+    loads[0].wait()
+    loads[1].wait()
     tail = emb[:, 3 * hw :]
     col = iota((8, tail.shape[1]), 1)
     digits = jnp.where(col == 0, 64.0, jnp.where(col == 1, 1.0, 0.0)).astype(BF)
@@ -270,8 +276,8 @@
     total[...] = jnp.broadcast_to(jnp.sum(e, axis=-1, keepdims=True), total.shape)
     acc[...] = dot(e.astype(BF), emb[:, hw : 2 * hw])
 
-    for load in loads:
-        load.wait()
+    loads[2].wait()
+    loads[3].wait()
     for level in range(BRANCHES):
         n = ROWS >> level
         qb = full_q if level == 0 else queries(level)
@@ -322,6 +328,7 @@
         attended = jnp.where(head_mask(ROWS, h), acc[rows, :] / total[rows, 0:1], attended)
     turn = (local_row(iota((ROWS, ROWS), 1), 0, 0) == iota((ROWS, ROWS), 0)).astype(BF)
     attended = dot(turn, attended.astype(BF)).astype(BF)
+    loads[4].wait()
     for d, o in enumerate((o0, o1, o2, o3)):
         o[...] = dot(attended, out_w[lax.rem(mp + d, 4)]).astype(BF)
 
@@ -331,20 +338,19 @@
     return pl.pallas_call(
         attend_kernel,
         out_shape=(jax.ShapeDtypeStruct((ROWS, hw), BF),) * 4,
-        in_specs=[whole(pltpu.SMEM), whole()] + [whole(pl.ANY)] * 2 + [whole()] * 2,
+        in_specs=[whole(pltpu.SMEM)] + [whole(pl.ANY)] * 5,
         out_specs=(whole(),) * 4,
-        scratch_shapes=[
+        scratch_shapes=[pltpu.VMEM(x.shape, x.dtype) for x in (emb, q_cache, mine, theirs, out_w)]
+        + [
             pltpu.VMEM((ROWS, hw), F32),
-            pltpu.VMEM(mine.shape, BF),
-            pltpu.VMEM(mine.shape, BF),
             pltpu.VMEM((4 * ROWS, 128), F32),
             pltpu.VMEM((4 * ROWS, 128), F32),
             pltpu.VMEM((4 * ROWS, hw), F32),
-            pltpu.SemaphoreType.DMA((2,)),
+            pltpu.SemaphoreType.DMA((5,)),
         ],
         compiler_params=params(),
         name="attend",
-    )(idx, q_cache, mine, theirs, emb, out_w)
+    )(idx, emb, q_cache, mine, theirs, out_w)
 
 
 def shift_mp(x, k):
@@ -376,7 +382,7 @@
 
     left, right = shift_mp(tile_batch, 1), shift_mp(tile_batch, 3)
     tile_w = vit_qkv.transpose(1, 0, 2)
-    gain = vit_gain.reshape(4, 1, width)
+    gain = vit_gain.reshape(1, 4 * width)
 
     slide_w = long_qkv.transpose(1, 2, 0).reshape(3 * hw, model)
     gain_row = long_gain.reshape(1, model)
@@ -395,20 +401,18 @@
         kept.append(have[:, 0:n].reshape(-1, 2 * hw))
         return have[:, n:]
 
-    have = step(step(picks[None], 0), 1)
+    have = step(step(step(picks[None], 0), 1), 2)
     far[0], have, joined = lax.optimization_barrier((far[0], have, joined))
     first = encode(idx, 0, tile_batch, left, right, far[0], gain, tile_w)
-    have = step(have, 2)
+    have = step(have, 3)
     far[1], have, first = lax.optimization_barrier((far[1], have, first))
     second = encode(idx, 1, tile_batch, left, right, far[1], gain, tile_w)
-    have = step(have, 3)
-    first, second, have = lax.optimization_barrier((first, second, have))
+    have = step(have, 4)
+    mine = jnp.concatenate(kept + [have.reshape(-1, 2 * hw)], axis=0)
+    first, second, mine = lax.optimization_barrier((first, second, mine))
+    theirs = swap_seq(mine, 1)
     partial = dot(jnp.concatenate([first, second], axis=0).astype(BF), joined)
     shares = [partial] + [shift_mp(partial, k) for k in (1, 3, 2)]
-    have = step(have, 4)
-    mine = jnp.concatenate(kept + [have.reshape(-1, 2 * hw)], axis=0)
-    shares, mine = lax.optimization_barrier((shares, mine))
-    theirs = swap_seq(mine, 1)
     emb = embed_rows(idx, shares, gain_row, slide_w)
     emb = lax.all_to_all(jnp.broadcast_to(emb[None], (64,) + emb.shape), "seq", 0, 0)
     emb = emb.reshape(64 * slots, emb.shape[2])

time: 110 us -> 113 us (1.027)
  waiting for transfers between devices: 18.4 us -> 32.2 us
  starting transfers between devices: 42.7 us -> 37.6 us
  local copies, waits for them, and re-layouts: 18.9 us -> 15.7 us
  other arithmetic: 3.82 us -> 1.03 us
  Pallas kernels: 20.6 us -> 22.2 us
    ppermute x6, waiting for transfers between devices: 4.56 us -> 15.6 us  [swap_seq(): return lax.ppermute(x, 'seq', [(i, i ^ bit) for i in range(64)])]
    ppermute x10, starting transfers between devices: 12.9 us -> 10 us  [shift_mp(): return lax.ppermute(x, 'mp', [(i, (i + k) % 4) for i in range(4)])]
    ppermute x6, starting transfers between devices: 21.8 us -> 18.9 us  [swap_seq(): return lax.ppermute(x, 'seq', [(i, i ^ bit) for i in range(64)])]
    ppermute x10, waiting for transfers between devices: 4.54 us -> 7.23 us  [shift_mp(): return lax.ppermute(x, 'mp', [(i, (i + k) % 4) for i in range(4)])]
    unnamed x38 -> x31, local copies, waits for them, and re-layouts: 8.84 us -> 6.54 us
    pallas_call x2, Pallas kernels: 11.8 us -> 13.8 us  [encode(): pl.pallas_call(encode_kernel, grid=(1,), out_shape=jax.ShapeDtypeStruct((...]
    concatenate x3 -> x4, other arithmetic: 1.92 us -> 0.17 us  [step(): have = jnp.concatenate([have, swap_seq(have, 2 << level)], axis=0)]
  transfers between devices with their start and end apart: 17 -> 17, of which waited for: 8 -> 8; matrix products, arithmetic and copies ran while one was open for 16% -> 11% of each run, Pallas kernels for 13% -> 14%
where the time goes in v5:
time: 113 us; the launch traced here: 112 us
  starting transfers between devices  37.6 us (33%)
  waiting for transfers between devices  32.2 us (28%)
  Pallas kernels  22.2 us (20%)
  local copies, waits for them, and re-layouts  15.7 us (14%)
  matrix products  2.61 us (2%)
    ppermute x6, starting transfers between devices, swap_seq(): return lax.ppermute(x, 'seq', [(i, i ^ bit) for i in range(64)])  18.9 us
    ppermute x6, waiting for transfers between devices, swap_seq(): return lax.ppermute(x, 'seq', [(i, i ^ bit) for i in range(64)])  15.6 us
    pallas_call x2, Pallas kernels, encode(): pl.pallas_call(encode_kernel, grid=(1,), out_shape=jax.ShapeDtypeStruct((...  13.8 us
    ppermute x10, starting transfers between devices, shift_mp(): return lax.ppermute(x, 'mp', [(i, (i + k) % 4) for i in range(4)])  10 us
    all_to_all x1, waiting for transfers between devices, local(): lax.all_to_all(jnp.broadcast_to(emb[None], (64,) + emb.shape), 'seq', 0, 0)  9.32 us
    all_to_all x1, starting transfers between devices, local(): lax.all_to_all(jnp.broadcast_to(emb[None], (64,) + emb.shape), 'seq', 0, 0)  8.68 us
    ppermute x10, waiting for transfers between devices, shift_mp(): return lax.ppermute(x, 'mp', [(i, (i + k) % 4) for i in range(4)])  7.23 us
    unnamed x31, local copies, waits for them, and re-layouts  6.54 us
  transfers between devices with their start and end apart: 17, of which 8 were waited for; matrix products, arithmetic and copies ran while one was open for 11% of the time, Pallas kernels for 14%

profile of v5, /device:TPU:1, one launch (start us, length us, event | category | flops | bytes accessed | tf_op | source)
XLA Modules:
  0.0 112.3 jit_solution(14339465799879704393)
XLA Ops:
  0.0 2.0 %collective-permute-start.2 = (bf16[4,256,384]{2,1,0:T(8,128)(2,1)}, bf16[4,256,384]{2,1,0:T(8,128)(2,1)S(1)}, u32[]{:S(2)}, u32[]{:S(2)}) collective-permute-start(bf16[4,256,384]{2,1,0:T(8,128)(2,1)} %own.3), channel_id=1, source_target_pairs={{0,1},{1,2},{2,3},{3,0},{4,5},{5,6},{6,7},{7,4},{8,9},{9,10},{10,1... | collective-permute-start | bytes 2359304 | tf_op jit(solution)/shard_map/ppermute | solution.py:357
  2.0 1.4 %collective-permute-start = (bf16[4,256,384]{2,1,0:T(8,128)(2,1)}, bf16[4,256,384]{2,1,0:T(8,128)(2,1)}, u32[]{:S(2)}, u32[]{:S(2)}) collective-permute-start(bf16[4,256,384]{2,1,0:T(8,128)(2,1)} %own.3), channel_id=1, source_target_pairs={{0,3},{1,0},{2,1},{3,2},{4,7},{5,4},{6,5},{7,6},{8,11},{9,8},{10,9... | collective-permute-start | bytes 2359304 | tf_op jit(solution)/shard_map/ppermute | solution.py:357
  5.5 1.2 %copy-done.1 = bf16[768,3,192]{0,2,1:T(8,128)(2,1)S(1)} copy-done((bf16[768,3,192]{0,2,1:T(8,128)(2,1)S(1)}, bf16[768,3,192]{0,2,1:T(8,128)(2,1)}, u32[]{:S(2)}) %copy-start.1) | copy-done | bytes 884760
  7.6 1.3 %slide_project.1 = (f32[128,192]{1,0:T(8,128)S(1)}, bf16[256,384]{1,0:T(8,128)(2,1)S(1)}) custom-call(s32[7]{0:T(128)S(1)} %pad_add_fusion.idx, bf16[128,768]{1,0:T(8,128)(2,1)S(1)} %copy-done.5, f32[1,768]{1,0:T(1,128)S(1)} %reshape.31.gain, bf16[576,768]{1,0:T(8,128)(2,1)S(1)} %bitcast.18), custom_call_target="tpu_custom_call" | custom-call | tf_op jit(solution)/shard_map/slide_project/pallas_call | solution.py:202
  9.6 1.8 %collective-permute-start.4 = (bf16[1,256,384]{2,1,0:T(8,128)(2,1)S(1)}, bf16[1,256,384]{2,1,0:T(8,128)(2,1)S(1)}, u32[]{:S(2)}, u32[]{:S(2)}) collective-permute-start(bf16[1,256,384]{2,1,0:T(8,128)(2,1)S(1)} %bitcast.21), channel_id=1, source_target_pairs={{0,8},{4,12},{8,0},{12,4},{16,24},{20,28},{24,16},{28,20},{32,40},... | collective-permute-start | bytes 589832 | tf_op jit(solution)/shard_map/ppermute | solution.py:361
  11.3 2.3 %convolution_convert_fusion = bf16[384,768]{1,0:T(8,128)(2,1)S(1)} fusion(bf16[384,1536]{1,0:T(8,128)(2,1)} %param.16, bf16[1536,768]{1,0:T(8,128)(2,1)S(1)} %copy-done), kind=kOutput, calls=%fused_computation | convolution fusion | flops 906264576 | bytes 4128768 | tf_op jit(solution)/shard_map/dot_general | solution.py:31
  13.7 1.1 collective-permute-done.4
  14.8 3.6 %collective-permute-start.5 = (bf16[2,128,384]{2,1,0:T(8,128)(2,1)S(1)}, bf16[2,128,384]{2,1,0:T(8,128)(2,1)S(1)}, u32[]{:S(2)}, u32[]{:S(2)}) collective-permute-start(bf16[2,128,384]{2,1,0:T(8,128)(2,1)S(1)} %get-tuple-element.42), channel_id=1, source_target_pairs={{0,16},{4,20},{8,24},{12,28},{16,0},{20,4},{24,8},{28,12},{32,48},... | collective-permute-start | bytes 589832 | tf_op jit(solution)/shard_map/ppermute | solution.py:361
  18.6 8.3 %collective-permute-done.5 = bf16[2,128,384]{2,1,0:T(8,128)(2,1)S(1)} collective-permute-done((bf16[2,128,384]{2,1,0:T(8,128)(2,1)S(1)}, bf16[2,128,384]{2,1,0:T(8,128)(2,1)S(1)}, u32[]{:S(2)}, u32[]{:S(2)}) %collective-permute-start.5) | collective-permute-done | bytes 196640 | tf_op jit(solution)/shard_map/ppermute | solution.py:361
  27.0 6.6 %collective-permute-start.6 = (bf16[4,64,384]{2,1,0:T(8,128)(2,1)S(1)}, bf16[4,64,384]{2,1,0:T(8,128)(2,1)S(1)}, u32[]{:S(2)}, u32[]{:S(2)}) collective-permute-start(bf16[4,64,384]{2,1,0:T(8,128)(2,1)S(1)} %get-tuple-element.40), channel_id=1, source_target_pairs={{0,32},{4,36},{8,40},{12,44},{16,48},{20,52},{24,56},{28,60},{32,0... | collective-permute-start | bytes 589832 | tf_op jit(solution)/shard_map/ppermute | solution.py:361
  34.5 6.2 %collective-permute-done.6 = bf16[4,64,384]{2,1,0:T(8,128)(2,1)S(1)} collective-permute-done((bf16[4,64,384]{2,1,0:T(8,128)(2,1)S(1)}, bf16[4,64,384]{2,1,0:T(8,128)(2,1)S(1)}, u32[]{:S(2)}, u32[]{:S(2)}) %collective-permute-start.6) | collective-permute-done | bytes 196640 | tf_op jit(solution)/shard_map/ppermute | solution.py:361
  40.8 1.0 slice.40
  41.8 1.4 %collective-permute-start.1 = (bf16[2,256,384]{2,1,0:T(8,128)(2,1)S(1)}, bf16[2,256,384]{2,1,0:T(8,128)(2,1)S(1)}, u32[]{:S(2)}, u32[]{:S(2)}) collective-permute-start(bf16[2,256,384]{2,1,0:T(8,128)(2,1)S(1)} %slice.40), channel_id=1, source_target_pairs={{0,3},{1,0},{2,1},{3,2},{4,7},{5,4},{6,5},{7,6},{8,11},{9,8},{10,9... | collective-permute-start | bytes 1179656 | tf_op jit(solution)/shard_map/ppermute | solution.py:357
  44.2 1.3 %collective-permute-start.7 = (bf16[8,32,384]{2,1,0:T(8,128)(2,1)S(1)}, bf16[8,32,384]{2,1,0:T(8,128)(2,1)S(1)}, u32[]{:S(2)}, u32[]{:S(2)}) collective-permute-start(bf16[8,32,384]{2,1,0:T(8,128)(2,1)S(1)} %get-tuple-element.21), channel_id=1, source_target_pairs={{0,64},{4,68},{8,72},{12,76},{16,80},{20,84},{24,88},{28,92},{32,9... | collective-permute-start | bytes 589832 | tf_op jit(solution)/shard_map/ppermute | solution.py:361
  45.5 6.9 %encode.2 = f32[2,768]{1,0:T(2,128)S(1)} custom-call(s32[7]{0:T(128)S(1)} %pad_add_fusion.idx, bf16[4,256,384]{2,1,0:T(8,128)(2,1)S(1)} %copy-done.11, bf16[4,256,384]{2,1,0:T(8,128)(2,1)S(1)} %copy-done.7, bf16[4,256,384]{2,1,0:T(8,128)(2,1)} %collective-permute-done.right, bf16[2,256,384]{2,1,0:T(8,128)(2,1)S(1)} %collective-permute-done.3.far, ...), custom_call_target="tpu_custom_call" | custom-call | flops 6000000000 | bytes 8000000 | tf_op jit(solution)/shard_map/encode/pallas_call | solution.py:100
  52.5 2.9 %collective-permute-start.8 = (bf16[16,16,384]{2,1,0:T(8,128)(2,1)S(1)}, bf16[16,16,384]{2,1,0:T(8,128)(2,1)S(1)}, u32[]{:S(2)}, u32[]{:S(2)}) collective-permute-start(bf16[16,16,384]{2,1,0:T(8,128)(2,1)S(1)} %get-tuple-element.25), channel_id=1, source_target_pairs={{0,128},{4,132},{8,136},{12,140},{16,144},{20,148},{24,152},{28,15... | collective-permute-start | bytes 589832 | tf_op jit(solution)/shard_map/ppermute | solution.py:361
  55.4 6.9 %encode.3 = f32[2,768]{1,0:T(2,128)S(1)} custom-call(s32[7]{0:T(128)S(1)} %pad_add_fusion.idx, bf16[4,256,384]{2,1,0:T(8,128)(2,1)S(1)} %copy-done.11, bf16[4,256,384]{2,1,0:T(8,128)(2,1)S(1)} %copy-done.7, bf16[4,256,384]{2,1,0:T(8,128)(2,1)} %collective-permute-done.right, bf16[2,256,384]{2,1,0:T(8,128)(2,1)S(1)} %collective-permute-done.1.far, ...), custom_call_target="tpu_custom_call" | custom-call | flops 6000000000 | bytes 8000000 | tf_op jit(solution)/shard_map/encode/pallas_call | solution.py:100
  62.5 2.9 %collective-permute-start.12 = (bf16[1536,384]{1,0:T(8,128)(2,1)S(1)}, bf16[1536,384]{1,0:T(8,128)(2,1)}, u32[]{:S(2)}, u32[]{:S(2)}) collective-permute-start(bf16[1536,384]{1,0:T(8,128)(2,1)S(1)} %constant_dynamic-update-slice_fusion.2.refs_2_), channel_id=1, source_target_pairs={{0,4},{4,0},{8,12},{12,8},{16,20},{20,16},{24,28},{28,24},{32,36},... | collective-permute-start | bytes 3538952 | tf_op jit(solution)/shard_map/ppermute | solution.py:361
  66.0 1.0 collective-permute-start.10
  67.5 2.3 %collective-permute-done.11.d = f32[4,768]{1,0:T(4,128)S(1)} collective-permute-done((f32[4,768]{1,0:T(4,128)S(1)}, f32[4,768]{1,0:T(4,128)S(1)}, u32[]{:S(2)}, u32[]{:S(2)}) %collective-permute-start.11) | collective-permute-done | bytes 12320 | tf_op jit(solution)/shard_map/ppermute | solution.py:357
  69.7 1.0 collective-permute-done.9.b
  70.8 1.0 embed_rows.1
  72.6 8.7 %all-to-all-start = ((bf16[64,4,640]{2,1,0:T(4,128)(2,1)}), bf16[64,4,640]{2,1,0:T(4,128)(2,1)}, u32[]{:S(2)}, u32[]{:S(2)}) async-start(bf16[64,4,640]{2,1,0:T(4,128)(2,1)} %broadcast_in_dim.10), calls=%async_computation | async-start | bytes 655360 | tf_op jit(solution)/shard_map/all_to_all | solution.py:417
  81.3 2.1 %reshape.40 = bf16[192,4,192]{2,1,0:T(4,128)(2,1)} reshape(bf16[192,768]{1,0:T(8,128)(2,1)} %param.21) | data formatting | bytes 589824 | tf_op jit(solution)/shard_map/reshape | solution.py:420
  83.4 1.8 %copy.16 = bf16[192,4,192]{2,0,1:T(8,128)(2,1)} copy(bf16[192,4,192]{2,1,0:T(4,128)(2,1)} %reshape.40) | data formatting | bytes 589824 | tf_op jit(solution)/shard_map/reshape | solution.py:420
  85.2 9.3 %all-to-all-done = bf16[64,4,640]{2,1,0:T(4,128)(2,1)} async-done(((bf16[64,4,640]{2,1,0:T(4,128)(2,1)}), bf16[64,4,640]{2,1,0:T(4,128)(2,1)}, u32[]{:S(2)}, u32[]{:S(2)}) %all-to-all-start) | async-done | bytes 327712 | tf_op jit(solution)/shard_map/all_to_all | solution.py:417
  94.5 1.8 %reshape.39.refs_0_ = bf16[256,640]{1,0:T(8,128)(2,1)} reshape(bf16[64,4,640]{2,1,0:T(4,128)(2,1)} %all-to-all-done) | data formatting | bytes 655360 | tf_op jit(solution)/shard_map/reshape | solution.py:418
  96.3 1.0 copy-done.3
  99.2 6.0 %attend.1 = (bf16[128,192]{1,0:T(8,128)(2,1)S(1)}, bf16[128,192]{1,0:T(8,128)(2,1)S(1)}, bf16[128,192]{1,0:T(8,128)(2,1)S(1)}, bf16[128,192]{1,0:T(8,128)(2,1)S(1)}) custom-call(s32[7]{0:T(128)S(1)} %pad_add_fusion.idx, bf16[256,640]{1,0:T(8,128)(2,1)S(1)} %copy-done.4, f32[128,192]{1,0:T(8,128)S(1)} %copy-done.9, ...), custom_call_target="tpu_custom_call" | custom-call | tf_op jit(solution)/shard_map/attend/pallas_call | solution.py:338
  105.3 1.3 %collective-permute-start.14 = (bf16[128,192]{1,0:T(8,128)(2,1)S(1)}, bf16[128,192]{1,0:T(8,128)(2,1)S(1)}, u32[]{:S(2)}, u32[]{:S(2)}) collective-permute-start(bf16[128,192]{1,0:T(8,128)(2,1)S(1)} %get-tuple-element.33), channel_id=1, source_target_pairs={{0,2},{1,3},{2,0},{3,1},{4,6},{5,7},{6,4},{7,5},{8,10},{9,11},{10,... | collective-permute-start | bytes 147464 | tf_op jit(solution)/shard_map/ppermute | solution.py:357
  106.6 2.0 %collective-permute-start.15 = (bf16[128,192]{1,0:T(8,128)(2,1)S(1)}, bf16[128,192]{1,0:T(8,128)(2,1)S(1)}, u32[]{:S(2)}, u32[]{:S(2)}) collective-permute-start(bf16[128,192]{1,0:T(8,128)(2,1)S(1)} %get-tuple-element.34), channel_id=1, source_target_pairs={{0,3},{1,0},{2,1},{3,2},{4,7},{5,4},{6,5},{7,6},{8,11},{9,8},{10,9... | collective-permute-start | bytes 147464 | tf_op jit(solution)/shard_map/ppermute | solution.py:357
  108.6 3.0 %collective-permute-done.13 = bf16[128,192]{1,0:T(8,128)(2,1)S(1)} collective-permute-done((bf16[128,192]{1,0:T(8,128)(2,1)S(1)}, bf16[128,192]{1,0:T(8,128)(2,1)S(1)}, u32[]{:S(2)}, u32[]{:S(2)}) %collective-permute-start.13) | collective-permute-done | bytes 49184 | tf_op jit(solution)/shard_map/ppermute | solution.py:357
  (62 shorter events, 10.2 us)
Async XLA Ops:
  0.0 11.3 %copy-start = (bf16[1536,768]{1,0:T(8,128)(2,1)S(1)}, bf16[1536,768]{1,0:T(8,128)(2,1)}, u32[]{:S(2)}) copy-start(bf16[1536,768]{1,0:T(8,128)(2,1)} %param.17) | copy-start | bytes 7077892
  0.0 33.5 %collective-permute-start.2 = (bf16[4,256,384]{2,1,0:T(8,128)(2,1)}, bf16[4,256,384]{2,1,0:T(8,128)(2,1)S(1)}, u32[]{:S(2)}, u32[]{:S(2)}) collective-permute-start(bf16[4,256,384]{2,1,0:T(8,128)(2,1)} %own.3), channel_id=1, source_target_pairs={{0,1},{1,2},{2,3},{3,0},{4,5},{5,6},{6,7},{7,4},{8,9},{9,10},{10,1... | collective-permute-start | bytes 2359304 | tf_op jit(solution)/shard_map/ppermute | solution.py:357
  2.0 38.7 %collective-permute-start = (bf16[4,256,384]{2,1,0:T(8,128)(2,1)}, bf16[4,256,384]{2,1,0:T(8,128)(2,1)}, u32[]{:S(2)}, u32[]{:S(2)}) collective-permute-start(bf16[4,256,384]{2,1,0:T(8,128)(2,1)} %own.3), channel_id=1, source_target_pairs={{0,3},{1,0},{2,1},{3,2},{4,7},{5,4},{6,5},{7,6},{8,11},{9,8},{10,9... | collective-permute-start | bytes 2359304 | tf_op jit(solution)/shard_map/ppermute | solution.py:357
  5.5 1.2 %copy-start.1 = (bf16[768,3,192]{0,2,1:T(8,128)(2,1)S(1)}, bf16[768,3,192]{0,2,1:T(8,128)(2,1)}, u32[]{:S(2)}) copy-start(bf16[768,3,192]{0,2,1:T(8,128)(2,1)} %param.20) | copy-start | bytes 2654212
  6.6 0.9 copy-start.5
  8.9 0.7 copy-start.8
  9.6 5.2 %collective-permute-start.4 = (bf16[1,256,384]{2,1,0:T(8,128)(2,1)S(1)}, bf16[1,256,384]{2,1,0:T(8,128)(2,1)S(1)}, u32[]{:S(2)}, u32[]{:S(2)}) collective-permute-start(bf16[1,256,384]{2,1,0:T(8,128)(2,1)S(1)} %bitcast.21), channel_id=1, source_target_pairs={{0,8},{4,12},{8,0},{12,4},{16,24},{20,28},{24,16},{28,20},{32,40},... | collective-permute-start | bytes 589832 | tf_op jit(solution)/shard_map/ppermute | solution.py:361
  13.7 4.8 %copy-start.12 = (f32[1536]{0:T(1024)S(1)}, f32[1536]{0:T(1024)}, u32[]{:S(2)}) copy-start(f32[1536]{0:T(1024)} %param.14) | copy-start | bytes 18436
  14.8 12.1 %collective-permute-start.5 = (bf16[2,128,384]{2,1,0:T(8,128)(2,1)S(1)}, bf16[2,128,384]{2,1,0:T(8,128)(2,1)S(1)}, u32[]{:S(2)}, u32[]{:S(2)}) collective-permute-start(bf16[2,128,384]{2,1,0:T(8,128)(2,1)S(1)} %get-tuple-element.42), channel_id=1, source_target_pairs={{0,16},{4,20},{8,24},{12,28},{16,0},{20,4},{24,8},{28,12},{32,48},... | collective-permute-start | bytes 589832 | tf_op jit(solution)/shard_map/ppermute | solution.py:361
  18.5 27.0 %copy-start.11 = (bf16[4,256,384]{2,1,0:T(8,128)(2,1)S(1)}, bf16[4,256,384]{2,1,0:T(8,128)(2,1)}, u32[]{:S(2)}) copy-start(bf16[4,256,384]{2,1,0:T(8,128)(2,1)} %own.3) | copy-start | bytes 2359300
  26.9 18.6 %copy-start.10 = (bf16[1536,3,384]{2,0,1:T(8,128)(2,1)S(1)}, bf16[1536,3,384]{2,0,1:T(8,128)(2,1)}, u32[]{:S(2)}) copy-start(bf16[1536,3,384]{2,0,1:T(8,128)(2,1)} %param.15) | copy-start | bytes 10616836
  27.0 13.7 %collective-permute-start.6 = (bf16[4,64,384]{2,1,0:T(8,128)(2,1)S(1)}, bf16[4,64,384]{2,1,0:T(8,128)(2,1)S(1)}, u32[]{:S(2)}, u32[]{:S(2)}) collective-permute-start(bf16[4,64,384]{2,1,0:T(8,128)(2,1)S(1)} %get-tuple-element.40), channel_id=1, source_target_pairs={{0,32},{4,36},{8,40},{12,44},{16,48},{20,52},{24,56},{28,60},{32,0... | collective-permute-start | bytes 589832 | tf_op jit(solution)/shard_map/ppermute | solution.py:361
  33.5 0.9 copy-start.6
  33.6 10.6 %collective-permute-start.3 = (bf16[2,256,384]{2,1,0:T(8,128)(2,1)S(1)}, bf16[2,256,384]{2,1,0:T(8,128)(2,1)S(1)}, u32[]{:S(2)}, u32[]{:S(2)}) collective-permute-start(bf16[2,256,384]{2,1,0:T(8,128)(2,1)S(1)} %slice.41), channel_id=1, source_target_pairs={{0,1},{1,2},{2,3},{3,0},{4,5},{5,6},{6,7},{7,4},{8,9},{9,10},{10,1... | collective-permute-start | bytes 1179656 | tf_op jit(solution)/shard_map/ppermute | solution.py:357
  34.4 11.0 %copy-start.7 = (bf16[4,256,384]{2,1,0:T(8,128)(2,1)S(1)}, bf16[4,256,384]{2,1,0:T(8,128)(2,1)}, u32[]{:S(2)}) copy-start(bf16[4,256,384]{2,1,0:T(8,128)(2,1)} %copy-done.6) | copy-start | bytes 2359300
  41.8 10.7 %collective-permute-start.1 = (bf16[2,256,384]{2,1,0:T(8,128)(2,1)S(1)}, bf16[2,256,384]{2,1,0:T(8,128)(2,1)S(1)}, u32[]{:S(2)}, u32[]{:S(2)}) collective-permute-start(bf16[2,256,384]{2,1,0:T(8,128)(2,1)S(1)} %slice.40), channel_id=1, source_target_pairs={{0,3},{1,0},{2,1},{3,2},{4,7},{5,4},{6,5},{7,6},{8,11},{9,8},{10,9... | collective-permute-start | bytes 1179656 | tf_op jit(solution)/shard_map/ppermute | solution.py:357
  44.2 8.3 %collective-permute-start.7 = (bf16[8,32,384]{2,1,0:T(8,128)(2,1)S(1)}, bf16[8,32,384]{2,1,0:T(8,128)(2,1)S(1)}, u32[]{:S(2)}, u32[]{:S(2)}) collective-permute-start(bf16[8,32,384]{2,1,0:T(8,128)(2,1)S(1)} %get-tuple-element.21), channel_id=1, source_target_pairs={{0,64},{4,68},{8,72},{12,76},{16,80},{20,84},{24,88},{28,92},{32,9... | collective-permute-start | bytes 589832 | tf_op jit(solution)/shard_map/ppermute | solution.py:361
  52.5 9.8 %collective-permute-start.8 = (bf16[16,16,384]{2,1,0:T(8,128)(2,1)S(1)}, bf16[16,16,384]{2,1,0:T(8,128)(2,1)S(1)}, u32[]{:S(2)}, u32[]{:S(2)}) collective-permute-start(bf16[16,16,384]{2,1,0:T(8,128)(2,1)S(1)} %get-tuple-element.25), channel_id=1, source_target_pairs={{0,128},{4,132},{8,136},{12,140},{16,144},{20,148},{24,152},{28,15... | collective-permute-start | bytes 589832 | tf_op jit(solution)/shard_map/ppermute | solution.py:361
  62.4 8.3 %copy-start.2 = (bf16[768,3,192]{0,2,1:T(8,128)(2,1)S(1)}, bf16[768,3,192]{0,2,1:T(8,128)(2,1)}, u32[]{:S(2)}) copy-start(bf16[768,3,192]{0,2,1:T(8,128)(2,1)} %param.20) | copy-start | bytes 2654212
  62.5 33.8 %collective-permute-start.12 = (bf16[1536,384]{1,0:T(8,128)(2,1)S(1)}, bf16[1536,384]{1,0:T(8,128)(2,1)}, u32[]{:S(2)}, u32[]{:S(2)}) collective-permute-start(bf16[1536,384]{1,0:T(8,128)(2,1)S(1)} %constant_dynamic-update-slice_fusion.2.refs_2_), channel_id=1, source_target_pairs={{0,4},{4,0},{8,12},{12,8},{16,20},{20,16},{24,28},{28,24},{32,36},... | collective-permute-start | bytes 3538952 | tf_op jit(solution)/shard_map/ppermute | solution.py:361
  65.7 4.1 %collective-permute-start.11 = (f32[4,768]{1,0:T(4,128)S(1)}, f32[4,768]{1,0:T(4,128)S(1)}, u32[]{:S(2)}, u32[]{:S(2)}) collective-permute-start(f32[4,768]{1,0:T(4,128)S(1)} %fusion.3.a), channel_id=1, source_target_pairs={{0,2},{1,3},{2,0},{3,1},{4,6},{5,7},{6,4},{7,5},{8,10},{9,11},{10,... | collective-permute-start | bytes 36872 | tf_op jit(solution)/shard_map/ppermute | solution.py:357
  66.0 3.7 %collective-permute-start.10 = (f32[4,768]{1,0:T(4,128)S(1)}, f32[4,768]{1,0:T(4,128)S(1)}, u32[]{:S(2)}, u32[]{:S(2)}) collective-permute-start(f32[4,768]{1,0:T(4,128)S(1)} %fusion.3.a), channel_id=1, source_target_pairs={{0,3},{1,0},{2,1},{3,2},{4,7},{5,4},{6,5},{7,6},{8,11},{9,8},{10,9... | collective-permute-start | bytes 36872 | tf_op jit(solution)/shard_map/ppermute | solution.py:357
  67.0 3.8 %collective-permute-start.9 = (f32[4,768]{1,0:T(4,128)S(1)}, f32[4,768]{1,0:T(4,128)S(1)}, u32[]{:S(2)}, u32[]{:S(2)}) collective-permute-start(f32[4,768]{1,0:T(4,128)S(1)} %fusion.3.a), channel_id=1, source_target_pairs={{0,1},{1,2},{2,3},{3,0},{4,5},{5,6},{6,7},{7,4},{8,9},{9,10},{10,1... | collective-permute-start | bytes 36872 | tf_op jit(solution)/shard_map/ppermute | solution.py:357
  72.6 21.9 %all-to-all-start = ((bf16[64,4,640]{2,1,0:T(4,128)(2,1)}), bf16[64,4,640]{2,1,0:T(4,128)(2,1)}, u32[]{:S(2)}, u32[]{:S(2)}) async-start(bf16[64,4,640]{2,1,0:T(4,128)(2,1)} %broadcast_in_dim.10), calls=%async_computation | async-start | bytes 655360 | tf_op jit(solution)/shard_map/all_to_all | solution.py:417
  96.3 1.0 copy-start.3
  97.3 1.0 copy-start.4
  98.2 0.9 copy-start.9
  105.2 6.3 %collective-permute-start.13 = (bf16[128,192]{1,0:T(8,128)(2,1)S(1)}, bf16[128,192]{1,0:T(8,128)(2,1)S(1)}, u32[]{:S(2)}, u32[]{:S(2)}) collective-permute-start(bf16[128,192]{1,0:T(8,128)(2,1)S(1)} %get-tuple-element.32), channel_id=1, source_target_pairs={{0,1},{1,2},{2,3},{3,0},{4,5},{5,6},{6,7},{7,4},{8,9},{9,10},{10,1... | collective-permute-start | bytes 147464 | tf_op jit(solution)/shard_map/ppermute | solution.py:357
  105.3 6.2 %collective-permute-start.14 = (bf16[128,192]{1,0:T(8,128)(2,1)S(1)}, bf16[128,192]{1,0:T(8,128)(2,1)S(1)}, u32[]{:S(2)}, u32[]{:S(2)}) collective-permute-start(bf16[128,192]{1,0:T(8,128)(2,1)S(1)} %get-tuple-element.33), channel_id=1, source_target_pairs={{0,2},{1,3},{2,0},{3,1},{4,6},{5,7},{6,4},{7,5},{8,10},{9,11},{10,... | collective-permute-start | bytes 147464 | tf_op jit(solution)/shard_map/ppermute | solution.py:357
  106.6 4.9 %collective-permute-start.15 = (bf16[128,192]{1,0:T(8,128)(2,1)S(1)}, bf16[128,192]{1,0:T(8,128)(2,1)S(1)}, u32[]{:S(2)}, u32[]{:S(2)}) collective-permute-start(bf16[128,192]{1,0:T(8,128)(2,1)S(1)} %get-tuple-element.34), channel_id=1, source_target_pairs={{0,3},{1,0},{2,1},{3,2},{4,7},{5,4},{6,5},{7,6},{8,11},{9,8},{10,9... | collective-permute-start | bytes 147464 | tf_op jit(solution)/shard_map/ppermute | solution.py:357

commit v6 on v5

--- a/solution.py
+++ b/solution.py
@@ -39,18 +39,12 @@
     return lax.broadcasted_iota(jnp.int32, shape, dim)
 
 
-def encode_kernel(idx, own, left, right, far, gain, weight_hbm, out, weight, xn, qk, sems):
+def encode_kernel(idx, own, left, right, far, gain, weight, out, xn, qk):
     mp = idx[0]
     tokens, width = own.shape[1], own.shape[2]
     unit = HDT ** (-0.5) * math.log2(math.e)
     features = 4 * width
     starts = [pl.multiple_of(lax.rem(mp + shift, 4) * width, 128) for shift in (0, 3, 1, 2)]
-    loads = [
-        pltpu.make_async_copy(weight_hbm.at[part], weight.at[part], sems.at[part])
-        for part in range(3)
-    ]
-    for load in loads:
-        load.start()
     for t in range(2):
         parts = [own[t], left[t], right[t], far[t]]
         wide = [part.astype(F32) for part in parts]
@@ -66,7 +60,6 @@
             ).astype(BF)
         out[t : t + 1, width : 2 * width] = jnp.sum(wide[0], axis=0, keepdims=True) * (1.0 / tokens)
     for part in range(2):
-        loads[part].wait()
         qk[:, part * width : (part + 1) * width] = dot(xn[...], weight[part]).astype(BF)
     lane = iota((tokens, 2 * HDT), 1)
     pooled = []
@@ -85,7 +78,6 @@
         rows.append(jnp.zeros((8 - len(rows), tokens), F32))
         mix = jnp.concatenate(rows, axis=0).astype(BF)
         pooled.append(dot(mix, xn[low:high, :]))
-    loads[2].wait()
     acc = dot(jnp.concatenate(pooled, axis=0).astype(BF), weight[2])
     keep = (iota((16, width), 0) & 7) == (iota((16, width), 1) >> 6)
     acc = jnp.where(keep, acc, 0.0)
@@ -101,15 +93,13 @@
         encode_kernel,
         grid=(1,),
         out_shape=jax.ShapeDtypeStruct((2, 2 * width), F32),
-        in_specs=[whole(pltpu.SMEM), block, block, block, far_block, whole(), whole(pl.ANY)],
+        in_specs=[whole(pltpu.SMEM), block, block, block, far_block, whole(), whole()],
         out_specs=whole(),
         scratch_shapes=[
-            pltpu.VMEM(weight.shape, BF),
             pltpu.VMEM((2 * tokens, 4 * width), BF),
             pltpu.VMEM((2 * tokens, 2 * width), BF),
-            pltpu.SemaphoreType.DMA((3,)),
         ],
-        compiler_params=params(),
+        compiler_params=params(20),
         cost_estimate=pl.CostEstimate(
             flops=6 * 10**9, bytes_accessed=8 * 10**6, transcendentals=8 * 10**5
         ),
@@ -153,7 +143,7 @@
         out_shape=jax.ShapeDtypeStruct((rows, width + 64), BF),
         in_specs=[whole(pltpu.SMEM)] + [whole()] * 6,
         out_specs=whole(),
-        compiler_params=params(),
+        compiler_params=params(20),
         name="embed_rows",
     )(idx, *parts, gain, weight)
 
@@ -208,7 +198,7 @@
         in_specs=[whole(pltpu.SMEM)] + [whole()] * 3,
         out_specs=(whole(),) * 2,
         scratch_shapes=[pltpu.VMEM((ROWS, 2 * hw), F32)],
-        compiler_params=params(),
+        compiler_params=params(20),
         name="slide_project",
     )(idx, cache, gain, weight)
 
@@ -338,7 +328,7 @@
     return pl.pallas_call(
         attend_kernel,
         out_shape=(jax.ShapeDtypeStruct((ROWS, hw), BF),) * 4,
-        in_specs=[whole(pltpu.SMEM)] + [whole(pl.ANY)] * 5,
+        in_specs=[whole(pltpu.SMEM)] + [whole(pltpu.HBM)] * 5,
         out_specs=(whole(),) * 4,
         scratch_shapes=[pltpu.VMEM(x.shape, x.dtype) for x in (emb, q_cache, mine, theirs, out_w)]
         + [
@@ -348,7 +338,7 @@
             pltpu.VMEM((4 * ROWS, hw), F32),
             pltpu.SemaphoreType.DMA((5,)),
         ],
-        compiler_params=params(),
+        compiler_params=params(20),
         name="attend",
     )(idx, emb, q_cache, mine, theirs, out_w)
 
@@ -401,18 +391,20 @@
         kept.append(have[:, 0:n].reshape(-1, 2 * hw))
         return have[:, n:]
 
-    have = step(step(step(picks[None], 0), 1), 2)
+    have = step(step(picks[None], 0), 1)
     far[0], have, joined = lax.optimization_barrier((far[0], have, joined))
     first = encode(idx, 0, tile_batch, left, right, far[0], gain, tile_w)
-    have = step(have, 3)
+    have = step(have, 2)
     far[1], have, first = lax.optimization_barrier((far[1], have, first))
     second = encode(idx, 1, tile_batch, left, right, far[1], gain, tile_w)
+    have = step(have, 3)
+    first, second, have = lax.optimization_barrier((first, second, have))
+    partial = dot(jnp.concatenate([first, second], axis=0).astype(BF), joined)
+    shares = [partial] + [shift_mp(partial, k) for k in (1, 3, 2)]
     have = step(have, 4)
     mine = jnp.concatenate(kept + [have.reshape(-1, 2 * hw)], axis=0)
-    first, second, mine = lax.optimization_barrier((first, second, mine))
+    shares, mine = lax.optimization_barrier((shares, mine))
     theirs = swap_seq(mine, 1)
-    partial = dot(jnp.concatenate([first, second], axis=0).astype(BF), joined)
-    shares = [partial] + [shift_mp(partial, k) for k in (1, 3, 2)]
     emb = embed_rows(idx, shares, gain_row, slide_w)
     emb = lax.all_to_all(jnp.broadcast_to(emb[None], (64,) + emb.shape), "seq", 0, 0)
     emb = emb.reshape(64 * slots, emb.shape[2])

time: 113 us -> 108 us (0.956)
  waiting for transfers between devices: 32.2 us -> 20.5 us
  starting transfers between devices: 37.6 us -> 46.8 us
  Pallas kernels: 22.2 us -> 19.7 us
    ppermute x6, waiting for transfers between devices: 15.6 us -> 6.37 us  [swap_seq(): return lax.ppermute(x, 'seq', [(i, i ^ bit) for i in range(64)])]
    ppermute x6, starting transfers between devices: 18.9 us -> 23.5 us  [swap_seq(): return lax.ppermute(x, 'seq', [(i, i ^ bit) for i in range(64)])]
    ppermute x10, starting transfers between devices: 10 us -> 13.4 us  [shift_mp(): return lax.ppermute(x, 'mp', [(i, (i + k) % 4) for i in range(4)])]
    pallas_call x2, Pallas kernels: 13.8 us -> 11.3 us  [encode(): pl.pallas_call(encode_kernel, grid=(1,), out_shape=jax.ShapeDtypeStruct((...]
    ppermute x10, waiting for transfers between devices: 7.23 us -> 4.82 us  [shift_mp(): return lax.ppermute(x, 'mp', [(i, (i + k) % 4) for i in range(4)])]
    all_to_all x1, starting transfers between devices: 8.68 us -> 10 us  [local(): lax.all_to_all(jnp.broadcast_to(emb[None], (64,) + emb.shape), 'seq', 0, 0)]
    unnamed x31 -> x34, local copies, waits for them, and re-layouts: 6.54 us -> 5.81 us
  transfers between devices with their start and end apart: 17 -> 17, of which waited for: 8 -> 9; matrix products, arithmetic and copies ran while one was open for 11% -> 12% of each run, Pallas kernels for 14% -> 13%
where the time goes in v6:
time: 108 us; the launch traced here: 107 us
  starting transfers between devices  46.8 us (43%)
  waiting for transfers between devices  20.5 us (19%)
  Pallas kernels  19.7 us (18%)
  local copies, waits for them, and re-layouts  15 us (14%)
  matrix products  3.45 us (3%)
    ppermute x6, starting transfers between devices, swap_seq(): return lax.ppermute(x, 'seq', [(i, i ^ bit) for i in range(64)])  23.5 us
    ppermute x10, starting transfers between devices, shift_mp(): return lax.ppermute(x, 'mp', [(i, (i + k) % 4) for i in range(4)])  13.4 us
    pallas_call x2, Pallas kernels, encode(): pl.pallas_call(encode_kernel, grid=(1,), out_shape=jax.ShapeDtypeStruct((...  11.3 us
    all_to_all x1, starting transfers between devices, local(): lax.all_to_all(jnp.broadcast_to(emb[None], (64,) + emb.shape), 'seq', 0, 0)  10 us
    all_to_all x1, waiting for transfers between devices, local(): lax.all_to_all(jnp.broadcast_to(emb[None], (64,) + emb.shape), 'seq', 0, 0)  9.33 us
    ppermute x6, waiting for transfers between devices, swap_seq(): return lax.ppermute(x, 'seq', [(i, i ^ bit) for i in range(64)])  6.37 us
    pallas_call x1, Pallas kernels, attend(): pl.pallas_call(attend_kernel, out_shape=(jax.ShapeDtypeStruct((ROWS, hw),...  6.02 us
    unnamed x34, local copies, waits for them, and re-layouts  5.81 us
  transfers between devices with their start and end apart: 17, of which 9 were waited for; matrix products, arithmetic and copies ran while one was open for 12% of the time, Pallas kernels for 13%

profile of v6, /device:TPU:1, one launch (start us, length us, event | category | flops | bytes accessed | tf_op | source)
XLA Modules:
  0.0 107.4 jit_solution(14321330433894770702)
XLA Ops:
  0.0 2.0 %collective-permute-start.2 = (bf16[4,256,384]{2,1,0:T(8,128)(2,1)}, bf16[4,256,384]{2,1,0:T(8,128)(2,1)S(1)}, u32[]{:S(2)}, u32[]{:S(2)}) collective-permute-start(bf16[4,256,384]{2,1,0:T(8,128)(2,1)} %own.3), channel_id=1, source_target_pairs={{0,1},{1,2},{2,3},{3,0},{4,5},{5,6},{6,7},{7,4},{8,9},{9,10},{10,1... | collective-permute-start | bytes 2359304 | tf_op jit(solution)/shard_map/ppermute | solution.py:347
  2.0 1.4 %collective-permute-start = (bf16[4,256,384]{2,1,0:T(8,128)(2,1)}, bf16[4,256,384]{2,1,0:T(8,128)(2,1)}, u32[]{:S(2)}, u32[]{:S(2)}) collective-permute-start(bf16[4,256,384]{2,1,0:T(8,128)(2,1)} %own.3), channel_id=1, source_target_pairs={{0,3},{1,0},{2,1},{3,2},{4,7},{5,4},{6,5},{7,6},{8,11},{9,8},{10,9... | collective-permute-start | bytes 2359304 | tf_op jit(solution)/shard_map/ppermute | solution.py:347
  5.5 1.2 %copy-done.1 = bf16[768,3,192]{0,2,1:T(8,128)(2,1)S(1)} copy-done((bf16[768,3,192]{0,2,1:T(8,128)(2,1)S(1)}, bf16[768,3,192]{0,2,1:T(8,128)(2,1)}, u32[]{:S(2)}) %copy-start.1) | copy-done | bytes 884760
  6.6 0.9 copy-done.5
  7.6 1.3 %slide_project.1 = (f32[128,192]{1,0:T(8,128)S(1)}, bf16[256,384]{1,0:T(8,128)(2,1)S(1)}) custom-call(s32[7]{0:T(128)S(1)} %pad_add_fusion.idx, bf16[128,768]{1,0:T(8,128)(2,1)S(1)} %copy-done.5, f32[1,768]{1,0:T(1,128)S(1)} %reshape.31.gain, bf16[576,768]{1,0:T(8,128)(2,1)S(1)} %bitcast.18), custom_call_target="tpu_custom_call" | custom-call | tf_op jit(solution)/shard_map/slide_project/pallas_call | solution.py:192
  9.6 1.8 %collective-permute-start.4 = (bf16[1,256,384]{2,1,0:T(8,128)(2,1)S(1)}, bf16[1,256,384]{2,1,0:T(8,128)(2,1)S(1)}, u32[]{:S(2)}, u32[]{:S(2)}) collective-permute-start(bf16[1,256,384]{2,1,0:T(8,128)(2,1)S(1)} %bitcast.21), channel_id=1, source_target_pairs={{0,8},{4,12},{8,0},{12,4},{16,24},{20,28},{24,16},{28,20},{32,40},... | collective-permute-start | bytes 589832 | tf_op jit(solution)/shard_map/ppermute | solution.py:351
  11.3 3.2 %convolution_convert_fusion = bf16[384,768]{1,0:T(8,128)(2,1)} fusion(bf16[384,1536]{1,0:T(8,128)(2,1)} %param.16, bf16[1536,768]{1,0:T(8,128)(2,1)S(1)} %copy-done), kind=kOutput, calls=%fused_computation | convolution fusion | flops 906264576 | bytes 4128768 | tf_op jit(solution)/shard_map/dot_general | solution.py:31
  14.8 3.6 %collective-permute-start.5 = (bf16[2,128,384]{2,1,0:T(8,128)(2,1)S(1)}, bf16[2,128,384]{2,1,0:T(8,128)(2,1)S(1)}, u32[]{:S(2)}, u32[]{:S(2)}) collective-permute-start(bf16[2,128,384]{2,1,0:T(8,128)(2,1)S(1)} %get-tuple-element.52), channel_id=1, source_target_pairs={{0,16},{4,20},{8,24},{12,28},{16,0},{20,4},{24,8},{28,12},{32,48},... | collective-permute-start | bytes 589832 | tf_op jit(solution)/shard_map/ppermute | solution.py:351
  18.5 2.1 %collective-permute-start.3 = (bf16[2,256,384]{2,1,0:T(8,128)(2,1)S(1)}, bf16[2,256,384]{2,1,0:T(8,128)(2,1)S(1)}, u32[]{:S(2)}, u32[]{:S(2)}) collective-permute-start(bf16[2,256,384]{2,1,0:T(8,128)(2,1)S(1)} %slice.41), channel_id=1, source_target_pairs={{0,1},{1,2},{2,3},{3,0},{4,5},{5,6},{6,7},{7,4},{8,9},{9,10},{10,1... | collective-permute-start | bytes 1179656 | tf_op jit(solution)/shard_map/ppermute | solution.py:347
  20.8 6.1 %collective-permute-done.5 = bf16[2,128,384]{2,1,0:T(8,128)(2,1)S(1)} collective-permute-done((bf16[2,128,384]{2,1,0:T(8,128)(2,1)S(1)}, bf16[2,128,384]{2,1,0:T(8,128)(2,1)S(1)}, u32[]{:S(2)}, u32[]{:S(2)}) %collective-permute-start.5) | collective-permute-done | bytes 196640 | tf_op jit(solution)/shard_map/ppermute | solution.py:351
  27.0 1.0 slice.40
  28.0 1.3 %collective-permute-start.1 = (bf16[2,256,384]{2,1,0:T(8,128)(2,1)S(1)}, bf16[2,256,384]{2,1,0:T(8,128)(2,1)S(1)}, u32[]{:S(2)}, u32[]{:S(2)}) collective-permute-start(bf16[2,256,384]{2,1,0:T(8,128)(2,1)S(1)} %slice.40), channel_id=1, source_target_pairs={{0,3},{1,0},{2,1},{3,2},{4,7},{5,4},{6,5},{7,6},{8,11},{9,8},{10,9... | collective-permute-start | bytes 1179656 | tf_op jit(solution)/shard_map/ppermute | solution.py:347
  29.4 8.6 %collective-permute-start.6 = (bf16[4,64,384]{2,1,0:T(8,128)(2,1)S(1)}, bf16[4,64,384]{2,1,0:T(8,128)(2,1)S(1)}, u32[]{:S(2)}, u32[]{:S(2)}) collective-permute-start(bf16[4,64,384]{2,1,0:T(8,128)(2,1)S(1)} %get-tuple-element.26), channel_id=1, source_target_pairs={{0,32},{4,36},{8,40},{12,44},{16,48},{20,52},{24,56},{28,60},{32,0... | collective-permute-start | bytes 589832 | tf_op jit(solution)/shard_map/ppermute | solution.py:351
  38.0 5.7 %encode.2 = f32[2,768]{1,0:T(2,128)S(1)} custom-call(s32[7]{0:T(128)S(1)} %pad_add_fusion.idx, bf16[4,256,384]{2,1,0:T(8,128)(2,1)S(1)} %copy-done.11, bf16[4,256,384]{2,1,0:T(8,128)(2,1)S(1)} %copy-done.7, bf16[4,256,384]{2,1,0:T(8,128)(2,1)} %collective-permute-done.right, bf16[2,256,384]{2,1,0:T(8,128)(2,1)S(1)} %collective-permute-done.3.far, ...), custom_call_target="tpu_custom_call" | custom-call | flops 6000000000 | bytes 8000000 | tf_op jit(solution)/shard_map/encode/pallas_call | solution.py:92
  43.8 1.6 %collective-permute-start.7 = (bf16[8,32,384]{2,1,0:T(8,128)(2,1)S(1)}, bf16[8,32,384]{2,1,0:T(8,128)(2,1)S(1)}, u32[]{:S(2)}, u32[]{:S(2)}) collective-permute-start(bf16[8,32,384]{2,1,0:T(8,128)(2,1)S(1)} %get-tuple-element.30), channel_id=1, source_target_pairs={{0,64},{4,68},{8,72},{12,76},{16,80},{20,84},{24,88},{28,92},{32,9... | collective-permute-start | bytes 589832 | tf_op jit(solution)/shard_map/ppermute | solution.py:351
  45.4 5.7 %encode.3 = f32[2,768]{1,0:T(2,128)S(1)} custom-call(s32[7]{0:T(128)S(1)} %pad_add_fusion.idx, bf16[4,256,384]{2,1,0:T(8,128)(2,1)S(1)} %copy-done.11, bf16[4,256,384]{2,1,0:T(8,128)(2,1)S(1)} %copy-done.7, bf16[4,256,384]{2,1,0:T(8,128)(2,1)} %collective-permute-done.right, bf16[2,256,384]{2,1,0:T(8,128)(2,1)S(1)} %collective-permute-done.1.far, ...), custom_call_target="tpu_custom_call" | custom-call | flops 6000000000 | bytes 8000000 | tf_op jit(solution)/shard_map/encode/pallas_call | solution.py:92
  51.2 2.7 %collective-permute-start.11 = (bf16[16,16,384]{2,1,0:T(8,128)(2,1)S(1)}, bf16[16,16,384]{2,1,0:T(8,128)(2,1)S(1)}, u32[]{:S(2)}, u32[]{:S(2)}) collective-permute-start(bf16[16,16,384]{2,1,0:T(8,128)(2,1)S(1)} %get-tuple-element.34), channel_id=1, source_target_pairs={{0,128},{4,132},{8,136},{12,140},{16,144},{20,148},{24,152},{28,15... | collective-permute-start | bytes 589832 | tf_op jit(solution)/shard_map/ppermute | solution.py:351
  55.1 2.4 %collective-permute-start.9 = (f32[4,768]{1,0:T(4,128)S(1)}, f32[4,768]{1,0:T(4,128)S(1)}, u32[]{:S(2)}, u32[]{:S(2)}) collective-permute-start(f32[4,768]{1,0:T(4,128)S(1)} %fusion.2.a), channel_id=1, source_target_pairs={{0,3},{1,0},{2,1},{3,2},{4,7},{5,4},{6,5},{7,6},{8,11},{9,8},{10,9... | collective-permute-start | bytes 36872 | tf_op jit(solution)/shard_map/ppermute | solution.py:347
  58.6 5.2 %collective-permute-start.12 = (bf16[1536,384]{1,0:T(8,128)(2,1)S(1)}, bf16[1536,384]{1,0:T(8,128)(2,1)}, u32[]{:S(2)}, u32[]{:S(2)}) collective-permute-start(bf16[1536,384]{1,0:T(8,128)(2,1)S(1)} %constant_dynamic-update-slice_fusion.4.refs_2_), channel_id=1, source_target_pairs={{0,4},{4,0},{8,12},{12,8},{16,20},{20,16},{24,28},{28,24},{32,36},... | collective-permute-start | bytes 3538952 | tf_op jit(solution)/shard_map/ppermute | solution.py:351
  63.8 1.0 embed_rows.1
  65.7 10.0 %all-to-all-start = ((bf16[64,4,640]{2,1,0:T(4,128)(2,1)}), bf16[64,4,640]{2,1,0:T(4,128)(2,1)}, u32[]{:S(2)}, u32[]{:S(2)}) async-start(bf16[64,4,640]{2,1,0:T(4,128)(2,1)} %broadcast_in_dim.10), calls=%async_computation | async-start | bytes 655360 | tf_op jit(solution)/shard_map/all_to_all | solution.py:409
  75.7 2.1 %reshape.40 = bf16[192,4,192]{2,1,0:T(4,128)(2,1)} reshape(bf16[192,768]{1,0:T(8,128)(2,1)} %param.21) | data formatting | bytes 589824 | tf_op jit(solution)/shard_map/reshape | solution.py:412
  77.8 1.8 %copy.16 = bf16[192,4,192]{2,0,1:T(8,128)(2,1)} copy(bf16[192,4,192]{2,1,0:T(4,128)(2,1)} %reshape.40) | data formatting | bytes 589824 | tf_op jit(solution)/shard_map/reshape | solution.py:412
  79.5 9.3 %all-to-all-done = bf16[64,4,640]{2,1,0:T(4,128)(2,1)} async-done(((bf16[64,4,640]{2,1,0:T(4,128)(2,1)}), bf16[64,4,640]{2,1,0:T(4,128)(2,1)}, u32[]{:S(2)}, u32[]{:S(2)}) %all-to-all-start) | async-done | bytes 327712 | tf_op jit(solution)/shard_map/all_to_all | solution.py:409
  88.9 1.8 %reshape.39.refs_0_ = bf16[256,640]{1,0:T(8,128)(2,1)} reshape(bf16[64,4,640]{2,1,0:T(4,128)(2,1)} %all-to-all-done) | data formatting | bytes 655360 | tf_op jit(solution)/shard_map/reshape | solution.py:410
  90.6 1.0 copy-done.3
  91.6 1.0 copy-done.4
  93.5 6.0 %attend.1 = (bf16[128,192]{1,0:T(8,128)(2,1)S(1)}, bf16[128,192]{1,0:T(8,128)(2,1)S(1)}, bf16[128,192]{1,0:T(8,128)(2,1)S(1)}, bf16[128,192]{1,0:T(8,128)(2,1)S(1)}) custom-call(s32[7]{0:T(128)S(1)} %pad_add_fusion.idx, bf16[256,640]{1,0:T(8,128)(2,1)S(1)} %copy-done.4, f32[128,192]{1,0:T(8,128)S(1)} %copy-done.9, ...), custom_call_target="tpu_custom_call" | custom-call | tf_op jit(solution)/shard_map/attend/pallas_call | solution.py:328
  100.0 2.9 %collective-permute-start.14 = (bf16[128,192]{1,0:T(8,128)(2,1)S(1)}, bf16[128,192]{1,0:T(8,128)(2,1)S(1)}, u32[]{:S(2)}, u32[]{:S(2)}) collective-permute-start(bf16[128,192]{1,0:T(8,128)(2,1)S(1)} %get-tuple-element.43), channel_id=1, source_target_pairs={{0,2},{1,3},{2,0},{3,1},{4,6},{5,7},{6,4},{7,5},{8,10},{9,11},{10,... | collective-permute-start | bytes 147464 | tf_op jit(solution)/shard_map/ppermute | solution.py:347
  102.8 1.1 %collective-permute-done.13 = bf16[128,192]{1,0:T(8,128)(2,1)S(1)} collective-permute-done((bf16[128,192]{1,0:T(8,128)(2,1)S(1)}, bf16[128,192]{1,0:T(8,128)(2,1)S(1)}, u32[]{:S(2)}, u32[]{:S(2)}) %collective-permute-start.13) | collective-permute-done | bytes 49184 | tf_op jit(solution)/shard_map/ppermute | solution.py:347
  103.9 1.8 %collective-permute-done.14 = bf16[128,192]{1,0:T(8,128)(2,1)S(1)} collective-permute-done((bf16[128,192]{1,0:T(8,128)(2,1)S(1)}, bf16[128,192]{1,0:T(8,128)(2,1)S(1)}, u32[]{:S(2)}, u32[]{:S(2)}) %collective-permute-start.14) | collective-permute-done | bytes 49184 | tf_op jit(solution)/shard_map/ppermute | solution.py:347
  105.7 0.9 collective-permute-done.15
  (66 shorter events, 8.1 us)
Async XLA Ops:
  0.0 11.3 %copy-start = (bf16[1536,768]{1,0:T(8,128)(2,1)S(1)}, bf16[1536,768]{1,0:T(8,128)(2,1)}, u32[]{:S(2)}) copy-start(bf16[1536,768]{1,0:T(8,128)(2,1)} %param.17) | copy-start | bytes 7077892
  0.0 18.5 %collective-permute-start.2 = (bf16[4,256,384]{2,1,0:T(8,128)(2,1)}, bf16[4,256,384]{2,1,0:T(8,128)(2,1)S(1)}, u32[]{:S(2)}, u32[]{:S(2)}) collective-permute-start(bf16[4,256,384]{2,1,0:T(8,128)(2,1)} %own.3), channel_id=1, source_target_pairs={{0,1},{1,2},{2,3},{3,0},{4,5},{5,6},{6,7},{7,4},{8,9},{9,10},{10,1... | collective-permute-start | bytes 2359304 | tf_op jit(solution)/shard_map/ppermute | solution.py:347
  2.0 24.9 %collective-permute-start = (bf16[4,256,384]{2,1,0:T(8,128)(2,1)}, bf16[4,256,384]{2,1,0:T(8,128)(2,1)}, u32[]{:S(2)}, u32[]{:S(2)}) collective-permute-start(bf16[4,256,384]{2,1,0:T(8,128)(2,1)} %own.3), channel_id=1, source_target_pairs={{0,3},{1,0},{2,1},{3,2},{4,7},{5,4},{6,5},{7,6},{8,11},{9,8},{10,9... | collective-permute-start | bytes 2359304 | tf_op jit(solution)/shard_map/ppermute | solution.py:347
  5.5 1.2 %copy-start.1 = (bf16[768,3,192]{0,2,1:T(8,128)(2,1)S(1)}, bf16[768,3,192]{0,2,1:T(8,128)(2,1)}, u32[]{:S(2)}) copy-start(bf16[768,3,192]{0,2,1:T(8,128)(2,1)} %param.20) | copy-start | bytes 2654212
  6.6 0.9 copy-start.5
  8.9 0.7 copy-start.8
  9.6 5.2 %collective-permute-start.4 = (bf16[1,256,384]{2,1,0:T(8,128)(2,1)S(1)}, bf16[1,256,384]{2,1,0:T(8,128)(2,1)S(1)}, u32[]{:S(2)}, u32[]{:S(2)}) collective-permute-start(bf16[1,256,384]{2,1,0:T(8,128)(2,1)S(1)} %bitcast.21), channel_id=1, source_target_pairs={{0,8},{4,12},{8,0},{12,4},{16,24},{20,28},{24,16},{28,20},{32,40},... | collective-permute-start | bytes 589832 | tf_op jit(solution)/shard_map/ppermute | solution.py:351
  14.5 6.1 %copy-start.12 = (bf16[384,768]{1,0:T(8,128)(2,1)S(1)}, bf16[384,768]{1,0:T(8,128)(2,1)}, u32[]{:S(2)}) copy-start(bf16[384,768]{1,0:T(8,128)(2,1)} %convolution_convert_fusion) | copy-start | bytes 1769476
  14.8 12.1 %collective-permute-start.5 = (bf16[2,128,384]{2,1,0:T(8,128)(2,1)S(1)}, bf16[2,128,384]{2,1,0:T(8,128)(2,1)S(1)}, u32[]{:S(2)}, u32[]{:S(2)}) collective-permute-start(bf16[2,128,384]{2,1,0:T(8,128)(2,1)S(1)} %get-tuple-element.52), channel_id=1, source_target_pairs={{0,16},{4,20},{8,24},{12,28},{16,0},{20,4},{24,8},{28,12},{32,48},... | collective-permute-start | bytes 589832 | tf_op jit(solution)/shard_map/ppermute | solution.py:351
  18.5 2.2 %copy-start.6 = (bf16[4,256,384]{2,1,0:T(8,128)(2,1)}, bf16[4,256,384]{2,1,0:T(8,128)(2,1)S(1)}, u32[]{:S(2)}) copy-start(bf16[4,256,384]{2,1,0:T(8,128)(2,1)S(1)} %collective-permute-done.2.left) | copy-start | bytes 2359300
  18.5 19.5 %copy-start.11 = (bf16[4,256,384]{2,1,0:T(8,128)(2,1)S(1)}, bf16[4,256,384]{2,1,0:T(8,128)(2,1)}, u32[]{:S(2)}) copy-start(bf16[4,256,384]{2,1,0:T(8,128)(2,1)} %own.3) | copy-start | bytes 2359300
  18.5 2.2 %copy-start.13 = (f32[1536]{0:T(1024)S(1)}, f32[1536]{0:T(1024)}, u32[]{:S(2)}) copy-start(f32[1536]{0:T(1024)} %param.14) | copy-start | bytes 18436
  18.5 10.8 %collective-permute-start.3 = (bf16[2,256,384]{2,1,0:T(8,128)(2,1)S(1)}, bf16[2,256,384]{2,1,0:T(8,128)(2,1)S(1)}, u32[]{:S(2)}, u32[]{:S(2)}) collective-permute-start(bf16[2,256,384]{2,1,0:T(8,128)(2,1)S(1)} %slice.41), channel_id=1, source_target_pairs={{0,1},{1,2},{2,3},{3,0},{4,5},{5,6},{6,7},{7,4},{8,9},{9,10},{10,1... | collective-permute-start | bytes 1179656 | tf_op jit(solution)/shard_map/ppermute | solution.py:347
  20.6 17.4 %copy-start.10 = (bf16[1536,3,384]{2,0,1:T(8,128)(2,1)S(1)}, bf16[1536,3,384]{2,0,1:T(8,128)(2,1)}, u32[]{:S(2)}) copy-start(bf16[1536,3,384]{2,0,1:T(8,128)(2,1)} %param.15) | copy-start | bytes 10616836
  20.7 17.2 %copy-start.7 = (bf16[4,256,384]{2,1,0:T(8,128)(2,1)S(1)}, bf16[4,256,384]{2,1,0:T(8,128)(2,1)}, u32[]{:S(2)}) copy-start(bf16[4,256,384]{2,1,0:T(8,128)(2,1)} %copy-done.6) | copy-start | bytes 2359300
  28.0 15.8 %collective-permute-start.1 = (bf16[2,256,384]{2,1,0:T(8,128)(2,1)S(1)}, bf16[2,256,384]{2,1,0:T(8,128)(2,1)S(1)}, u32[]{:S(2)}, u32[]{:S(2)}) collective-permute-start(bf16[2,256,384]{2,1,0:T(8,128)(2,1)S(1)} %slice.40), channel_id=1, source_target_pairs={{0,3},{1,0},{2,1},{3,2},{4,7},{5,4},{6,5},{7,6},{8,11},{9,8},{10,9... | collective-permute-start | bytes 1179656 | tf_op jit(solution)/shard_map/ppermute | solution.py:347
  29.4 14.3 %collective-permute-start.6 = (bf16[4,64,384]{2,1,0:T(8,128)(2,1)S(1)}, bf16[4,64,384]{2,1,0:T(8,128)(2,1)S(1)}, u32[]{:S(2)}, u32[]{:S(2)}) collective-permute-start(bf16[4,64,384]{2,1,0:T(8,128)(2,1)S(1)} %get-tuple-element.26), channel_id=1, source_target_pairs={{0,32},{4,36},{8,40},{12,44},{16,48},{20,52},{24,56},{28,60},{32,0... | collective-permute-start | bytes 589832 | tf_op jit(solution)/shard_map/ppermute | solution.py:351
  43.8 7.3 %collective-permute-start.7 = (bf16[8,32,384]{2,1,0:T(8,128)(2,1)S(1)}, bf16[8,32,384]{2,1,0:T(8,128)(2,1)S(1)}, u32[]{:S(2)}, u32[]{:S(2)}) collective-permute-start(bf16[8,32,384]{2,1,0:T(8,128)(2,1)S(1)} %get-tuple-element.30), channel_id=1, source_target_pairs={{0,64},{4,68},{8,72},{12,76},{16,80},{20,84},{24,88},{28,92},{32,9... | collective-permute-start | bytes 589832 | tf_op jit(solution)/shard_map/ppermute | solution.py:351
  51.2 6.3 %collective-permute-start.11 = (bf16[16,16,384]{2,1,0:T(8,128)(2,1)S(1)}, bf16[16,16,384]{2,1,0:T(8,128)(2,1)S(1)}, u32[]{:S(2)}, u32[]{:S(2)}) collective-permute-start(bf16[16,16,384]{2,1,0:T(8,128)(2,1)S(1)} %get-tuple-element.34), channel_id=1, source_target_pairs={{0,128},{4,132},{8,136},{12,140},{16,144},{20,148},{24,152},{28,15... | collective-permute-start | bytes 589832 | tf_op jit(solution)/shard_map/ppermute | solution.py:351
  54.2 9.6 %copy-start.2 = (bf16[768,3,192]{0,2,1:T(8,128)(2,1)S(1)}, bf16[768,3,192]{0,2,1:T(8,128)(2,1)}, u32[]{:S(2)}) copy-start(bf16[768,3,192]{0,2,1:T(8,128)(2,1)} %param.20) | copy-start | bytes 2654212
  54.2 4.1 %collective-permute-start.10 = (f32[4,768]{1,0:T(4,128)S(1)}, f32[4,768]{1,0:T(4,128)S(1)}, u32[]{:S(2)}, u32[]{:S(2)}) collective-permute-start(f32[4,768]{1,0:T(4,128)S(1)} %fusion.2.a), channel_id=1, source_target_pairs={{0,2},{1,3},{2,0},{3,1},{4,6},{5,7},{6,4},{7,5},{8,10},{9,11},{10,... | collective-permute-start | bytes 36872 | tf_op jit(solution)/shard_map/ppermute | solution.py:347
  54.8 3.8 %collective-permute-start.8 = (f32[4,768]{1,0:T(4,128)S(1)}, f32[4,768]{1,0:T(4,128)S(1)}, u32[]{:S(2)}, u32[]{:S(2)}) collective-permute-start(f32[4,768]{1,0:T(4,128)S(1)} %fusion.2.a), channel_id=1, source_target_pairs={{0,1},{1,2},{2,3},{3,0},{4,5},{5,6},{6,7},{7,4},{8,9},{9,10},{10,1... | collective-permute-start | bytes 36872 | tf_op jit(solution)/shard_map/ppermute | solution.py:347
  55.1 3.5 %collective-permute-start.9 = (f32[4,768]{1,0:T(4,128)S(1)}, f32[4,768]{1,0:T(4,128)S(1)}, u32[]{:S(2)}, u32[]{:S(2)}) collective-permute-start(f32[4,768]{1,0:T(4,128)S(1)} %fusion.2.a), channel_id=1, source_target_pairs={{0,3},{1,0},{2,1},{3,2},{4,7},{5,4},{6,5},{7,6},{8,11},{9,8},{10,9... | collective-permute-start | bytes 36872 | tf_op jit(solution)/shard_map/ppermute | solution.py:347
  58.6 32.1 %collective-permute-start.12 = (bf16[1536,384]{1,0:T(8,128)(2,1)S(1)}, bf16[1536,384]{1,0:T(8,128)(2,1)}, u32[]{:S(2)}, u32[]{:S(2)}) collective-permute-start(bf16[1536,384]{1,0:T(8,128)(2,1)S(1)} %constant_dynamic-update-slice_fusion.4.refs_2_), channel_id=1, source_target_pairs={{0,4},{4,0},{8,12},{12,8},{16,20},{20,16},{24,28},{28,24},{32,36},... | collective-permute-start | bytes 3538952 | tf_op jit(solution)/shard_map/ppermute | solution.py:351
  65.7 23.2 %all-to-all-start = ((bf16[64,4,640]{2,1,0:T(4,128)(2,1)}), bf16[64,4,640]{2,1,0:T(4,128)(2,1)}, u32[]{:S(2)}, u32[]{:S(2)}) async-start(bf16[64,4,640]{2,1,0:T(4,128)(2,1)} %broadcast_in_dim.10), calls=%async_computation | async-start | bytes 655360 | tf_op jit(solution)/shard_map/all_to_all | solution.py:409
  90.6 1.0 copy-start.3
  91.6 1.0 copy-start.4
  92.6 0.9 copy-start.9
  99.5 4.4 %collective-permute-start.13 = (bf16[128,192]{1,0:T(8,128)(2,1)S(1)}, bf16[128,192]{1,0:T(8,128)(2,1)S(1)}, u32[]{:S(2)}, u32[]{:S(2)}) collective-permute-start(bf16[128,192]{1,0:T(8,128)(2,1)S(1)} %get-tuple-element.42), channel_id=1, source_target_pairs={{0,1},{1,2},{2,3},{3,0},{4,5},{5,6},{6,7},{7,4},{8,9},{9,10},{10,1... | collective-permute-start | bytes 147464 | tf_op jit(solution)/shard_map/ppermute | solution.py:347
  100.0 5.8 %collective-permute-start.14 = (bf16[128,192]{1,0:T(8,128)(2,1)S(1)}, bf16[128,192]{1,0:T(8,128)(2,1)S(1)}, u32[]{:S(2)}, u32[]{:S(2)}) collective-permute-start(bf16[128,192]{1,0:T(8,128)(2,1)S(1)} %get-tuple-element.43), channel_id=1, source_target_pairs={{0,2},{1,3},{2,0},{3,1},{4,6},{5,7},{6,4},{7,5},{8,10},{9,11},{10,... | collective-permute-start | bytes 147464 | tf_op jit(solution)/shard_map/ppermute | solution.py:347
  102.8 3.8 %collective-permute-start.15 = (bf16[128,192]{1,0:T(8,128)(2,1)S(1)}, bf16[128,192]{1,0:T(8,128)(2,1)S(1)}, u32[]{:S(2)}, u32[]{:S(2)}) collective-permute-start(bf16[128,192]{1,0:T(8,128)(2,1)S(1)} %get-tuple-element.44), channel_id=1, source_target_pairs={{0,3},{1,0},{2,1},{3,2},{4,7},{5,4},{6,5},{7,6},{8,11},{9,8},{10,9... | collective-permute-start | bytes 147464 | tf_op jit(solution)/shard_map/ppermute | solution.py:347

commit v7 on v6

--- a/solution.py
+++ b/solution.py
@@ -338,7 +338,7 @@
             pltpu.VMEM((4 * ROWS, hw), F32),
             pltpu.SemaphoreType.DMA((5,)),
         ],
-        compiler_params=params(20),
+        compiler_params=params(60),
         name="attend",
     )(idx, emb, q_cache, mine, theirs, out_w)
 
@@ -395,15 +395,15 @@
     far[0], have, joined = lax.optimization_barrier((far[0], have, joined))
     first = encode(idx, 0, tile_batch, left, right, far[0], gain, tile_w)
     have = step(have, 2)
-    far[1], have, first = lax.optimization_barrier((far[1], have, first))
+    far[1], first = lax.optimization_barrier((far[1], first))
     second = encode(idx, 1, tile_batch, left, right, far[1], gain, tile_w)
-    have = step(have, 3)
     first, second, have = lax.optimization_barrier((first, second, have))
     partial = dot(jnp.concatenate([first, second], axis=0).astype(BF), joined)
     shares = [partial] + [shift_mp(partial, k) for k in (1, 3, 2)]
+    have = step(have, 3)
+    shares, have = lax.optimization_barrier((shares, have))
     have = step(have, 4)
     mine = jnp.concatenate(kept + [have.reshape(-1, 2 * hw)], axis=0)
-    shares, mine = lax.optimization_barrier((shares, mine))
     theirs = swap_seq(mine, 1)
     emb = embed_rows(idx, shares, gain_row, slide_w)
     emb = lax.all_to_all(jnp.broadcast_to(emb[None], (64,) + emb.shape), "seq", 0, 0)

time: 108 us -> 108 us (level)
  waiting for transfers between devices: 20.5 us -> 27.6 us
  starting transfers between devices: 46.8 us -> 41.7 us
  local copies, waits for them, and re-layouts: 15 us -> 11.8 us
    all_to_all x1, starting transfers between devices: 10 us -> 6.21 us  [local(): lax.all_to_all(jnp.broadcast_to(emb[None], (64,) + emb.shape), 'seq', 0, 0)]
    ppermute x10, waiting for transfers between devices: 4.82 us -> 7.61 us  [shift_mp(): return lax.ppermute(x, 'mp', [(i, (i + k) % 4) for i in range(4)])]
    all_to_all x1, waiting for transfers between devices: 9.33 us -> 12.1 us  [local(): lax.all_to_all(jnp.broadcast_to(emb[None], (64,) + emb.shape), 'seq', 0, 0)]
    reshape x2, local copies, waits for them, and re-layouts: 3.86 us -> 1.15 us  [local(): out_w = long_out.reshape(hw, 4, hw).transpose(1, 0, 2)]
    ppermute x6, waiting for transfers between devices: 6.37 us -> 7.92 us  [swap_seq(): return lax.ppermute(x, 'seq', [(i, i ^ bit) for i in range(64)])]
    ppermute x10, starting transfers between devices: 13.4 us -> 12.3 us  [shift_mp(): return lax.ppermute(x, 'mp', [(i, (i + k) % 4) for i in range(4)])]
    unnamed x34 -> x28, local copies, waits for them, and re-layouts: 5.81 us -> 5.59 us
  transfers between devices with their start and end apart: 17 -> 17, of which waited for: 9 -> 9; matrix products, arithmetic and copies ran while one was open for 12% -> 11% of each run, Pallas kernels for 13% -> 13%
where the time goes in v7:
time: 108 us
  starting transfers between devices  41.7 us (39%)
  waiting for transfers between devices  27.6 us (26%)
  Pallas kernels  20.6 us (19%)
  local copies, waits for them, and re-layouts  11.8 us (11%)
  matrix products  3.46 us (3%)
  other arithmetic  1.83 us (2%)
    ppermute x6, starting transfers between devices, swap_seq(): return lax.ppermute(x, 'seq', [(i, i ^ bit) for i in range(64)])  23.2 us
    ppermute x10, starting transfers between devices, shift_mp(): return lax.ppermute(x, 'mp', [(i, (i + k) % 4) for i in range(4)])  12.3 us
    all_to_all x1, waiting for transfers between devices, local(): lax.all_to_all(jnp.broadcast_to(emb[None], (64,) + emb.shape), 'seq', 0, 0)  12.1 us
    pallas_call x2, Pallas kernels, encode(): pl.pallas_call(encode_kernel, grid=(1,), out_shape=jax.ShapeDtypeStruct((...  11.3 us
    ppermute x6, waiting for transfers between devices, swap_seq(): return lax.ppermute(x, 'seq', [(i, i ^ bit) for i in range(64)])  7.92 us
    ppermute x10, waiting for transfers between devices, shift_mp(): return lax.ppermute(x, 'mp', [(i, (i + k) % 4) for i in range(4)])  7.61 us
    pallas_call x1, Pallas kernels, attend(): pl.pallas_call(attend_kernel, out_shape=(jax.ShapeDtypeStruct((ROWS, hw),...  6.92 us
    all_to_all x1, starting transfers between devices, local(): lax.all_to_all(jnp.broadcast_to(emb[None], (64,) + emb.shape), 'seq', 0, 0)  6.21 us
  transfers between devices with their start and end apart: 17, of which 9 were waited for; matrix products, arithmetic and copies ran while one was open for 11% of the time, Pallas kernels for 13%

profile of v7, /device:TPU:1, one launch (start us, length us, event | category | flops | bytes accessed | tf_op | source)
XLA Modules:
  0.0 107.9 jit_solution(16866291211490836060)
XLA Ops:
  0.0 2.0 %collective-permute-start.2 = (bf16[4,256,384]{2,1,0:T(8,128)(2,1)}, bf16[4,256,384]{2,1,0:T(8,128)(2,1)S(1)}, u32[]{:S(2)}, u32[]{:S(2)}) collective-permute-start(bf16[4,256,384]{2,1,0:T(8,128)(2,1)} %own.3), channel_id=1, source_target_pairs={{0,1},{1,2},{2,3},{3,0},{4,5},{5,6},{6,7},{7,4},{8,9},{9,10},{10,1... | collective-permute-start | bytes 2359304 | tf_op jit(solution)/shard_map/ppermute | solution.py:347
  2.0 1.4 %collective-permute-start = (bf16[4,256,384]{2,1,0:T(8,128)(2,1)}, bf16[4,256,384]{2,1,0:T(8,128)(2,1)}, u32[]{:S(2)}, u32[]{:S(2)}) collective-permute-start(bf16[4,256,384]{2,1,0:T(8,128)(2,1)} %own.3), channel_id=1, source_target_pairs={{0,3},{1,0},{2,1},{3,2},{4,7},{5,4},{6,5},{7,6},{8,11},{9,8},{10,9... | collective-permute-start | bytes 2359304 | tf_op jit(solution)/shard_map/ppermute | solution.py:347
  5.5 1.2 %copy-done.1 = bf16[768,3,192]{0,2,1:T(8,128)(2,1)S(1)} copy-done((bf16[768,3,192]{0,2,1:T(8,128)(2,1)S(1)}, bf16[768,3,192]{0,2,1:T(8,128)(2,1)}, u32[]{:S(2)}) %copy-start.1) | copy-done | bytes 884760
  6.6 0.9 copy-done.3
  7.6 1.3 %slide_project.1 = (f32[128,192]{1,0:T(8,128)S(1)}, bf16[256,384]{1,0:T(8,128)(2,1)S(1)}) custom-call(s32[7]{0:T(128)S(1)} %pad_add_fusion.idx, bf16[128,768]{1,0:T(8,128)(2,1)S(1)} %copy-done.3, f32[1,768]{1,0:T(1,128)S(1)} %reshape.31.gain, bf16[576,768]{1,0:T(8,128)(2,1)S(1)} %bitcast.18), custom_call_target="tpu_custom_call" | custom-call | tf_op jit(solution)/shard_map/slide_project/pallas_call | solution.py:192
  9.5 1.8 %collective-permute-start.4 = (bf16[1,256,384]{2,1,0:T(8,128)(2,1)S(1)}, bf16[1,256,384]{2,1,0:T(8,128)(2,1)S(1)}, u32[]{:S(2)}, u32[]{:S(2)}) collective-permute-start(bf16[1,256,384]{2,1,0:T(8,128)(2,1)S(1)} %bitcast.20), channel_id=1, source_target_pairs={{0,8},{4,12},{8,0},{12,4},{16,24},{20,28},{24,16},{28,20},{32,40},... | collective-permute-start | bytes 589832 | tf_op jit(solution)/shard_map/ppermute | solution.py:351
  11.3 3.2 %convolution_convert_fusion = bf16[384,768]{1,0:T(8,128)(2,1)} fusion(bf16[384,1536]{1,0:T(8,128)(2,1)} %param.16, bf16[1536,768]{1,0:T(8,128)(2,1)S(1)} %copy-done), kind=kOutput, calls=%fused_computation | convolution fusion | flops 906264576 | bytes 4128768 | tf_op jit(solution)/shard_map/dot_general | solution.py:31
  14.8 3.6 %collective-permute-start.5 = (bf16[2,128,384]{2,1,0:T(8,128)(2,1)S(1)}, bf16[2,128,384]{2,1,0:T(8,128)(2,1)S(1)}, u32[]{:S(2)}, u32[]{:S(2)}) collective-permute-start(bf16[2,128,384]{2,1,0:T(8,128)(2,1)S(1)} %get-tuple-element.50), channel_id=1, source_target_pairs={{0,16},{4,20},{8,24},{12,28},{16,0},{20,4},{24,8},{28,12},{32,48},... | collective-permute-start | bytes 589832 | tf_op jit(solution)/shard_map/ppermute | solution.py:351
  18.5 2.1 %collective-permute-start.3 = (bf16[2,256,384]{2,1,0:T(8,128)(2,1)S(1)}, bf16[2,256,384]{2,1,0:T(8,128)(2,1)S(1)}, u32[]{:S(2)}, u32[]{:S(2)}) collective-permute-start(bf16[2,256,384]{2,1,0:T(8,128)(2,1)S(1)} %slice.41), channel_id=1, source_target_pairs={{0,1},{1,2},{2,3},{3,0},{4,5},{5,6},{6,7},{7,4},{8,9},{9,10},{10,1... | collective-permute-start | bytes 1179656 | tf_op jit(solution)/shard_map/ppermute | solution.py:347
  21.4 5.5 %collective-permute-done.5 = bf16[2,128,384]{2,1,0:T(8,128)(2,1)S(1)} collective-permute-done((bf16[2,128,384]{2,1,0:T(8,128)(2,1)S(1)}, bf16[2,128,384]{2,1,0:T(8,128)(2,1)S(1)}, u32[]{:S(2)}, u32[]{:S(2)}) %collective-permute-start.5) | collective-permute-done | bytes 196640 | tf_op jit(solution)/shard_map/ppermute | solution.py:351
  27.6 1.0 slice.40
  28.7 1.4 %collective-permute-start.1 = (bf16[2,256,384]{2,1,0:T(8,128)(2,1)S(1)}, bf16[2,256,384]{2,1,0:T(8,128)(2,1)S(1)}, u32[]{:S(2)}, u32[]{:S(2)}) collective-permute-start(bf16[2,256,384]{2,1,0:T(8,128)(2,1)S(1)} %slice.40), channel_id=1, source_target_pairs={{0,3},{1,0},{2,1},{3,2},{4,7},{5,4},{6,5},{7,6},{8,11},{9,8},{10,9... | collective-permute-start | bytes 1179656 | tf_op jit(solution)/shard_map/ppermute | solution.py:347
  30.0 7.9 %collective-permute-start.6 = (bf16[4,64,384]{2,1,0:T(8,128)(2,1)S(1)}, bf16[4,64,384]{2,1,0:T(8,128)(2,1)S(1)}, u32[]{:S(2)}, u32[]{:S(2)}) collective-permute-start(bf16[4,64,384]{2,1,0:T(8,128)(2,1)S(1)} %get-tuple-element.28), channel_id=1, source_target_pairs={{0,32},{4,36},{8,40},{12,44},{16,48},{20,52},{24,56},{28,60},{32,0... | collective-permute-start | bytes 589832 | tf_op jit(solution)/shard_map/ppermute | solution.py:351
  38.0 5.7 %encode.2 = f32[2,768]{1,0:T(2,128)S(1)} custom-call(s32[7]{0:T(128)S(1)} %pad_add_fusion.idx, bf16[4,256,384]{2,1,0:T(8,128)(2,1)S(1)} %copy-done.7, bf16[4,256,384]{2,1,0:T(8,128)(2,1)S(1)} %collective-permute-done.2.left, bf16[4,256,384]{2,1,0:T(8,128)(2,1)} %collective-permute-done.right, bf16[2,256,384]{2,1,0:T(8,128)(2,1)S(1)} %collective-permute-done.3.far, ...), custom_call_target="tpu_custom_call" | custom-call | flops 6000000000 | bytes 8000000 | tf_op jit(solution)/shard_map/encode/pallas_call | solution.py:92
  43.7 5.7 %encode.3 = f32[2,768]{1,0:T(2,128)S(1)} custom-call(s32[7]{0:T(128)S(1)} %pad_add_fusion.idx, bf16[4,256,384]{2,1,0:T(8,128)(2,1)S(1)} %copy-done.7, bf16[4,256,384]{2,1,0:T(8,128)(2,1)S(1)} %collective-permute-done.2.left, bf16[4,256,384]{2,1,0:T(8,128)(2,1)} %collective-permute-done.right, bf16[2,256,384]{2,1,0:T(8,128)(2,1)S(1)} %collective-permute-done.1.far, ...), custom_call_target="tpu_custom_call" | custom-call | flops 6000000000 | bytes 8000000 | tf_op jit(solution)/shard_map/encode/pallas_call | solution.py:92
  49.5 1.4 %collective-permute-start.10 = (bf16[8,32,384]{2,1,0:T(8,128)(2,1)S(1)}, bf16[8,32,384]{2,1,0:T(8,128)(2,1)S(1)}, u32[]{:S(2)}, u32[]{:S(2)}) collective-permute-start(bf16[8,32,384]{2,1,0:T(8,128)(2,1)S(1)} %get-tuple-element.32), channel_id=1, source_target_pairs={{0,64},{4,68},{8,72},{12,76},{16,80},{20,84},{24,88},{28,92},{32,9... | collective-permute-start | bytes 589832 | tf_op jit(solution)/shard_map/ppermute | solution.py:351
  51.2 2.7 %collective-permute-start.8 = (f32[4,768]{1,0:T(4,128)S(1)}, f32[4,768]{1,0:T(4,128)S(1)}, u32[]{:S(2)}, u32[]{:S(2)}) collective-permute-start(f32[4,768]{1,0:T(4,128)S(1)} %fusion.2.a), channel_id=1, source_target_pairs={{0,3},{1,0},{2,1},{3,2},{4,7},{5,4},{6,5},{7,6},{8,11},{9,8},{10,9... | collective-permute-start | bytes 36872 | tf_op jit(solution)/shard_map/ppermute | solution.py:347
  54.9 3.0 %collective-permute-done.9.d = f32[4,768]{1,0:T(4,128)S(1)} collective-permute-done((f32[4,768]{1,0:T(4,128)S(1)}, f32[4,768]{1,0:T(4,128)S(1)}, u32[]{:S(2)}, u32[]{:S(2)}) %collective-permute-start.9) | collective-permute-done | bytes 12320 | tf_op jit(solution)/shard_map/ppermute | solution.py:347
  57.9 2.6 %collective-permute-start.11 = (bf16[16,16,384]{2,1,0:T(8,128)(2,1)S(1)}, bf16[16,16,384]{2,1,0:T(8,128)(2,1)S(1)}, u32[]{:S(2)}, u32[]{:S(2)}) collective-permute-start(bf16[16,16,384]{2,1,0:T(8,128)(2,1)S(1)} %get-tuple-element.38), channel_id=1, source_target_pairs={{0,128},{4,132},{8,136},{12,140},{16,144},{20,148},{24,152},{28,15... | collective-permute-start | bytes 589832 | tf_op jit(solution)/shard_map/ppermute | solution.py:351
  61.9 2.0 %collective-permute-done.11 = bf16[16,16,384]{2,1,0:T(8,128)(2,1)S(1)} collective-permute-done((bf16[16,16,384]{2,1,0:T(8,128)(2,1)S(1)}, bf16[16,16,384]{2,1,0:T(8,128)(2,1)S(1)}, u32[]{:S(2)}, u32[]{:S(2)}) %collective-permute-start.11) | collective-permute-done | bytes 196640 | tf_op jit(solution)/shard_map/ppermute | solution.py:351
  64.8 5.9 %collective-permute-start.12 = (bf16[1536,384]{1,0:T(8,128)(2,1)}, bf16[1536,384]{1,0:T(8,128)(2,1)}, u32[]{:S(2)}, u32[]{:S(2)}) collective-permute-start(bf16[1536,384]{1,0:T(8,128)(2,1)} %constant_dynamic-update-slice_fusion.4.refs_2_), channel_id=1, source_target_pairs={{0,4},{4,0},{8,12},{12,8},{16,20},{20,16},{24,28},{28,24},{32,36},... | collective-permute-start | bytes 3538952 | tf_op jit(solution)/shard_map/ppermute | solution.py:351
  70.7 1.0 embed_rows.1
  71.7 0.8 broadcast_in_dim.10
  72.5 6.2 %all-to-all-start = ((bf16[64,4,640]{2,1,0:T(4,128)(2,1)}), bf16[64,4,640]{2,1,0:T(4,128)(2,1)S(1)}, u32[]{:S(2)}, u32[]{:S(2)}) async-start(bf16[64,4,640]{2,1,0:T(4,128)(2,1)} %broadcast_in_dim.10), calls=%async_computation | async-start | bytes 655360 | tf_op jit(solution)/shard_map/all_to_all | solution.py:409
  79.1 0.8 copy.16
  79.9 12.1 %all-to-all-done = bf16[64,4,640]{2,1,0:T(4,128)(2,1)S(1)} async-done(((bf16[64,4,640]{2,1,0:T(4,128)(2,1)}), bf16[64,4,640]{2,1,0:T(4,128)(2,1)S(1)}, u32[]{:S(2)}, u32[]{:S(2)}) %all-to-all-start) | async-done | bytes 327712 | tf_op jit(solution)/shard_map/all_to_all | solution.py:409
  92.0 0.8 reshape.34.refs_0_
  92.8 6.9 %attend.1 = (bf16[128,192]{1,0:T(8,128)(2,1)}, bf16[128,192]{1,0:T(8,128)(2,1)}, bf16[128,192]{1,0:T(8,128)(2,1)}, bf16[128,192]{1,0:T(8,128)(2,1)}) custom-call(s32[7]{0:T(128)} %copy-done.5, bf16[256,640]{1,0:T(8,128)(2,1)} %reshape.34.refs_0_, f32[128,192]{1,0:T(8,128)} %copy-done.4, bf16[1536,384]{1,0:T(8,128)(2,1)} %constant_dynamic-update-slice_fusion.4.refs_2_, ...), custom_call_target="tpu_custom_call" | custom-call | tf_op jit(solution)/shard_map/attend/pallas_call | solution.py:328
  99.8 1.1 %collective-permute-start.14 = (bf16[128,192]{1,0:T(8,128)(2,1)}, bf16[128,192]{1,0:T(8,128)(2,1)S(1)}, u32[]{:S(2)}, u32[]{:S(2)}) collective-permute-start(bf16[128,192]{1,0:T(8,128)(2,1)} %get-tuple-element.41), channel_id=1, source_target_pairs={{0,2},{1,3},{2,0},{3,1},{4,6},{5,7},{6,4},{7,5},{8,10},{9,11},{10,... | collective-permute-start | bytes 147464 | tf_op jit(solution)/shard_map/ppermute | solution.py:347
  100.9 1.5 %collective-permute-start.15 = (bf16[128,192]{1,0:T(8,128)(2,1)}, bf16[128,192]{1,0:T(8,128)(2,1)S(1)}, u32[]{:S(2)}, u32[]{:S(2)}) collective-permute-start(bf16[128,192]{1,0:T(8,128)(2,1)} %get-tuple-element.42), channel_id=1, source_target_pairs={{0,3},{1,0},{2,1},{3,2},{4,7},{5,4},{6,5},{7,6},{8,11},{9,8},{10,9... | collective-permute-start | bytes 147464 | tf_op jit(solution)/shard_map/ppermute | solution.py:347
  102.5 3.8 %collective-permute-done.13 = bf16[128,192]{1,0:T(8,128)(2,1)S(1)} collective-permute-done((bf16[128,192]{1,0:T(8,128)(2,1)}, bf16[128,192]{1,0:T(8,128)(2,1)S(1)}, u32[]{:S(2)}, u32[]{:S(2)}) %collective-permute-start.13) | collective-permute-done | bytes 49184 | tf_op jit(solution)/shard_map/ppermute | solution.py:347
  106.2 0.9 add_convert_fusion
  (60 shorter events, 8.9 us)
Async XLA Ops:
  0.0 11.3 %copy-start = (bf16[1536,768]{1,0:T(8,128)(2,1)S(1)}, bf16[1536,768]{1,0:T(8,128)(2,1)}, u32[]{:S(2)}) copy-start(bf16[1536,768]{1,0:T(8,128)(2,1)} %param.17) | copy-start | bytes 7077892
  0.0 18.5 %collective-permute-start.2 = (bf16[4,256,384]{2,1,0:T(8,128)(2,1)}, bf16[4,256,384]{2,1,0:T(8,128)(2,1)S(1)}, u32[]{:S(2)}, u32[]{:S(2)}) collective-permute-start(bf16[4,256,384]{2,1,0:T(8,128)(2,1)} %own.3), channel_id=1, source_target_pairs={{0,1},{1,2},{2,3},{3,0},{4,5},{5,6},{6,7},{7,4},{8,9},{9,10},{10,1... | collective-permute-start | bytes 2359304 | tf_op jit(solution)/shard_map/ppermute | solution.py:347
  2.0 25.6 %collective-permute-start = (bf16[4,256,384]{2,1,0:T(8,128)(2,1)}, bf16[4,256,384]{2,1,0:T(8,128)(2,1)}, u32[]{:S(2)}, u32[]{:S(2)}) collective-permute-start(bf16[4,256,384]{2,1,0:T(8,128)(2,1)} %own.3), channel_id=1, source_target_pairs={{0,3},{1,0},{2,1},{3,2},{4,7},{5,4},{6,5},{7,6},{8,11},{9,8},{10,9... | collective-permute-start | bytes 2359304 | tf_op jit(solution)/shard_map/ppermute | solution.py:347
  5.5 65.2 %copy-start.5 = (s32[7]{0:T(128)}, s32[7]{0:T(128)S(1)}, u32[]{:S(2)}) copy-start(s32[7]{0:T(128)S(1)} %pad_add_fusion.idx) | copy-start | bytes 88
  5.5 1.2 %copy-start.1 = (bf16[768,3,192]{0,2,1:T(8,128)(2,1)S(1)}, bf16[768,3,192]{0,2,1:T(8,128)(2,1)}, u32[]{:S(2)}) copy-start(bf16[768,3,192]{0,2,1:T(8,128)(2,1)} %param.20) | copy-start | bytes 2654212
  6.6 0.9 copy-start.3
  8.9 0.6 copy-start.4
  9.5 5.2 %collective-permute-start.4 = (bf16[1,256,384]{2,1,0:T(8,128)(2,1)S(1)}, bf16[1,256,384]{2,1,0:T(8,128)(2,1)S(1)}, u32[]{:S(2)}, u32[]{:S(2)}) collective-permute-start(bf16[1,256,384]{2,1,0:T(8,128)(2,1)S(1)} %bitcast.20), channel_id=1, source_target_pairs={{0,8},{4,12},{8,0},{12,4},{16,24},{20,28},{24,16},{28,20},{32,40},... | collective-permute-start | bytes 589832 | tf_op jit(solution)/shard_map/ppermute | solution.py:351
  14.5 6.1 %copy-start.8 = (bf16[384,768]{1,0:T(8,128)(2,1)S(1)}, bf16[384,768]{1,0:T(8,128)(2,1)}, u32[]{:S(2)}) copy-start(bf16[384,768]{1,0:T(8,128)(2,1)} %convolution_convert_fusion) | copy-start | bytes 1769476
  14.8 12.1 %collective-permute-start.5 = (bf16[2,128,384]{2,1,0:T(8,128)(2,1)S(1)}, bf16[2,128,384]{2,1,0:T(8,128)(2,1)S(1)}, u32[]{:S(2)}, u32[]{:S(2)}) collective-permute-start(bf16[2,128,384]{2,1,0:T(8,128)(2,1)S(1)} %get-tuple-element.50), channel_id=1, source_target_pairs={{0,16},{4,20},{8,24},{12,28},{16,0},{20,4},{24,8},{28,12},{32,48},... | collective-permute-start | bytes 589832 | tf_op jit(solution)/shard_map/ppermute | solution.py:351
  18.5 2.2 %copy-start.10 = (f32[1536]{0:T(1024)S(1)}, f32[1536]{0:T(1024)}, u32[]{:S(2)}) copy-start(f32[1536]{0:T(1024)} %param.14) | copy-start | bytes 18436
  18.5 11.5 %collective-permute-start.3 = (bf16[2,256,384]{2,1,0:T(8,128)(2,1)S(1)}, bf16[2,256,384]{2,1,0:T(8,128)(2,1)S(1)}, u32[]{:S(2)}, u32[]{:S(2)}) collective-permute-start(bf16[2,256,384]{2,1,0:T(8,128)(2,1)S(1)} %slice.41), channel_id=1, source_target_pairs={{0,1},{1,2},{2,3},{3,0},{4,5},{5,6},{6,7},{7,4},{8,9},{9,10},{10,1... | collective-permute-start | bytes 1179656 | tf_op jit(solution)/shard_map/ppermute | solution.py:347
  20.6 17.4 %copy-start.6 = (bf16[1536,3,384]{2,0,1:T(8,128)(2,1)S(1)}, bf16[1536,3,384]{2,0,1:T(8,128)(2,1)}, u32[]{:S(2)}) copy-start(bf16[1536,3,384]{2,0,1:T(8,128)(2,1)} %param.15) | copy-start | bytes 10616836
  20.7 17.3 %copy-start.7 = (bf16[4,256,384]{2,1,0:T(8,128)(2,1)S(1)}, bf16[4,256,384]{2,1,0:T(8,128)(2,1)}, u32[]{:S(2)}) copy-start(bf16[4,256,384]{2,1,0:T(8,128)(2,1)} %own.3) | copy-start | bytes 2359300
  28.7 15.0 %collective-permute-start.1 = (bf16[2,256,384]{2,1,0:T(8,128)(2,1)S(1)}, bf16[2,256,384]{2,1,0:T(8,128)(2,1)S(1)}, u32[]{:S(2)}, u32[]{:S(2)}) collective-permute-start(bf16[2,256,384]{2,1,0:T(8,128)(2,1)S(1)} %slice.40), channel_id=1, source_target_pairs={{0,3},{1,0},{2,1},{3,2},{4,7},{5,4},{6,5},{7,6},{8,11},{9,8},{10,9... | collective-permute-start | bytes 1179656 | tf_op jit(solution)/shard_map/ppermute | solution.py:347
  30.0 19.4 %collective-permute-start.6 = (bf16[4,64,384]{2,1,0:T(8,128)(2,1)S(1)}, bf16[4,64,384]{2,1,0:T(8,128)(2,1)S(1)}, u32[]{:S(2)}, u32[]{:S(2)}) collective-permute-start(bf16[4,64,384]{2,1,0:T(8,128)(2,1)S(1)} %get-tuple-element.28), channel_id=1, source_target_pairs={{0,32},{4,36},{8,40},{12,44},{16,48},{20,52},{24,56},{28,60},{32,0... | collective-permute-start | bytes 589832 | tf_op jit(solution)/shard_map/ppermute | solution.py:351
  49.5 4.6 %collective-permute-start.10 = (bf16[8,32,384]{2,1,0:T(8,128)(2,1)S(1)}, bf16[8,32,384]{2,1,0:T(8,128)(2,1)S(1)}, u32[]{:S(2)}, u32[]{:S(2)}) collective-permute-start(bf16[8,32,384]{2,1,0:T(8,128)(2,1)S(1)} %get-tuple-element.32), channel_id=1, source_target_pairs={{0,64},{4,68},{8,72},{12,76},{16,80},{20,84},{24,88},{28,92},{32,9... | collective-permute-start | bytes 589832 | tf_op jit(solution)/shard_map/ppermute | solution.py:351
  51.2 3.8 %collective-permute-start.7 = (f32[4,768]{1,0:T(4,128)S(1)}, f32[4,768]{1,0:T(4,128)S(1)}, u32[]{:S(2)}, u32[]{:S(2)}) collective-permute-start(f32[4,768]{1,0:T(4,128)S(1)} %fusion.2.a), channel_id=1, source_target_pairs={{0,1},{1,2},{2,3},{3,0},{4,5},{5,6},{6,7},{7,4},{8,9},{9,10},{10,1... | collective-permute-start | bytes 36872 | tf_op jit(solution)/shard_map/ppermute | solution.py:347
  51.2 3.8 %collective-permute-start.8 = (f32[4,768]{1,0:T(4,128)S(1)}, f32[4,768]{1,0:T(4,128)S(1)}, u32[]{:S(2)}, u32[]{:S(2)}) collective-permute-start(f32[4,768]{1,0:T(4,128)S(1)} %fusion.2.a), channel_id=1, source_target_pairs={{0,3},{1,0},{2,1},{3,2},{4,7},{5,4},{6,5},{7,6},{8,11},{9,8},{10,9... | collective-permute-start | bytes 36872 | tf_op jit(solution)/shard_map/ppermute | solution.py:347
  53.8 4.0 %collective-permute-start.9 = (f32[4,768]{1,0:T(4,128)S(1)}, f32[4,768]{1,0:T(4,128)S(1)}, u32[]{:S(2)}, u32[]{:S(2)}) collective-permute-start(f32[4,768]{1,0:T(4,128)S(1)} %fusion.2.a), channel_id=1, source_target_pairs={{0,2},{1,3},{2,0},{3,1},{4,6},{5,7},{6,4},{7,5},{8,10},{9,11},{10,... | collective-permute-start | bytes 36872 | tf_op jit(solution)/shard_map/ppermute | solution.py:347
  57.9 6.0 %collective-permute-start.11 = (bf16[16,16,384]{2,1,0:T(8,128)(2,1)S(1)}, bf16[16,16,384]{2,1,0:T(8,128)(2,1)S(1)}, u32[]{:S(2)}, u32[]{:S(2)}) collective-permute-start(bf16[16,16,384]{2,1,0:T(8,128)(2,1)S(1)} %get-tuple-element.38), channel_id=1, source_target_pairs={{0,128},{4,132},{8,136},{12,140},{16,144},{20,148},{24,152},{28,15... | collective-permute-start | bytes 589832 | tf_op jit(solution)/shard_map/ppermute | solution.py:351
  60.5 10.2 %copy-start.2 = (bf16[768,3,192]{0,2,1:T(8,128)(2,1)S(1)}, bf16[768,3,192]{0,2,1:T(8,128)(2,1)}, u32[]{:S(2)}) copy-start(bf16[768,3,192]{0,2,1:T(8,128)(2,1)} %param.20) | copy-start | bytes 2654212
  64.0 14.7 %copy-start.9 = (bf16[192,768]{1,0:T(8,128)(2,1)S(1)}, bf16[192,768]{1,0:T(8,128)(2,1)}, u32[]{:S(2)}) copy-start(bf16[192,768]{1,0:T(8,128)(2,1)} %param.21) | copy-start | bytes 884740
  64.8 28.0 %collective-permute-start.12 = (bf16[1536,384]{1,0:T(8,128)(2,1)}, bf16[1536,384]{1,0:T(8,128)(2,1)}, u32[]{:S(2)}, u32[]{:S(2)}) collective-permute-start(bf16[1536,384]{1,0:T(8,128)(2,1)} %constant_dynamic-update-slice_fusion.4.refs_2_), channel_id=1, source_target_pairs={{0,4},{4,0},{8,12},{12,8},{16,20},{20,16},{24,28},{28,24},{32,36},... | collective-permute-start | bytes 3538952 | tf_op jit(solution)/shard_map/ppermute | solution.py:351
  72.5 19.5 %all-to-all-start = ((bf16[64,4,640]{2,1,0:T(4,128)(2,1)}), bf16[64,4,640]{2,1,0:T(4,128)(2,1)S(1)}, u32[]{:S(2)}, u32[]{:S(2)}) async-start(bf16[64,4,640]{2,1,0:T(4,128)(2,1)} %broadcast_in_dim.10), calls=%async_computation | async-start | bytes 655360 | tf_op jit(solution)/shard_map/all_to_all | solution.py:409
  99.7 6.5 %collective-permute-start.13 = (bf16[128,192]{1,0:T(8,128)(2,1)}, bf16[128,192]{1,0:T(8,128)(2,1)S(1)}, u32[]{:S(2)}, u32[]{:S(2)}) collective-permute-start(bf16[128,192]{1,0:T(8,128)(2,1)} %get-tuple-element.40), channel_id=1, source_target_pairs={{0,1},{1,2},{2,3},{3,0},{4,5},{5,6},{6,7},{7,4},{8,9},{9,10},{10,1... | collective-permute-start | bytes 147464 | tf_op jit(solution)/shard_map/ppermute | solution.py:347
  99.8 6.5 %collective-permute-start.14 = (bf16[128,192]{1,0:T(8,128)(2,1)}, bf16[128,192]{1,0:T(8,128)(2,1)S(1)}, u32[]{:S(2)}, u32[]{:S(2)}) collective-permute-start(bf16[128,192]{1,0:T(8,128)(2,1)} %get-tuple-element.41), channel_id=1, source_target_pairs={{0,2},{1,3},{2,0},{3,1},{4,6},{5,7},{6,4},{7,5},{8,10},{9,11},{10,... | collective-permute-start | bytes 147464 | tf_op jit(solution)/shard_map/ppermute | solution.py:347
  100.9 5.3 %collective-permute-start.15 = (bf16[128,192]{1,0:T(8,128)(2,1)}, bf16[128,192]{1,0:T(8,128)(2,1)S(1)}, u32[]{:S(2)}, u32[]{:S(2)}) collective-permute-start(bf16[128,192]{1,0:T(8,128)(2,1)} %get-tuple-element.42), channel_id=1, source_target_pairs={{0,3},{1,0},{2,1},{3,2},{4,7},{5,4},{6,5},{7,6},{8,11},{9,8},{10,9... | collective-permute-start | bytes 147464 | tf_op jit(solution)/shard_map/ppermute | solution.py:347

commit v8 on v7

--- a/solution.py
+++ b/solution.py
@@ -385,8 +385,6 @@
 
     def step(have, level):
         have = jnp.concatenate([have, swap_seq(have, 2 << level)], axis=0)
-        if level == BRANCHES - 1:
-            return have
         n = ROWS >> level
         kept.append(have[:, 0:n].reshape(-1, 2 * hw))
         return have[:, n:]
@@ -400,10 +398,12 @@
     first, second, have = lax.optimization_barrier((first, second, have))
     partial = dot(jnp.concatenate([first, second], axis=0).astype(BF), joined)
     shares = [partial] + [shift_mp(partial, k) for k in (1, 3, 2)]
-    have = step(have, 3)
-    shares, have = lax.optimization_barrier((shares, have))
-    have = step(have, 4)
-    mine = jnp.concatenate(kept + [have.reshape(-1, 2 * hw)], axis=0)
+    last = have[:, 16:]
+    across = [swap_seq(have, 16), swap_seq(last, 32), swap_seq(last, 48)]
+    shares, across = lax.optimization_barrier((shares, across))
+    kept += [x[:, 0:16].reshape(-1, 2 * hw) for x in (have, across[0])]
+    kept += [x.reshape(-1, 2 * hw) for x in (last, across[0][:, 16:], across[1], across[2])]
+    mine = jnp.concatenate(kept, axis=0)
     theirs = swap_seq(mine, 1)
     emb = embed_rows(idx, shares, gain_row, slide_w)
     emb = lax.all_to_all(jnp.broadcast_to(emb[None], (64,) + emb.shape), "seq", 0, 0)

time: 108 us -> 113 us (1.046)
  local copies, waits for them, and re-layouts: 11.8 us -> 14.3 us
  starting transfers between devices: 41.7 us -> 43.7 us
    unnamed x28 -> x31, local copies, waits for them, and re-layouts: 5.59 us -> 8.14 us
    ppermute x10, starting transfers between devices: 12.3 us -> 14.7 us  [shift_mp(): return lax.ppermute(x, 'mp', [(i, (i + k) % 4) for i in range(4)])]
    ppermute x6 -> x7, waiting for transfers between devices: 7.92 us -> 9.75 us  [swap_seq(): return lax.ppermute(x, 'seq', [(i, i ^ bit) for i in range(64)])]
    ppermute x6 -> x7, starting transfers between devices: 23.2 us -> 21.4 us  [swap_seq(): return lax.ppermute(x, 'seq', [(i, i ^ bit) for i in range(64)])]
    all_to_all x1, starting transfers between devices: 6.21 us -> 7.61 us  [local(): lax.all_to_all(jnp.broadcast_to(emb[None], (64,) + emb.shape), 'seq', 0, 0)]
    ppermute x10, waiting for transfers between devices: 7.61 us -> 6.24 us  [shift_mp(): return lax.ppermute(x, 'mp', [(i, (i + k) % 4) for i in range(4)])]
  transfers between devices with their start and end apart: 17 -> 18, of which waited for: 9 -> 9; matrix products, arithmetic and copies ran while one was open for 11% -> 10% of each run, Pallas kernels for 13% -> 12%
where the time goes in v8:
time: 113 us
  starting transfers between devices  43.7 us (39%)
  waiting for transfers between devices  28 us (25%)
  Pallas kernels  20.7 us (18%)
  local copies, waits for them, and re-layouts  14.3 us (13%)
  matrix products  3.44 us (3%)
  other arithmetic  1.78 us (2%)
    ppermute x7, starting transfers between devices, swap_seq(): return lax.ppermute(x, 'seq', [(i, i ^ bit) for i in range(64)])  21.4 us
    ppermute x10, starting transfers between devices, shift_mp(): return lax.ppermute(x, 'mp', [(i, (i + k) % 4) for i in range(4)])  14.7 us
    all_to_all x1, waiting for transfers between devices, local(): lax.all_to_all(jnp.broadcast_to(emb[None], (64,) + emb.shape), 'seq', 0, 0)  12.1 us
    pallas_call x2, Pallas kernels, encode(): pl.pallas_call(encode_kernel, grid=(1,), out_shape=jax.ShapeDtypeStruct((...  11.5 us
    ppermute x7, waiting for transfers between devices, swap_seq(): return lax.ppermute(x, 'seq', [(i, i ^ bit) for i in range(64)])  9.75 us
    unnamed x31, local copies, waits for them, and re-layouts  8.14 us
    all_to_all x1, starting transfers between devices, local(): lax.all_to_all(jnp.broadcast_to(emb[None], (64,) + emb.shape), 'seq', 0, 0)  7.61 us
    pallas_call x1, Pallas kernels, attend(): pl.pallas_call(attend_kernel, out_shape=(jax.ShapeDtypeStruct((ROWS, hw),...  6.92 us
  transfers between devices with their start and end apart: 18, of which 9 were waited for; matrix products, arithmetic and copies ran while one was open for 10% of the time, Pallas kernels for 12%

profile of v8, /device:TPU:1, one launch (start us, length us, event | category | flops | bytes accessed | tf_op | source)
XLA Modules:
  0.0 112.8 jit_solution(1666143513576114474)
XLA Ops:
  0.0 2.0 %collective-permute-start.2 = (bf16[4,256,384]{2,1,0:T(8,128)(2,1)}, bf16[4,256,384]{2,1,0:T(8,128)(2,1)S(1)}, u32[]{:S(2)}, u32[]{:S(2)}) collective-permute-start(bf16[4,256,384]{2,1,0:T(8,128)(2,1)} %own.3), channel_id=1, source_target_pairs={{0,1},{1,2},{2,3},{3,0},{4,5},{5,6},{6,7},{7,4},{8,9},{9,10},{10,1... | collective-permute-start | bytes 2359304 | tf_op jit(solution)/shard_map/ppermute | solution.py:347
  2.0 1.4 %collective-permute-start = (bf16[4,256,384]{2,1,0:T(8,128)(2,1)}, bf16[4,256,384]{2,1,0:T(8,128)(2,1)}, u32[]{:S(2)}, u32[]{:S(2)}) collective-permute-start(bf16[4,256,384]{2,1,0:T(8,128)(2,1)} %own.3), channel_id=1, source_target_pairs={{0,3},{1,0},{2,1},{3,2},{4,7},{5,4},{6,5},{7,6},{8,11},{9,8},{10,9... | collective-permute-start | bytes 2359304 | tf_op jit(solution)/shard_map/ppermute | solution.py:347
  5.5 1.2 %copy-done.1 = bf16[768,3,192]{0,2,1:T(8,128)(2,1)S(1)} copy-done((bf16[768,3,192]{0,2,1:T(8,128)(2,1)S(1)}, bf16[768,3,192]{0,2,1:T(8,128)(2,1)}, u32[]{:S(2)}) %copy-start.1) | copy-done | bytes 884760
  6.6 0.9 copy-done.3
  7.6 1.3 %slide_project.1 = (f32[128,192]{1,0:T(8,128)S(1)}, bf16[256,384]{1,0:T(8,128)(2,1)S(1)}) custom-call(s32[7]{0:T(128)S(1)} %pad_add_fusion.idx, bf16[128,768]{1,0:T(8,128)(2,1)S(1)} %copy-done.3, f32[1,768]{1,0:T(1,128)S(1)} %reshape.43.gain, bf16[576,768]{1,0:T(8,128)(2,1)S(1)} %bitcast.22), custom_call_target="tpu_custom_call" | custom-call | tf_op jit(solution)/shard_map/slide_project/pallas_call | solution.py:192
  9.6 1.8 %collective-permute-start.4 = (bf16[1,256,384]{2,1,0:T(8,128)(2,1)S(1)}, bf16[1,256,384]{2,1,0:T(8,128)(2,1)S(1)}, u32[]{:S(2)}, u32[]{:S(2)}) collective-permute-start(bf16[1,256,384]{2,1,0:T(8,128)(2,1)S(1)} %bitcast.24), channel_id=1, source_target_pairs={{0,8},{4,12},{8,0},{12,4},{16,24},{20,28},{24,16},{28,20},{32,40},... | collective-permute-start | bytes 589832 | tf_op jit(solution)/shard_map/ppermute | solution.py:351
  11.3 3.2 %convolution_convert_fusion = bf16[384,768]{1,0:T(8,128)(2,1)} fusion(bf16[384,1536]{1,0:T(8,128)(2,1)} %param.16, bf16[1536,768]{1,0:T(8,128)(2,1)S(1)} %copy-done), kind=kOutput, calls=%fused_computation | convolution fusion | flops 906264576 | bytes 4128768 | tf_op jit(solution)/shard_map/dot_general | solution.py:31
  14.8 3.6 %collective-permute-start.5 = (bf16[2,128,384]{2,1,0:T(8,128)(2,1)S(1)}, bf16[2,128,384]{2,1,0:T(8,128)(2,1)S(1)}, u32[]{:S(2)}, u32[]{:S(2)}) collective-permute-start(bf16[2,128,384]{2,1,0:T(8,128)(2,1)S(1)} %get-tuple-element.52), channel_id=1, source_target_pairs={{0,16},{4,20},{8,24},{12,28},{16,0},{20,4},{24,8},{28,12},{32,48},... | collective-permute-start | bytes 589832 | tf_op jit(solution)/shard_map/ppermute | solution.py:351
  18.5 2.1 %collective-permute-start.3 = (bf16[2,256,384]{2,1,0:T(8,128)(2,1)S(1)}, bf16[2,256,384]{2,1,0:T(8,128)(2,1)S(1)}, u32[]{:S(2)}, u32[]{:S(2)}) collective-permute-start(bf16[2,256,384]{2,1,0:T(8,128)(2,1)S(1)} %slice.49), channel_id=1, source_target_pairs={{0,1},{1,2},{2,3},{3,0},{4,5},{5,6},{6,7},{7,4},{8,9},{9,10},{10,1... | collective-permute-start | bytes 1179656 | tf_op jit(solution)/shard_map/ppermute | solution.py:347
  21.4 5.5 %collective-permute-done.5 = bf16[2,128,384]{2,1,0:T(8,128)(2,1)S(1)} collective-permute-done((bf16[2,128,384]{2,1,0:T(8,128)(2,1)S(1)}, bf16[2,128,384]{2,1,0:T(8,128)(2,1)S(1)}, u32[]{:S(2)}, u32[]{:S(2)}) %collective-permute-start.5) | collective-permute-done | bytes 196640 | tf_op jit(solution)/shard_map/ppermute | solution.py:351
  27.7 1.0 slice.48
  28.7 1.4 %collective-permute-start.1 = (bf16[2,256,384]{2,1,0:T(8,128)(2,1)S(1)}, bf16[2,256,384]{2,1,0:T(8,128)(2,1)S(1)}, u32[]{:S(2)}, u32[]{:S(2)}) collective-permute-start(bf16[2,256,384]{2,1,0:T(8,128)(2,1)S(1)} %slice.48), channel_id=1, source_target_pairs={{0,3},{1,0},{2,1},{3,2},{4,7},{5,4},{6,5},{7,6},{8,11},{9,8},{10,9... | collective-permute-start | bytes 1179656 | tf_op jit(solution)/shard_map/ppermute | solution.py:347
  30.1 5.7 %encode.2 = f32[2,768]{1,0:T(2,128)S(1)} custom-call(s32[7]{0:T(128)S(1)} %pad_add_fusion.idx, bf16[4,256,384]{2,1,0:T(8,128)(2,1)S(1)} %copy-done.7, bf16[4,256,384]{2,1,0:T(8,128)(2,1)S(1)} %collective-permute-done.2.left, bf16[4,256,384]{2,1,0:T(8,128)(2,1)} %collective-permute-done.right, bf16[2,256,384]{2,1,0:T(8,128)(2,1)S(1)} %collective-permute-done.3.far, ...), custom_call_target="tpu_custom_call" | custom-call | flops 6000000000 | bytes 8000000 | tf_op jit(solution)/shard_map/encode/pallas_call | solution.py:92
  35.8 2.0 %collective-permute-done.1.far = bf16[2,256,384]{2,1,0:T(8,128)(2,1)S(1)} collective-permute-done((bf16[2,256,384]{2,1,0:T(8,128)(2,1)S(1)}, bf16[2,256,384]{2,1,0:T(8,128)(2,1)S(1)}, u32[]{:S(2)}, u32[]{:S(2)}) %collective-permute-start.1) | collective-permute-done | bytes 393248 | tf_op jit(solution)/shard_map/ppermute | solution.py:347
  37.8 7.0 %collective-permute-start.6 = (bf16[4,64,384]{2,1,0:T(8,128)(2,1)S(1)}, bf16[4,64,384]{2,1,0:T(8,128)(2,1)S(1)}, u32[]{:S(2)}, u32[]{:S(2)}) collective-permute-start(bf16[4,64,384]{2,1,0:T(8,128)(2,1)S(1)} %get-tuple-element.30), channel_id=1, source_target_pairs={{0,32},{4,36},{8,40},{12,44},{16,48},{20,52},{24,56},{28,60},{32,0... | collective-permute-start | bytes 589832 | tf_op jit(solution)/shard_map/ppermute | solution.py:351
  44.8 5.7 %encode.3 = f32[2,768]{1,0:T(2,128)S(1)} custom-call(s32[7]{0:T(128)S(1)} %pad_add_fusion.idx, bf16[4,256,384]{2,1,0:T(8,128)(2,1)S(1)} %copy-done.7, bf16[4,256,384]{2,1,0:T(8,128)(2,1)S(1)} %collective-permute-done.2.left, bf16[4,256,384]{2,1,0:T(8,128)(2,1)} %collective-permute-done.right, bf16[2,256,384]{2,1,0:T(8,128)(2,1)S(1)} %collective-permute-done.1.far, ...), custom_call_target="tpu_custom_call" | custom-call | flops 6000000000 | bytes 8000000 | tf_op jit(solution)/shard_map/encode/pallas_call | solution.py:92
  51.1 2.6 %collective-permute-start.8 = (f32[4,768]{1,0:T(4,128)S(1)}, f32[4,768]{1,0:T(4,128)S(1)}, u32[]{:S(2)}, u32[]{:S(2)}) collective-permute-start(f32[4,768]{1,0:T(4,128)S(1)} %fusion.2.a), channel_id=1, source_target_pairs={{0,3},{1,0},{2,1},{3,2},{4,7},{5,4},{6,5},{7,6},{8,11},{9,8},{10,9... | collective-permute-start | bytes 36872 | tf_op jit(solution)/shard_map/ppermute | solution.py:347
  53.7 1.0 collective-permute-start.9
  54.7 1.3 %collective-permute-start.10 = (bf16[8,32,384]{2,1,0:T(8,128)(2,1)S(1)}, bf16[8,32,384]{2,1,0:T(8,128)(2,1)S(1)}, u32[]{:S(2)}, u32[]{:S(2)}) collective-permute-start(bf16[8,32,384]{2,1,0:T(8,128)(2,1)S(1)} %get-tuple-element.34), channel_id=1, source_target_pairs={{0,64},{4,68},{8,72},{12,76},{16,80},{20,84},{24,88},{28,92},{32,9... | collective-permute-start | bytes 589832 | tf_op jit(solution)/shard_map/ppermute | solution.py:351
  56.0 2.7 %collective-permute-start.11 = (bf16[8,16,384]{2,1,0:T(8,128)(2,1)S(1)}, bf16[8,16,384]{2,1,0:T(8,128)(2,1)S(1)}, u32[]{:S(2)}, u32[]{:S(2)}) collective-permute-start(bf16[8,16,384]{2,1,0:T(8,128)(2,1)S(1)} %get-tuple-element.56), channel_id=1, source_target_pairs={{0,128},{4,132},{8,136},{12,140},{16,144},{20,148},{24,152},{28,15... | collective-permute-start | bytes 294920 | tf_op jit(solution)/shard_map/ppermute | solution.py:351
  60.1 2.6 %collective-permute-done.11 = bf16[8,16,384]{2,1,0:T(8,128)(2,1)S(1)} collective-permute-done((bf16[8,16,384]{2,1,0:T(8,128)(2,1)S(1)}, bf16[8,16,384]{2,1,0:T(8,128)(2,1)S(1)}, u32[]{:S(2)}, u32[]{:S(2)}) %collective-permute-start.11) | collective-permute-done | bytes 98336 | tf_op jit(solution)/shard_map/ppermute | solution.py:351
  62.7 1.4 %collective-permute-done.12 = bf16[8,16,384]{2,1,0:T(8,128)(2,1)S(1)} collective-permute-done((bf16[8,16,384]{2,1,0:T(8,128)(2,1)S(1)}, bf16[8,16,384]{2,1,0:T(8,128)(2,1)S(1)}, u32[]{:S(2)}, u32[]{:S(2)}) %collective-permute-start.12) | collective-permute-done | bytes 98336 | tf_op jit(solution)/shard_map/ppermute | solution.py:351
  67.4 5.0 %collective-permute-start.13 = (bf16[1536,384]{1,0:T(8,128)(2,1)}, bf16[1536,384]{1,0:T(8,128)(2,1)}, u32[]{:S(2)}, u32[]{:S(2)}) collective-permute-start(bf16[1536,384]{1,0:T(8,128)(2,1)} %constant_dynamic-update-slice_fusion.2.refs_2_), channel_id=1, source_target_pairs={{0,4},{4,0},{8,12},{12,8},{16,20},{20,16},{24,28},{28,24},{32,36},... | collective-permute-start | bytes 3538952 | tf_op jit(solution)/shard_map/ppermute | solution.py:351
  72.4 1.0 embed_rows.1
  74.2 7.6 %all-to-all-start = ((bf16[64,4,640]{2,1,0:T(4,128)(2,1)}), bf16[64,4,640]{2,1,0:T(4,128)(2,1)S(1)}, u32[]{:S(2)}, u32[]{:S(2)}) async-start(bf16[64,4,640]{2,1,0:T(4,128)(2,1)} %broadcast_in_dim.10), calls=%async_computation | async-start | bytes 655360 | tf_op jit(solution)/shard_map/all_to_all | solution.py:409
  83.0 12.1 %all-to-all-done = bf16[64,4,640]{2,1,0:T(4,128)(2,1)S(1)} async-done(((bf16[64,4,640]{2,1,0:T(4,128)(2,1)}), bf16[64,4,640]{2,1,0:T(4,128)(2,1)S(1)}, u32[]{:S(2)}, u32[]{:S(2)}) %all-to-all-start) | async-done | bytes 327712 | tf_op jit(solution)/shard_map/all_to_all | solution.py:409
  95.9 6.9 %attend.1 = (bf16[128,192]{1,0:T(8,128)(2,1)}, bf16[128,192]{1,0:T(8,128)(2,1)}, bf16[128,192]{1,0:T(8,128)(2,1)}, bf16[128,192]{1,0:T(8,128)(2,1)}) custom-call(s32[7]{0:T(128)} %copy-done.5, bf16[256,640]{1,0:T(8,128)(2,1)} %reshape.46.refs_0_, f32[128,192]{1,0:T(8,128)} %copy-done.4, bf16[1536,384]{1,0:T(8,128)(2,1)} %constant_dynamic-update-slice_fusion.2.refs_2_, ...), custom_call_target="tpu_custom_call" | custom-call | tf_op jit(solution)/shard_map/attend/pallas_call | solution.py:328
  102.8 1.3 %collective-permute-start.16 = (bf16[128,192]{1,0:T(8,128)(2,1)}, bf16[128,192]{1,0:T(8,128)(2,1)S(1)}, u32[]{:S(2)}, u32[]{:S(2)}) collective-permute-start(bf16[128,192]{1,0:T(8,128)(2,1)} %get-tuple-element.46), channel_id=1, source_target_pairs={{0,3},{1,0},{2,1},{3,2},{4,7},{5,4},{6,5},{7,6},{8,11},{9,8},{10,9... | collective-permute-start | bytes 147464 | tf_op jit(solution)/shard_map/ppermute | solution.py:347
  104.1 2.1 %collective-permute-start.15 = (bf16[128,192]{1,0:T(8,128)(2,1)}, bf16[128,192]{1,0:T(8,128)(2,1)S(1)}, u32[]{:S(2)}, u32[]{:S(2)}) collective-permute-start(bf16[128,192]{1,0:T(8,128)(2,1)} %get-tuple-element.45), channel_id=1, source_target_pairs={{0,2},{1,3},{2,0},{3,1},{4,6},{5,7},{6,4},{7,5},{8,10},{9,11},{10,... | collective-permute-start | bytes 147464 | tf_op jit(solution)/shard_map/ppermute | solution.py:347
  107.0 2.0 %collective-permute-done.15 = bf16[128,192]{1,0:T(8,128)(2,1)S(1)} collective-permute-done((bf16[128,192]{1,0:T(8,128)(2,1)}, bf16[128,192]{1,0:T(8,128)(2,1)S(1)}, u32[]{:S(2)}, u32[]{:S(2)}) %collective-permute-start.15) | collective-permute-done | bytes 49184 | tf_op jit(solution)/shard_map/ppermute | solution.py:347
  109.0 2.2 %collective-permute-done.14 = bf16[128,192]{1,0:T(8,128)(2,1)S(1)} collective-permute-done((bf16[128,192]{1,0:T(8,128)(2,1)}, bf16[128,192]{1,0:T(8,128)(2,1)S(1)}, u32[]{:S(2)}, u32[]{:S(2)}) %collective-permute-start.14) | collective-permute-done | bytes 49184 | tf_op jit(solution)/shard_map/ppermute | solution.py:347
  111.2 0.9 add_convert_fusion
  (64 shorter events, 13.4 us)
Async XLA Ops:
  0.0 11.3 %copy-start = (bf16[1536,768]{1,0:T(8,128)(2,1)S(1)}, bf16[1536,768]{1,0:T(8,128)(2,1)}, u32[]{:S(2)}) copy-start(bf16[1536,768]{1,0:T(8,128)(2,1)} %param.17) | copy-start | bytes 7077892
  0.0 18.5 %collective-permute-start.2 = (bf16[4,256,384]{2,1,0:T(8,128)(2,1)}, bf16[4,256,384]{2,1,0:T(8,128)(2,1)S(1)}, u32[]{:S(2)}, u32[]{:S(2)}) collective-permute-start(bf16[4,256,384]{2,1,0:T(8,128)(2,1)} %own.3), channel_id=1, source_target_pairs={{0,1},{1,2},{2,3},{3,0},{4,5},{5,6},{6,7},{7,4},{8,9},{9,10},{10,1... | collective-permute-start | bytes 2359304 | tf_op jit(solution)/shard_map/ppermute | solution.py:347
  2.0 25.6 %collective-permute-start = (bf16[4,256,384]{2,1,0:T(8,128)(2,1)}, bf16[4,256,384]{2,1,0:T(8,128)(2,1)}, u32[]{:S(2)}, u32[]{:S(2)}) collective-permute-start(bf16[4,256,384]{2,1,0:T(8,128)(2,1)} %own.3), channel_id=1, source_target_pairs={{0,3},{1,0},{2,1},{3,2},{4,7},{5,4},{6,5},{7,6},{8,11},{9,8},{10,9... | collective-permute-start | bytes 2359304 | tf_op jit(solution)/shard_map/ppermute | solution.py:347
  5.5 66.9 %copy-start.5 = (s32[7]{0:T(128)}, s32[7]{0:T(128)S(1)}, u32[]{:S(2)}) copy-start(s32[7]{0:T(128)S(1)} %pad_add_fusion.idx) | copy-start | bytes 88
  5.5 1.2 %copy-start.1 = (bf16[768,3,192]{0,2,1:T(8,128)(2,1)S(1)}, bf16[768,3,192]{0,2,1:T(8,128)(2,1)}, u32[]{:S(2)}) copy-start(bf16[768,3,192]{0,2,1:T(8,128)(2,1)} %param.20) | copy-start | bytes 2654212
  6.6 0.9 copy-start.3
  8.9 0.7 copy-start.4
  9.6 5.2 %collective-permute-start.4 = (bf16[1,256,384]{2,1,0:T(8,128)(2,1)S(1)}, bf16[1,256,384]{2,1,0:T(8,128)(2,1)S(1)}, u32[]{:S(2)}, u32[]{:S(2)}) collective-permute-start(bf16[1,256,384]{2,1,0:T(8,128)(2,1)S(1)} %bitcast.24), channel_id=1, source_target_pairs={{0,8},{4,12},{8,0},{12,4},{16,24},{20,28},{24,16},{28,20},{32,40},... | collective-permute-start | bytes 589832 | tf_op jit(solution)/shard_map/ppermute | solution.py:351
  14.5 6.1 %copy-start.8 = (bf16[384,768]{1,0:T(8,128)(2,1)S(1)}, bf16[384,768]{1,0:T(8,128)(2,1)}, u32[]{:S(2)}) copy-start(bf16[384,768]{1,0:T(8,128)(2,1)} %convolution_convert_fusion) | copy-start | bytes 1769476
  14.8 12.1 %collective-permute-start.5 = (bf16[2,128,384]{2,1,0:T(8,128)(2,1)S(1)}, bf16[2,128,384]{2,1,0:T(8,128)(2,1)S(1)}, u32[]{:S(2)}, u32[]{:S(2)}) collective-permute-start(bf16[2,128,384]{2,1,0:T(8,128)(2,1)S(1)} %get-tuple-element.52), channel_id=1, source_target_pairs={{0,16},{4,20},{8,24},{12,28},{16,0},{20,4},{24,8},{28,12},{32,48},... | collective-permute-start | bytes 589832 | tf_op jit(solution)/shard_map/ppermute | solution.py:351
  18.5 2.2 %copy-start.10 = (f32[1536]{0:T(1024)S(1)}, f32[1536]{0:T(1024)}, u32[]{:S(2)}) copy-start(f32[1536]{0:T(1024)} %param.14) | copy-start | bytes 18436
  18.5 11.5 %collective-permute-start.3 = (bf16[2,256,384]{2,1,0:T(8,128)(2,1)S(1)}, bf16[2,256,384]{2,1,0:T(8,128)(2,1)S(1)}, u32[]{:S(2)}, u32[]{:S(2)}) collective-permute-start(bf16[2,256,384]{2,1,0:T(8,128)(2,1)S(1)} %slice.49), channel_id=1, source_target_pairs={{0,1},{1,2},{2,3},{3,0},{4,5},{5,6},{6,7},{7,4},{8,9},{9,10},{10,1... | collective-permute-start | bytes 1179656 | tf_op jit(solution)/shard_map/ppermute | solution.py:347
  20.6 9.4 %copy-start.6 = (bf16[1536,3,384]{2,0,1:T(8,128)(2,1)S(1)}, bf16[1536,3,384]{2,0,1:T(8,128)(2,1)}, u32[]{:S(2)}) copy-start(bf16[1536,3,384]{2,0,1:T(8,128)(2,1)} %param.15) | copy-start | bytes 10616836
  20.7 9.3 %copy-start.7 = (bf16[4,256,384]{2,1,0:T(8,128)(2,1)S(1)}, bf16[4,256,384]{2,1,0:T(8,128)(2,1)}, u32[]{:S(2)}) copy-start(bf16[4,256,384]{2,1,0:T(8,128)(2,1)} %own.3) | copy-start | bytes 2359300
  28.7 9.1 %collective-permute-start.1 = (bf16[2,256,384]{2,1,0:T(8,128)(2,1)S(1)}, bf16[2,256,384]{2,1,0:T(8,128)(2,1)S(1)}, u32[]{:S(2)}, u32[]{:S(2)}) collective-permute-start(bf16[2,256,384]{2,1,0:T(8,128)(2,1)S(1)} %slice.48), channel_id=1, source_target_pairs={{0,3},{1,0},{2,1},{3,2},{4,7},{5,4},{6,5},{7,6},{8,11},{9,8},{10,9... | collective-permute-start | bytes 1179656 | tf_op jit(solution)/shard_map/ppermute | solution.py:347
  37.8 12.8 %collective-permute-start.6 = (bf16[4,64,384]{2,1,0:T(8,128)(2,1)S(1)}, bf16[4,64,384]{2,1,0:T(8,128)(2,1)S(1)}, u32[]{:S(2)}, u32[]{:S(2)}) collective-permute-start(bf16[4,64,384]{2,1,0:T(8,128)(2,1)S(1)} %get-tuple-element.30), channel_id=1, source_target_pairs={{0,32},{4,36},{8,40},{12,44},{16,48},{20,52},{24,56},{28,60},{32,0... | collective-permute-start | bytes 589832 | tf_op jit(solution)/shard_map/ppermute | solution.py:351
  51.0 21.4 %copy-start.2 = (bf16[768,3,192]{0,2,1:T(8,128)(2,1)S(1)}, bf16[768,3,192]{0,2,1:T(8,128)(2,1)}, u32[]{:S(2)}) copy-start(bf16[768,3,192]{0,2,1:T(8,128)(2,1)} %param.20) | copy-start | bytes 2654212
  51.0 8.4 %collective-permute-start.7 = (f32[4,768]{1,0:T(4,128)S(1)}, f32[4,768]{1,0:T(4,128)S(1)}, u32[]{:S(2)}, u32[]{:S(2)}) collective-permute-start(f32[4,768]{1,0:T(4,128)S(1)} %fusion.2.a), channel_id=1, source_target_pairs={{0,1},{1,2},{2,3},{3,0},{4,5},{5,6},{6,7},{7,4},{8,9},{9,10},{10,1... | collective-permute-start | bytes 36872 | tf_op jit(solution)/shard_map/ppermute | solution.py:347
  51.1 9.0 %collective-permute-start.8 = (f32[4,768]{1,0:T(4,128)S(1)}, f32[4,768]{1,0:T(4,128)S(1)}, u32[]{:S(2)}, u32[]{:S(2)}) collective-permute-start(f32[4,768]{1,0:T(4,128)S(1)} %fusion.2.a), channel_id=1, source_target_pairs={{0,3},{1,0},{2,1},{3,2},{4,7},{5,4},{6,5},{7,6},{8,11},{9,8},{10,9... | collective-permute-start | bytes 36872 | tf_op jit(solution)/shard_map/ppermute | solution.py:347
  53.7 6.4 %collective-permute-start.9 = (f32[4,768]{1,0:T(4,128)S(1)}, f32[4,768]{1,0:T(4,128)S(1)}, u32[]{:S(2)}, u32[]{:S(2)}) collective-permute-start(f32[4,768]{1,0:T(4,128)S(1)} %fusion.2.a), channel_id=1, source_target_pairs={{0,2},{1,3},{2,0},{3,1},{4,6},{5,7},{6,4},{7,5},{8,10},{9,11},{10,... | collective-permute-start | bytes 36872 | tf_op jit(solution)/shard_map/ppermute | solution.py:347
  54.7 9.4 %collective-permute-start.10 = (bf16[8,32,384]{2,1,0:T(8,128)(2,1)S(1)}, bf16[8,32,384]{2,1,0:T(8,128)(2,1)S(1)}, u32[]{:S(2)}, u32[]{:S(2)}) collective-permute-start(bf16[8,32,384]{2,1,0:T(8,128)(2,1)S(1)} %get-tuple-element.34), channel_id=1, source_target_pairs={{0,64},{4,68},{8,72},{12,76},{16,80},{20,84},{24,88},{28,92},{32,9... | collective-permute-start | bytes 589832 | tf_op jit(solution)/shard_map/ppermute | solution.py:351
  56.0 6.7 %collective-permute-start.11 = (bf16[8,16,384]{2,1,0:T(8,128)(2,1)S(1)}, bf16[8,16,384]{2,1,0:T(8,128)(2,1)S(1)}, u32[]{:S(2)}, u32[]{:S(2)}) collective-permute-start(bf16[8,16,384]{2,1,0:T(8,128)(2,1)S(1)} %get-tuple-element.56), channel_id=1, source_target_pairs={{0,128},{4,132},{8,136},{12,140},{16,144},{20,148},{24,152},{28,15... | collective-permute-start | bytes 294920 | tf_op jit(solution)/shard_map/ppermute | solution.py:351
  59.4 4.7 %collective-permute-start.12 = (bf16[8,16,384]{2,1,0:T(8,128)(2,1)S(1)}, bf16[8,16,384]{2,1,0:T(8,128)(2,1)S(1)}, u32[]{:S(2)}, u32[]{:S(2)}) collective-permute-start(bf16[8,16,384]{2,1,0:T(8,128)(2,1)S(1)} %get-tuple-element.56), channel_id=1, source_target_pairs={{0,192},{4,196},{8,200},{12,204},{16,208},{20,212},{24,216},{28,22... | collective-permute-start | bytes 294920 | tf_op jit(solution)/shard_map/ppermute | solution.py:351
  66.1 15.8 %copy-start.9 = (bf16[192,768]{1,0:T(8,128)(2,1)S(1)}, bf16[192,768]{1,0:T(8,128)(2,1)}, u32[]{:S(2)}) copy-start(bf16[192,768]{1,0:T(8,128)(2,1)} %param.21) | copy-start | bytes 884740
  67.4 28.5 %collective-permute-start.13 = (bf16[1536,384]{1,0:T(8,128)(2,1)}, bf16[1536,384]{1,0:T(8,128)(2,1)}, u32[]{:S(2)}, u32[]{:S(2)}) collective-permute-start(bf16[1536,384]{1,0:T(8,128)(2,1)} %constant_dynamic-update-slice_fusion.2.refs_2_), channel_id=1, source_target_pairs={{0,4},{4,0},{8,12},{12,8},{16,20},{20,16},{24,28},{28,24},{32,36},... | collective-permute-start | bytes 3538952 | tf_op jit(solution)/shard_map/ppermute | solution.py:351
  74.2 20.9 %all-to-all-start = ((bf16[64,4,640]{2,1,0:T(4,128)(2,1)}), bf16[64,4,640]{2,1,0:T(4,128)(2,1)S(1)}, u32[]{:S(2)}, u32[]{:S(2)}) async-start(bf16[64,4,640]{2,1,0:T(4,128)(2,1)} %broadcast_in_dim.10), calls=%async_computation | async-start | bytes 655360 | tf_op jit(solution)/shard_map/all_to_all | solution.py:409
  102.8 4.2 %collective-permute-start.16 = (bf16[128,192]{1,0:T(8,128)(2,1)}, bf16[128,192]{1,0:T(8,128)(2,1)S(1)}, u32[]{:S(2)}, u32[]{:S(2)}) collective-permute-start(bf16[128,192]{1,0:T(8,128)(2,1)} %get-tuple-element.46), channel_id=1, source_target_pairs={{0,3},{1,0},{2,1},{3,2},{4,7},{5,4},{6,5},{7,6},{8,11},{9,8},{10,9... | collective-permute-start | bytes 147464 | tf_op jit(solution)/shard_map/ppermute | solution.py:347
  104.1 4.8 %collective-permute-start.15 = (bf16[128,192]{1,0:T(8,128)(2,1)}, bf16[128,192]{1,0:T(8,128)(2,1)S(1)}, u32[]{:S(2)}, u32[]{:S(2)}) collective-permute-start(bf16[128,192]{1,0:T(8,128)(2,1)} %get-tuple-element.45), channel_id=1, source_target_pairs={{0,2},{1,3},{2,0},{3,1},{4,6},{5,7},{6,4},{7,5},{8,10},{9,11},{10,... | collective-permute-start | bytes 147464 | tf_op jit(solution)/shard_map/ppermute | solution.py:347
  106.2 4.9 %collective-permute-start.14 = (bf16[128,192]{1,0:T(8,128)(2,1)}, bf16[128,192]{1,0:T(8,128)(2,1)S(1)}, u32[]{:S(2)}, u32[]{:S(2)}) collective-permute-start(bf16[128,192]{1,0:T(8,128)(2,1)} %get-tuple-element.44), channel_id=1, source_target_pairs={{0,1},{1,2},{2,3},{3,0},{4,5},{5,6},{6,7},{7,4},{8,9},{9,10},{10,1... | collective-permute-start | bytes 147464 | tf_op jit(solution)/shard_map/ppermute | solution.py:347

commit v9 on v6

--- a/solution.py
+++ b/solution.py
@@ -338,7 +338,7 @@
             pltpu.VMEM((4 * ROWS, hw), F32),
             pltpu.SemaphoreType.DMA((5,)),
         ],
-        compiler_params=params(20),
+        compiler_params=params(60),
         name="attend",
     )(idx, emb, q_cache, mine, theirs, out_w)
 

time: 108 us -> 106 us (0.981)
  local copies, waits for them, and re-layouts: 15 us -> 11.8 us
  starting transfers between devices: 46.8 us -> 45 us
  waiting for transfers between devices: 20.5 us -> 22 us
    all_to_all x1, waiting for transfers between devices: 9.33 us -> 12.1 us  [local(): lax.all_to_all(jnp.broadcast_to(emb[None], (64,) + emb.shape), 'seq', 0, 0)]
    reshape x2, local copies, waits for them, and re-layouts: 3.86 us -> 1.15 us  [local(): out_w = long_out.reshape(hw, 4, hw).transpose(1, 0, 2)]
    ppermute x6, starting transfers between devices: 23.5 us -> 22.3 us  [swap_seq(): return lax.ppermute(x, 'seq', [(i, i ^ bit) for i in range(64)])]
    unnamed x34 -> x28, local copies, waits for them, and re-layouts: 5.81 us -> 5.59 us
  transfers between devices with their start and end apart: 17 -> 17, of which waited for: 9 -> 7; matrix products, arithmetic and copies ran while one was open for 12% -> 12% of each run, Pallas kernels for 13% -> 13%
where the time goes in v9:
time: 106 us
  starting transfers between devices  45 us (42%)
  waiting for transfers between devices  22 us (21%)
  Pallas kernels  20.6 us (19%)
  local copies, waits for them, and re-layouts  11.8 us (11%)
  matrix products  3.45 us (3%)
  other arithmetic  1.83 us (2%)
    ppermute x6, starting transfers between devices, swap_seq(): return lax.ppermute(x, 'seq', [(i, i ^ bit) for i in range(64)])  22.3 us
    ppermute x10, starting transfers between devices, shift_mp(): return lax.ppermute(x, 'mp', [(i, (i + k) % 4) for i in range(4)])  12.8 us
    all_to_all x1, waiting for transfers between devices, local(): lax.all_to_all(jnp.broadcast_to(emb[None], (64,) + emb.shape), 'seq', 0, 0)  12.1 us
    pallas_call x2, Pallas kernels, encode(): pl.pallas_call(encode_kernel, grid=(1,), out_shape=jax.ShapeDtypeStruct((...  11.3 us
    all_to_all x1, starting transfers between devices, local(): lax.all_to_all(jnp.broadcast_to(emb[None], (64,) + emb.shape), 'seq', 0, 0)  9.84 us
    pallas_call x1, Pallas kernels, attend(): pl.pallas_call(attend_kernel, out_shape=(jax.ShapeDtypeStruct((ROWS, hw),...  6.93 us
    ppermute x6, waiting for transfers between devices, swap_seq(): return lax.ppermute(x, 'seq', [(i, i ^ bit) for i in range(64)])  5.7 us
    unnamed x28, local copies, waits for them, and re-layouts  5.59 us
  transfers between devices with their start and end apart: 17, of which 7 were waited for; matrix products, arithmetic and copies ran while one was open for 12% of the time, Pallas kernels for 13%

profile of v9, /device:TPU:1, one launch (start us, length us, event | category | flops | bytes accessed | tf_op | source)
XLA Modules:
  0.0 105.6 jit_solution(5532509902231492054)
XLA Ops:
  0.0 2.0 %collective-permute-start.2 = (bf16[4,256,384]{2,1,0:T(8,128)(2,1)}, bf16[4,256,384]{2,1,0:T(8,128)(2,1)S(1)}, u32[]{:S(2)}, u32[]{:S(2)}) collective-permute-start(bf16[4,256,384]{2,1,0:T(8,128)(2,1)} %own.3), channel_id=1, source_target_pairs={{0,1},{1,2},{2,3},{3,0},{4,5},{5,6},{6,7},{7,4},{8,9},{9,10},{10,1... | collective-permute-start | bytes 2359304 | tf_op jit(solution)/shard_map/ppermute | solution.py:347
  2.0 1.4 %collective-permute-start = (bf16[4,256,384]{2,1,0:T(8,128)(2,1)}, bf16[4,256,384]{2,1,0:T(8,128)(2,1)}, u32[]{:S(2)}, u32[]{:S(2)}) collective-permute-start(bf16[4,256,384]{2,1,0:T(8,128)(2,1)} %own.3), channel_id=1, source_target_pairs={{0,3},{1,0},{2,1},{3,2},{4,7},{5,4},{6,5},{7,6},{8,11},{9,8},{10,9... | collective-permute-start | bytes 2359304 | tf_op jit(solution)/shard_map/ppermute | solution.py:347
  5.5 1.2 %copy-done.1 = bf16[768,3,192]{0,2,1:T(8,128)(2,1)S(1)} copy-done((bf16[768,3,192]{0,2,1:T(8,128)(2,1)S(1)}, bf16[768,3,192]{0,2,1:T(8,128)(2,1)}, u32[]{:S(2)}) %copy-start.1) | copy-done | bytes 884760
  6.6 0.9 copy-done.3
  7.6 1.3 %slide_project.1 = (f32[128,192]{1,0:T(8,128)S(1)}, bf16[256,384]{1,0:T(8,128)(2,1)S(1)}) custom-call(s32[7]{0:T(128)S(1)} %pad_add_fusion.idx, bf16[128,768]{1,0:T(8,128)(2,1)S(1)} %copy-done.3, f32[1,768]{1,0:T(1,128)S(1)} %reshape.31.gain, bf16[576,768]{1,0:T(8,128)(2,1)S(1)} %bitcast.18), custom_call_target="tpu_custom_call" | custom-call | tf_op jit(solution)/shard_map/slide_project/pallas_call | solution.py:192
  9.5 1.8 %collective-permute-start.4 = (bf16[1,256,384]{2,1,0:T(8,128)(2,1)S(1)}, bf16[1,256,384]{2,1,0:T(8,128)(2,1)S(1)}, u32[]{:S(2)}, u32[]{:S(2)}) collective-permute-start(bf16[1,256,384]{2,1,0:T(8,128)(2,1)S(1)} %bitcast.20), channel_id=1, source_target_pairs={{0,8},{4,12},{8,0},{12,4},{16,24},{20,28},{24,16},{28,20},{32,40},... | collective-permute-start | bytes 589832 | tf_op jit(solution)/shard_map/ppermute | solution.py:351
  11.3 3.2 %convolution_convert_fusion = bf16[384,768]{1,0:T(8,128)(2,1)} fusion(bf16[384,1536]{1,0:T(8,128)(2,1)} %param.16, bf16[1536,768]{1,0:T(8,128)(2,1)S(1)} %copy-done), kind=kOutput, calls=%fused_computation | convolution fusion | flops 906264576 | bytes 4128768 | tf_op jit(solution)/shard_map/dot_general | solution.py:31
  14.8 3.6 %collective-permute-start.5 = (bf16[2,128,384]{2,1,0:T(8,128)(2,1)S(1)}, bf16[2,128,384]{2,1,0:T(8,128)(2,1)S(1)}, u32[]{:S(2)}, u32[]{:S(2)}) collective-permute-start(bf16[2,128,384]{2,1,0:T(8,128)(2,1)S(1)} %get-tuple-element.52), channel_id=1, source_target_pairs={{0,16},{4,20},{8,24},{12,28},{16,0},{20,4},{24,8},{28,12},{32,48},... | collective-permute-start | bytes 589832 | tf_op jit(solution)/shard_map/ppermute | solution.py:351
  18.5 2.1 %collective-permute-start.3 = (bf16[2,256,384]{2,1,0:T(8,128)(2,1)S(1)}, bf16[2,256,384]{2,1,0:T(8,128)(2,1)S(1)}, u32[]{:S(2)}, u32[]{:S(2)}) collective-permute-start(bf16[2,256,384]{2,1,0:T(8,128)(2,1)S(1)} %slice.41), channel_id=1, source_target_pairs={{0,1},{1,2},{2,3},{3,0},{4,5},{5,6},{6,7},{7,4},{8,9},{9,10},{10,1... | collective-permute-start | bytes 1179656 | tf_op jit(solution)/shard_map/ppermute | solution.py:347
  21.4 5.5 %collective-permute-done.5 = bf16[2,128,384]{2,1,0:T(8,128)(2,1)S(1)} collective-permute-done((bf16[2,128,384]{2,1,0:T(8,128)(2,1)S(1)}, bf16[2,128,384]{2,1,0:T(8,128)(2,1)S(1)}, u32[]{:S(2)}, u32[]{:S(2)}) %collective-permute-start.5) | collective-permute-done | bytes 196640 | tf_op jit(solution)/shard_map/ppermute | solution.py:351
  27.6 1.0 slice.40
  28.7 1.4 %collective-permute-start.1 = (bf16[2,256,384]{2,1,0:T(8,128)(2,1)S(1)}, bf16[2,256,384]{2,1,0:T(8,128)(2,1)S(1)}, u32[]{:S(2)}, u32[]{:S(2)}) collective-permute-start(bf16[2,256,384]{2,1,0:T(8,128)(2,1)S(1)} %slice.40), channel_id=1, source_target_pairs={{0,3},{1,0},{2,1},{3,2},{4,7},{5,4},{6,5},{7,6},{8,11},{9,8},{10,9... | collective-permute-start | bytes 1179656 | tf_op jit(solution)/shard_map/ppermute | solution.py:347
  30.0 7.9 %collective-permute-start.6 = (bf16[4,64,384]{2,1,0:T(8,128)(2,1)S(1)}, bf16[4,64,384]{2,1,0:T(8,128)(2,1)S(1)}, u32[]{:S(2)}, u32[]{:S(2)}) collective-permute-start(bf16[4,64,384]{2,1,0:T(8,128)(2,1)S(1)} %get-tuple-element.26), channel_id=1, source_target_pairs={{0,32},{4,36},{8,40},{12,44},{16,48},{20,52},{24,56},{28,60},{32,0... | collective-permute-start | bytes 589832 | tf_op jit(solution)/shard_map/ppermute | solution.py:351
  38.0 5.7 %encode.2 = f32[2,768]{1,0:T(2,128)S(1)} custom-call(s32[7]{0:T(128)S(1)} %pad_add_fusion.idx, bf16[4,256,384]{2,1,0:T(8,128)(2,1)S(1)} %copy-done.7, bf16[4,256,384]{2,1,0:T(8,128)(2,1)S(1)} %collective-permute-done.2.left, bf16[4,256,384]{2,1,0:T(8,128)(2,1)} %collective-permute-done.right, bf16[2,256,384]{2,1,0:T(8,128)(2,1)S(1)} %collective-permute-done.3.far, ...), custom_call_target="tpu_custom_call" | custom-call | flops 6000000000 | bytes 8000000 | tf_op jit(solution)/shard_map/encode/pallas_call | solution.py:92
  43.8 1.6 %collective-permute-start.7 = (bf16[8,32,384]{2,1,0:T(8,128)(2,1)S(1)}, bf16[8,32,384]{2,1,0:T(8,128)(2,1)S(1)}, u32[]{:S(2)}, u32[]{:S(2)}) collective-permute-start(bf16[8,32,384]{2,1,0:T(8,128)(2,1)S(1)} %get-tuple-element.30), channel_id=1, source_target_pairs={{0,64},{4,68},{8,72},{12,76},{16,80},{20,84},{24,88},{28,92},{32,9... | collective-permute-start | bytes 589832 | tf_op jit(solution)/shard_map/ppermute | solution.py:351
  45.4 5.7 %encode.3 = f32[2,768]{1,0:T(2,128)S(1)} custom-call(s32[7]{0:T(128)S(1)} %pad_add_fusion.idx, bf16[4,256,384]{2,1,0:T(8,128)(2,1)S(1)} %copy-done.7, bf16[4,256,384]{2,1,0:T(8,128)(2,1)S(1)} %collective-permute-done.2.left, bf16[4,256,384]{2,1,0:T(8,128)(2,1)} %collective-permute-done.right, bf16[2,256,384]{2,1,0:T(8,128)(2,1)S(1)} %collective-permute-done.1.far, ...), custom_call_target="tpu_custom_call" | custom-call | flops 6000000000 | bytes 8000000 | tf_op jit(solution)/shard_map/encode/pallas_call | solution.py:92
  51.9 2.7 %collective-permute-start.11 = (bf16[16,16,384]{2,1,0:T(8,128)(2,1)S(1)}, bf16[16,16,384]{2,1,0:T(8,128)(2,1)S(1)}, u32[]{:S(2)}, u32[]{:S(2)}) collective-permute-start(bf16[16,16,384]{2,1,0:T(8,128)(2,1)S(1)} %get-tuple-element.34), channel_id=1, source_target_pairs={{0,128},{4,132},{8,136},{12,140},{16,144},{20,148},{24,152},{28,15... | collective-permute-start | bytes 589832 | tf_op jit(solution)/shard_map/ppermute | solution.py:351
  55.7 2.4 %collective-permute-start.9 = (f32[4,768]{1,0:T(4,128)S(1)}, f32[4,768]{1,0:T(4,128)S(1)}, u32[]{:S(2)}, u32[]{:S(2)}) collective-permute-start(f32[4,768]{1,0:T(4,128)S(1)} %fusion.2.a), channel_id=1, source_target_pairs={{0,3},{1,0},{2,1},{3,2},{4,7},{5,4},{6,5},{7,6},{8,11},{9,8},{10,9... | collective-permute-start | bytes 36872 | tf_op jit(solution)/shard_map/ppermute | solution.py:347
  58.9 0.8 constant_dynamic-update-slice_fusion.4.refs_2_
  59.7 4.8 %collective-permute-start.12 = (bf16[1536,384]{1,0:T(8,128)(2,1)}, bf16[1536,384]{1,0:T(8,128)(2,1)}, u32[]{:S(2)}, u32[]{:S(2)}) collective-permute-start(bf16[1536,384]{1,0:T(8,128)(2,1)} %constant_dynamic-update-slice_fusion.4.refs_2_), channel_id=1, source_target_pairs={{0,4},{4,0},{8,12},{12,8},{16,20},{20,16},{24,28},{28,24},{32,36},... | collective-permute-start | bytes 3538952 | tf_op jit(solution)/shard_map/ppermute | solution.py:351
  64.5 1.0 embed_rows.1
  65.5 0.8 broadcast_in_dim.10
  66.3 9.8 %all-to-all-start = ((bf16[64,4,640]{2,1,0:T(4,128)(2,1)}), bf16[64,4,640]{2,1,0:T(4,128)(2,1)S(1)}, u32[]{:S(2)}, u32[]{:S(2)}) async-start(bf16[64,4,640]{2,1,0:T(4,128)(2,1)} %broadcast_in_dim.10), calls=%async_computation | async-start | bytes 655360 | tf_op jit(solution)/shard_map/all_to_all | solution.py:409
  76.5 0.8 copy.16
  77.3 12.1 %all-to-all-done = bf16[64,4,640]{2,1,0:T(4,128)(2,1)S(1)} async-done(((bf16[64,4,640]{2,1,0:T(4,128)(2,1)}), bf16[64,4,640]{2,1,0:T(4,128)(2,1)S(1)}, u32[]{:S(2)}, u32[]{:S(2)}) %all-to-all-start) | async-done | bytes 327712 | tf_op jit(solution)/shard_map/all_to_all | solution.py:409
  89.4 0.8 reshape.39.refs_0_
  90.2 6.9 %attend.1 = (bf16[128,192]{1,0:T(8,128)(2,1)}, bf16[128,192]{1,0:T(8,128)(2,1)}, bf16[128,192]{1,0:T(8,128)(2,1)}, bf16[128,192]{1,0:T(8,128)(2,1)}) custom-call(s32[7]{0:T(128)} %copy-done.5, bf16[256,640]{1,0:T(8,128)(2,1)} %reshape.39.refs_0_, f32[128,192]{1,0:T(8,128)} %copy-done.4, bf16[1536,384]{1,0:T(8,128)(2,1)} %constant_dynamic-update-slice_fusion.4.refs_2_, ...), custom_call_target="tpu_custom_call" | custom-call | tf_op jit(solution)/shard_map/attend/pallas_call | solution.py:328
  97.2 2.7 %collective-permute-start.14 = (bf16[128,192]{1,0:T(8,128)(2,1)}, bf16[128,192]{1,0:T(8,128)(2,1)S(1)}, u32[]{:S(2)}, u32[]{:S(2)}) collective-permute-start(bf16[128,192]{1,0:T(8,128)(2,1)} %get-tuple-element.43), channel_id=1, source_target_pairs={{0,2},{1,3},{2,0},{3,1},{4,6},{5,7},{6,4},{7,5},{8,10},{9,11},{10,... | collective-permute-start | bytes 147464 | tf_op jit(solution)/shard_map/ppermute | solution.py:347
  99.9 1.9 %collective-permute-done.13 = bf16[128,192]{1,0:T(8,128)(2,1)S(1)} collective-permute-done((bf16[128,192]{1,0:T(8,128)(2,1)}, bf16[128,192]{1,0:T(8,128)(2,1)S(1)}, u32[]{:S(2)}, u32[]{:S(2)}) %collective-permute-start.13) | collective-permute-done | bytes 49184 | tf_op jit(solution)/shard_map/ppermute | solution.py:347
  101.7 1.3 %collective-permute-done.14 = bf16[128,192]{1,0:T(8,128)(2,1)S(1)} collective-permute-done((bf16[128,192]{1,0:T(8,128)(2,1)}, bf16[128,192]{1,0:T(8,128)(2,1)S(1)}, u32[]{:S(2)}, u32[]{:S(2)}) %collective-permute-start.14) | collective-permute-done | bytes 49184 | tf_op jit(solution)/shard_map/ppermute | solution.py:347
  103.0 0.9 collective-permute-done.15
  104.0 0.9 add_convert_fusion
  (60 shorter events, 8.0 us)
Async XLA Ops:
  0.0 11.3 %copy-start = (bf16[1536,768]{1,0:T(8,128)(2,1)S(1)}, bf16[1536,768]{1,0:T(8,128)(2,1)}, u32[]{:S(2)}) copy-start(bf16[1536,768]{1,0:T(8,128)(2,1)} %param.17) | copy-start | bytes 7077892
  0.0 18.5 %collective-permute-start.2 = (bf16[4,256,384]{2,1,0:T(8,128)(2,1)}, bf16[4,256,384]{2,1,0:T(8,128)(2,1)S(1)}, u32[]{:S(2)}, u32[]{:S(2)}) collective-permute-start(bf16[4,256,384]{2,1,0:T(8,128)(2,1)} %own.3), channel_id=1, source_target_pairs={{0,1},{1,2},{2,3},{3,0},{4,5},{5,6},{6,7},{7,4},{8,9},{9,10},{10,1... | collective-permute-start | bytes 2359304 | tf_op jit(solution)/shard_map/ppermute | solution.py:347
  2.0 25.6 %collective-permute-start = (bf16[4,256,384]{2,1,0:T(8,128)(2,1)}, bf16[4,256,384]{2,1,0:T(8,128)(2,1)}, u32[]{:S(2)}, u32[]{:S(2)}) collective-permute-start(bf16[4,256,384]{2,1,0:T(8,128)(2,1)} %own.3), channel_id=1, source_target_pairs={{0,3},{1,0},{2,1},{3,2},{4,7},{5,4},{6,5},{7,6},{8,11},{9,8},{10,9... | collective-permute-start | bytes 2359304 | tf_op jit(solution)/shard_map/ppermute | solution.py:347
  5.5 59.0 %copy-start.5 = (s32[7]{0:T(128)}, s32[7]{0:T(128)S(1)}, u32[]{:S(2)}) copy-start(s32[7]{0:T(128)S(1)} %pad_add_fusion.idx) | copy-start | bytes 88
  5.5 1.2 %copy-start.1 = (bf16[768,3,192]{0,2,1:T(8,128)(2,1)S(1)}, bf16[768,3,192]{0,2,1:T(8,128)(2,1)}, u32[]{:S(2)}) copy-start(bf16[768,3,192]{0,2,1:T(8,128)(2,1)} %param.20) | copy-start | bytes 2654212
  6.6 0.9 copy-start.3
  8.9 0.6 copy-start.4
  9.5 5.2 %collective-permute-start.4 = (bf16[1,256,384]{2,1,0:T(8,128)(2,1)S(1)}, bf16[1,256,384]{2,1,0:T(8,128)(2,1)S(1)}, u32[]{:S(2)}, u32[]{:S(2)}) collective-permute-start(bf16[1,256,384]{2,1,0:T(8,128)(2,1)S(1)} %bitcast.20), channel_id=1, source_target_pairs={{0,8},{4,12},{8,0},{12,4},{16,24},{20,28},{24,16},{28,20},{32,40},... | collective-permute-start | bytes 589832 | tf_op jit(solution)/shard_map/ppermute | solution.py:351
  14.5 6.1 %copy-start.8 = (bf16[384,768]{1,0:T(8,128)(2,1)S(1)}, bf16[384,768]{1,0:T(8,128)(2,1)}, u32[]{:S(2)}) copy-start(bf16[384,768]{1,0:T(8,128)(2,1)} %convolution_convert_fusion) | copy-start | bytes 1769476
  14.8 12.1 %collective-permute-start.5 = (bf16[2,128,384]{2,1,0:T(8,128)(2,1)S(1)}, bf16[2,128,384]{2,1,0:T(8,128)(2,1)S(1)}, u32[]{:S(2)}, u32[]{:S(2)}) collective-permute-start(bf16[2,128,384]{2,1,0:T(8,128)(2,1)S(1)} %get-tuple-element.52), channel_id=1, source_target_pairs={{0,16},{4,20},{8,24},{12,28},{16,0},{20,4},{24,8},{28,12},{32,48},... | collective-permute-start | bytes 589832 | tf_op jit(solution)/shard_map/ppermute | solution.py:351
  18.5 2.2 %copy-start.10 = (f32[1536]{0:T(1024)S(1)}, f32[1536]{0:T(1024)}, u32[]{:S(2)}) copy-start(f32[1536]{0:T(1024)} %param.14) | copy-start | bytes 18436
  18.5 11.5 %collective-permute-start.3 = (bf16[2,256,384]{2,1,0:T(8,128)(2,1)S(1)}, bf16[2,256,384]{2,1,0:T(8,128)(2,1)S(1)}, u32[]{:S(2)}, u32[]{:S(2)}) collective-permute-start(bf16[2,256,384]{2,1,0:T(8,128)(2,1)S(1)} %slice.41), channel_id=1, source_target_pairs={{0,1},{1,2},{2,3},{3,0},{4,5},{5,6},{6,7},{7,4},{8,9},{9,10},{10,1... | collective-permute-start | bytes 1179656 | tf_op jit(solution)/shard_map/ppermute | solution.py:347
  20.6 17.4 %copy-start.6 = (bf16[1536,3,384]{2,0,1:T(8,128)(2,1)S(1)}, bf16[1536,3,384]{2,0,1:T(8,128)(2,1)}, u32[]{:S(2)}) copy-start(bf16[1536,3,384]{2,0,1:T(8,128)(2,1)} %param.15) | copy-start | bytes 10616836
  20.7 17.3 %copy-start.7 = (bf16[4,256,384]{2,1,0:T(8,128)(2,1)S(1)}, bf16[4,256,384]{2,1,0:T(8,128)(2,1)}, u32[]{:S(2)}) copy-start(bf16[4,256,384]{2,1,0:T(8,128)(2,1)} %own.3) | copy-start | bytes 2359300
  28.7 15.1 %collective-permute-start.1 = (bf16[2,256,384]{2,1,0:T(8,128)(2,1)S(1)}, bf16[2,256,384]{2,1,0:T(8,128)(2,1)S(1)}, u32[]{:S(2)}, u32[]{:S(2)}) collective-permute-start(bf16[2,256,384]{2,1,0:T(8,128)(2,1)S(1)} %slice.40), channel_id=1, source_target_pairs={{0,3},{1,0},{2,1},{3,2},{4,7},{5,4},{6,5},{7,6},{8,11},{9,8},{10,9... | collective-permute-start | bytes 1179656 | tf_op jit(solution)/shard_map/ppermute | solution.py:347
  30.0 13.7 %collective-permute-start.6 = (bf16[4,64,384]{2,1,0:T(8,128)(2,1)S(1)}, bf16[4,64,384]{2,1,0:T(8,128)(2,1)S(1)}, u32[]{:S(2)}, u32[]{:S(2)}) collective-permute-start(bf16[4,64,384]{2,1,0:T(8,128)(2,1)S(1)} %get-tuple-element.26), channel_id=1, source_target_pairs={{0,32},{4,36},{8,40},{12,44},{16,48},{20,52},{24,56},{28,60},{32,0... | collective-permute-start | bytes 589832 | tf_op jit(solution)/shard_map/ppermute | solution.py:351
  43.8 8.0 %collective-permute-start.7 = (bf16[8,32,384]{2,1,0:T(8,128)(2,1)S(1)}, bf16[8,32,384]{2,1,0:T(8,128)(2,1)S(1)}, u32[]{:S(2)}, u32[]{:S(2)}) collective-permute-start(bf16[8,32,384]{2,1,0:T(8,128)(2,1)S(1)} %get-tuple-element.30), channel_id=1, source_target_pairs={{0,64},{4,68},{8,72},{12,76},{16,80},{20,84},{24,88},{28,92},{32,9... | collective-permute-start | bytes 589832 | tf_op jit(solution)/shard_map/ppermute | solution.py:351
  51.9 6.9 %collective-permute-start.11 = (bf16[16,16,384]{2,1,0:T(8,128)(2,1)S(1)}, bf16[16,16,384]{2,1,0:T(8,128)(2,1)S(1)}, u32[]{:S(2)}, u32[]{:S(2)}) collective-permute-start(bf16[16,16,384]{2,1,0:T(8,128)(2,1)S(1)} %get-tuple-element.34), channel_id=1, source_target_pairs={{0,128},{4,132},{8,136},{12,140},{16,144},{20,148},{24,152},{28,15... | collective-permute-start | bytes 589832 | tf_op jit(solution)/shard_map/ppermute | solution.py:351
  54.9 9.6 %copy-start.2 = (bf16[768,3,192]{0,2,1:T(8,128)(2,1)S(1)}, bf16[768,3,192]{0,2,1:T(8,128)(2,1)}, u32[]{:S(2)}) copy-start(bf16[768,3,192]{0,2,1:T(8,128)(2,1)} %param.20) | copy-start | bytes 2654212
  54.9 4.8 %collective-permute-start.10 = (f32[4,768]{1,0:T(4,128)S(1)}, f32[4,768]{1,0:T(4,128)S(1)}, u32[]{:S(2)}, u32[]{:S(2)}) collective-permute-start(f32[4,768]{1,0:T(4,128)S(1)} %fusion.2.a), channel_id=1, source_target_pairs={{0,2},{1,3},{2,0},{3,1},{4,6},{5,7},{6,4},{7,5},{8,10},{9,11},{10,... | collective-permute-start | bytes 36872 | tf_op jit(solution)/shard_map/ppermute | solution.py:347
  55.4 4.2 %collective-permute-start.8 = (f32[4,768]{1,0:T(4,128)S(1)}, f32[4,768]{1,0:T(4,128)S(1)}, u32[]{:S(2)}, u32[]{:S(2)}) collective-permute-start(f32[4,768]{1,0:T(4,128)S(1)} %fusion.2.a), channel_id=1, source_target_pairs={{0,1},{1,2},{2,3},{3,0},{4,5},{5,6},{6,7},{7,4},{8,9},{9,10},{10,1... | collective-permute-start | bytes 36872 | tf_op jit(solution)/shard_map/ppermute | solution.py:347
  55.7 4.0 %collective-permute-start.9 = (f32[4,768]{1,0:T(4,128)S(1)}, f32[4,768]{1,0:T(4,128)S(1)}, u32[]{:S(2)}, u32[]{:S(2)}) collective-permute-start(f32[4,768]{1,0:T(4,128)S(1)} %fusion.2.a), channel_id=1, source_target_pairs={{0,3},{1,0},{2,1},{3,2},{4,7},{5,4},{6,5},{7,6},{8,11},{9,8},{10,9... | collective-permute-start | bytes 36872 | tf_op jit(solution)/shard_map/ppermute | solution.py:347
  58.9 17.3 %copy-start.9 = (bf16[192,768]{1,0:T(8,128)(2,1)S(1)}, bf16[192,768]{1,0:T(8,128)(2,1)}, u32[]{:S(2)}) copy-start(bf16[192,768]{1,0:T(8,128)(2,1)} %param.21) | copy-start | bytes 884740
  59.7 30.5 %collective-permute-start.12 = (bf16[1536,384]{1,0:T(8,128)(2,1)}, bf16[1536,384]{1,0:T(8,128)(2,1)}, u32[]{:S(2)}, u32[]{:S(2)}) collective-permute-start(bf16[1536,384]{1,0:T(8,128)(2,1)} %constant_dynamic-update-slice_fusion.4.refs_2_), channel_id=1, source_target_pairs={{0,4},{4,0},{8,12},{12,8},{16,20},{20,16},{24,28},{28,24},{32,36},... | collective-permute-start | bytes 3538952 | tf_op jit(solution)/shard_map/ppermute | solution.py:351
  66.3 23.1 %all-to-all-start = ((bf16[64,4,640]{2,1,0:T(4,128)(2,1)}), bf16[64,4,640]{2,1,0:T(4,128)(2,1)S(1)}, u32[]{:S(2)}, u32[]{:S(2)}) async-start(bf16[64,4,640]{2,1,0:T(4,128)(2,1)} %broadcast_in_dim.10), calls=%async_computation | async-start | bytes 655360 | tf_op jit(solution)/shard_map/all_to_all | solution.py:409
  97.1 4.6 %collective-permute-start.13 = (bf16[128,192]{1,0:T(8,128)(2,1)}, bf16[128,192]{1,0:T(8,128)(2,1)S(1)}, u32[]{:S(2)}, u32[]{:S(2)}) collective-permute-start(bf16[128,192]{1,0:T(8,128)(2,1)} %get-tuple-element.42), channel_id=1, source_target_pairs={{0,1},{1,2},{2,3},{3,0},{4,5},{5,6},{6,7},{7,4},{8,9},{9,10},{10,1... | collective-permute-start | bytes 147464 | tf_op jit(solution)/shard_map/ppermute | solution.py:347
  97.2 5.8 %collective-permute-start.14 = (bf16[128,192]{1,0:T(8,128)(2,1)}, bf16[128,192]{1,0:T(8,128)(2,1)S(1)}, u32[]{:S(2)}, u32[]{:S(2)}) collective-permute-start(bf16[128,192]{1,0:T(8,128)(2,1)} %get-tuple-element.43), channel_id=1, source_target_pairs={{0,2},{1,3},{2,0},{3,1},{4,6},{5,7},{6,4},{7,5},{8,10},{9,11},{10,... | collective-permute-start | bytes 147464 | tf_op jit(solution)/shard_map/ppermute | solution.py:347
  99.9 4.1 %collective-permute-start.15 = (bf16[128,192]{1,0:T(8,128)(2,1)}, bf16[128,192]{1,0:T(8,128)(2,1)S(1)}, u32[]{:S(2)}, u32[]{:S(2)}) collective-permute-start(bf16[128,192]{1,0:T(8,128)(2,1)} %get-tuple-element.44), channel_id=1, source_target_pairs={{0,3},{1,0},{2,1},{3,2},{4,7},{5,4},{6,5},{7,6},{8,11},{9,8},{10,9... | collective-permute-start | bytes 147464 | tf_op jit(solution)/shard_map/ppermute | solution.py:347
